TPU v7x, 256 devices: a whole 4x4x8 slice. The times are simulated.
256 devices in a mesh: dp: 8 (over z), ctx: 32 (over y, x, core).
Axes of the slice: x: 4, y: 4, z: 8, core: 2. Of those that a mesh axis runs over, the one named last changes fastest.
Arguments:
- output_gate_input: bfloat16 [8, 4096, 4096], P('dp', 'ctx'), may hold values from -6 to 6
- key_input: bfloat16 [8, 4096, 4096], P('dp', 'ctx'), may hold values from -6 to 6
- value_input: bfloat16 [8, 4096, 4096], P('dp', 'ctx'), may hold values from -6 to 6
- upstream: bfloat16 [8, 4096, 4096], P('dp', 'ctx'), may hold values from -6 to 6
- filter_taps: float32 [256, 4096], P('ctx'), may hold values from -6 to 6
- block_of_shard: int32 [32], replicated, may hold values from 0 to 31, each once
Outputs:
- mixed_out: bfloat16 [8, 4096, 4096], P('dp', 'ctx')
- gate_grad: bfloat16 [8, 4096, 4096], P('dp', 'ctx')
- key_grad: bfloat16 [8, 4096, 4096], P('dp', 'ctx')
- value_grad: bfloat16 [8, 4096, 4096], P('dp', 'ctx')
- taps_grad: float32 [256, 4096], P('ctx')
Inputs may be any that keep to these rules, and one draw needn't show every extreme that they name: block_of_shard names every block of positions exactly once.
All inputs are finite; a program needn't handle non-finite values.
Results may differ from a plain program's by a relative error of at most 0.012.
Values may be sent and summed in bfloat16 or wider, within the bound.
No kernel may reach another device: no remote copies, remote signals or barrier semaphores. Data moves between devices by JAX's collectives and lax.ppermute only.
A program may use at most 192 MiB of HBM per device.

v0:
```python
import math

import jax
import jax.numpy as jnp
from jax import lax
from jax.sharding import PartitionSpec as P

epsilon = 1e-06


def inverse_order(block_of_shard):
    pieces = block_of_shard.shape[0]
    labels = jnp.arange(pieces, dtype=jnp.int32)
    matches = (block_of_shard[:, None] == labels[None, :]).astype(jnp.int32)
    return jnp.sum(labels[:, None] * matches, axis=0)


def reorder_blocks(row_data, placing):
    pieces = placing.shape[0]
    shaped = row_data.reshape((pieces, row_data.shape[0] // pieces) + row_data.shape[1:])
    return jnp.take(shaped, placing, axis=0).reshape(row_data.shape)


def toeplitz_tables(kernel, block_rows):
    groups, length = kernel.shape
    pieces = length // block_rows
    padded = jnp.concatenate([jnp.zeros((groups, block_rows), kernel.dtype), kernel], axis=1)
    padded = padded.reshape(groups, pieces + 1, block_rows)
    tables = []
    for lag_block in range(pieces):
        segment = jnp.concatenate([padded[:, lag_block], padded[:, lag_block + 1]], axis=1)
        turned = jnp.roll(segment[:, ::-1], -(block_rows - 1), axis=1)
        flat = jnp.tile(turned, (1, block_rows))[:, : block_rows * (2 * block_rows - 1)]
        tables.append(flat.reshape(groups, block_rows, 2 * block_rows - 1)[:, :, :block_rows])
    return tables


def diagonal_sums(square):
    groups, block_rows, _ = square.shape
    flipped = square[:, :, ::-1]
    padded = jnp.pad(flipped, ((0, 0), (0, 0), (0, block_rows + 1)))
    flat = padded.reshape(groups, block_rows * (2 * block_rows + 1))[
        :, : 2 * block_rows * block_rows
    ]
    return jnp.sum(flat.reshape(groups, block_rows, 2 * block_rows), axis=1)


def forward_part(tables, signal, groups, block_rows):
    length, channels = signal.shape
    pieces = length // block_rows
    blocks = signal.reshape(pieces, block_rows, groups, channels // groups)
    total = jnp.zeros(blocks.shape, jnp.float32)
    for lag_block in range(pieces):
        contrib = jnp.einsum(
            "grs,jsgc->jrgc",
            tables[lag_block],
            blocks[: pieces - lag_block],
            preferred_element_type=jnp.float32,
        )
        total = total + jnp.pad(contrib, ((lag_block, 0), (0, 0), (0, 0), (0, 0)))
    return total.reshape(length, channels).astype(jnp.bfloat16)


def backward_part(tables, signal, weighted_seq, groups, block_rows):
    length, channels = signal.shape
    pieces = length // block_rows
    blocks = signal.reshape(pieces, block_rows, groups, channels // groups)
    wblocks = weighted_seq.reshape(pieces, block_rows, groups, channels // groups)
    total = jnp.zeros(blocks.shape, jnp.float32)
    lag_buffer = jnp.zeros((groups, (pieces + 1) * block_rows), jnp.float32)
    for lag_block in range(pieces):
        later = wblocks[lag_block:]
        contrib = jnp.einsum(
            "grs,jrgc->jsgc", tables[lag_block], later, preferred_element_type=jnp.float32
        )
        total = total + jnp.pad(contrib, ((0, lag_block), (0, 0), (0, 0), (0, 0)))
        square = jnp.einsum(
            "jrgc,jsgc->grs",
            later,
            blocks[: pieces - lag_block],
            preferred_element_type=jnp.float32,
        )
        folded = diagonal_sums(square)[:, : 2 * block_rows - 1]
        start = lag_block * block_rows + 1
        lag_buffer = lag_buffer + jnp.pad(
            folded, ((0, 0), (start, (pieces + 1) * block_rows - start - 2 * block_rows + 1))
        )
    returned = total.reshape(length, channels).astype(jnp.bfloat16)
    return (returned, lag_buffer[:, block_rows : block_rows + length])


def gate_product(first, second):
    return (first.astype(jnp.float32) * second.astype(jnp.float32)).astype(jnp.bfloat16)


def shards(output_gate_input, key_input, value_input, upstream, filter_taps, block_of_shard):
    inverse = inverse_order(block_of_shard)
    groups, length = filter_taps.shape
    block_rows = min(length, max(256, length // 16))
    root_mean = jnp.sqrt(jnp.mean(filter_taps * filter_taps, axis=1, keepdims=True) + epsilon)
    norm_scale = 1.0 / (math.sqrt(length) * root_mean)
    kernel = (filter_taps * norm_scale).astype(jnp.bfloat16)
    tables = toeplitz_tables(kernel, block_rows)
    gates_here = output_gate_input[0]
    keys_here = key_input[0]
    values_here = value_input[0]
    upstream_here = upstream[0]
    product = gate_product(keys_here, values_here)
    arrived = (
        lax.all_to_all(product, "ctx", split_axis=1, concat_axis=0, tiled=True),
        lax.all_to_all(gates_here, "ctx", split_axis=1, concat_axis=0, tiled=True),
        lax.all_to_all(upstream_here, "ctx", split_axis=1, concat_axis=0, tiled=True),
    )
    signal = reorder_blocks(arrived[0], inverse)
    gates_seq = reorder_blocks(arrived[1], inverse)
    upstream_seq = reorder_blocks(arrived[2], inverse)
    mixing = forward_part(tables, signal, groups, block_rows)
    weighted_seq = gate_product(upstream_seq, gates_seq)
    returned, lag_sums = backward_part(tables, signal, weighted_seq, groups, block_rows)
    mixed_seq = reorder_blocks(gate_product(gates_seq, mixing), block_of_shard)
    gate_seq = reorder_blocks(gate_product(upstream_seq, mixing), block_of_shard)
    returned = reorder_blocks(returned, block_of_shard)
    mixed_out, gate_grad, returned_here = (
        lax.all_to_all(mixed_seq, "ctx", split_axis=0, concat_axis=1, tiled=True),
        lax.all_to_all(gate_seq, "ctx", split_axis=0, concat_axis=1, tiled=True),
        lax.all_to_all(returned, "ctx", split_axis=0, concat_axis=1, tiled=True),
    )
    key_grad = gate_product(returned_here, values_here)
    value_grad = gate_product(returned_here, keys_here)
    lag_total = lax.psum(lag_sums, "dp")
    lag_mean = lag_total / lax.axis_size("dp")
    projection = jnp.sum(lag_mean * filter_taps, axis=1, keepdims=True)
    taps_grad = (
        norm_scale * lag_mean - filter_taps * (norm_scale * norm_scale * norm_scale) * projection
    )
    return (mixed_out[None], gate_grad[None], key_grad[None], value_grad[None], taps_grad)


def solution(mesh):
    return jax.shard_map(
        shards,
        mesh=mesh,
        in_specs=(
            P("dp", "ctx", None),
            P("dp", "ctx", None),
            P("dp", "ctx", None),
            P("dp", "ctx", None),
            P("ctx", None),
            P(),
        ),
        out_specs=(
            P("dp", "ctx", None),
            P("dp", "ctx", None),
            P("dp", "ctx", None),
            P("dp", "ctx", None),
            P("ctx", None),
        ),
        check_vma=False,
    )
```

profile of v0, /device:TPU:2, one launch (start us, length us, event | category | flops | bytes accessed | tf_op | source)
XLA Modules:
  0.0 1128.7 jit_solution(15635006254996681494)
XLA Ops:
  11.2 7.7 all-to-all-start.1
  20.9 14.1 %all-to-all-done.1 = bf16[128,32,128]{2,0,1:T(8,128)(2,1)S(1)} async-done(((bf16[128,32,128]{2,0,1:T(8,128)(2,1)}), bf16[128,32,128]{2,0,1:T(8,128)(2,1)S(1)}, u32[]{:S(2)}, u32[]{:S(2)}) %all-to-all-start.1) | async-done | bytes 1048608 | tf_op jit(solution)/shard_map/all_to_all | solution.py:110
  43.2 13.2 %all-to-all-done = bf16[128,32,128]{2,0,1:T(8,128)(2,1)S(1)} async-done(((bf16[128,32,128]{2,0,1:T(8,128)(2,1)}), bf16[128,32,128]{2,0,1:T(8,128)(2,1)S(1)}, u32[]{:S(2)}, u32[]{:S(2)}) %all-to-all-start) | async-done | bytes 1048608 | tf_op jit(solution)/shard_map/all_to_all | solution.py:111
  67.2 11.1 all-to-all-done.3
  149.3 17.5 %rev.65 = f32[8,256,256]{2,1,0:T(8,128)} reverse(f32[8,256,256]{2,1,0:T(8,128)} %convolution_bitcast_fusion.10), dimensions={2} | reverse | bytes 4194304 | tf_op jit(solution)/shard_map/rev | solution.py:40
  168.6 17.7 %rev.64 = f32[8,256,256]{2,1,0:T(8,128)} reverse(f32[8,256,256]{2,1,0:T(8,128)} %convolution_bitcast_fusion.11), dimensions={2} | reverse | bytes 4194304 | tf_op jit(solution)/shard_map/rev | solution.py:40
  188.1 17.7 %rev.66 = f32[8,256,256]{2,1,0:T(8,128)} reverse(f32[8,256,256]{2,1,0:T(8,128)} %convolution_bitcast_fusion.9), dimensions={2} | reverse | bytes 4194304 | tf_op jit(solution)/shard_map/rev | solution.py:40
  207.6 17.7 %rev.67 = f32[8,256,256]{2,1,0:T(8,128)} reverse(f32[8,256,256]{2,1,0:T(8,128)} %convolution_bitcast_fusion.8), dimensions={2} | reverse | bytes 4194304 | tf_op jit(solution)/shard_map/rev | solution.py:40
  227.1 17.7 %rev.68 = f32[8,256,256]{2,1,0:T(8,128)} reverse(f32[8,256,256]{2,1,0:T(8,128)} %convolution_bitcast_fusion.7), dimensions={2} | reverse | bytes 4194304 | tf_op jit(solution)/shard_map/rev | solution.py:40
  246.6 17.7 %rev.69 = f32[8,256,256]{2,1,0:T(8,128)} reverse(f32[8,256,256]{2,1,0:T(8,128)} %convolution_bitcast_fusion.6), dimensions={2} | reverse | bytes 4194304 | tf_op jit(solution)/shard_map/rev | solution.py:40
  266.1 17.7 %rev.70 = f32[8,256,256]{2,1,0:T(8,128)} reverse(f32[8,256,256]{2,1,0:T(8,128)} %convolution_bitcast_fusion.5), dimensions={2} | reverse | bytes 4194304 | tf_op jit(solution)/shard_map/rev | solution.py:40
  285.6 17.6 %rev.71 = f32[8,256,256]{2,1,0:T(8,128)} reverse(f32[8,256,256]{2,1,0:T(8,128)} %convolution_bitcast_fusion.4), dimensions={2} | reverse | bytes 4194304 | tf_op jit(solution)/shard_map/rev | solution.py:40
  303.7 11.6 %rev.72 = f32[8,256,256]{2,1,0:T(8,128)} reverse(f32[8,256,256]{2,1,0:T(8,128)S(1)} %convolution_bitcast_fusion.14), dimensions={2} | reverse | bytes 4194304 | tf_op jit(solution)/shard_map/rev | solution.py:40
  317.0 11.6 %rev.73 = f32[8,256,256]{2,1,0:T(8,128)} reverse(f32[8,256,256]{2,1,0:T(8,128)S(1)} %convolution_bitcast_fusion.3), dimensions={2} | reverse | bytes 4194304 | tf_op jit(solution)/shard_map/rev | solution.py:40
  329.2 11.6 %rev.74 = f32[8,256,256]{2,1,0:T(8,128)} reverse(f32[8,256,256]{2,1,0:T(8,128)S(1)} %convolution_bitcast_fusion.2), dimensions={2} | reverse | bytes 4194304 | tf_op jit(solution)/shard_map/rev | solution.py:40
  341.3 11.6 %rev.75 = f32[8,256,256]{2,1,0:T(8,128)} reverse(f32[8,256,256]{2,1,0:T(8,128)S(1)} %convolution_bitcast_fusion.1), dimensions={2} | reverse | bytes 4194304 | tf_op jit(solution)/shard_map/rev | solution.py:40
  353.4 11.6 %rev.76 = f32[8,256,256]{2,1,0:T(8,128)} reverse(f32[8,256,256]{2,1,0:T(8,128)S(1)} %convolution_bitcast_fusion.13), dimensions={2} | reverse | bytes 4194304 | tf_op jit(solution)/shard_map/rev | solution.py:40
  365.5 11.6 %rev.77 = f32[8,256,256]{2,1,0:T(8,128)} reverse(f32[8,256,256]{2,1,0:T(8,128)S(1)} %convolution_bitcast_fusion.12), dimensions={2} | reverse | bytes 4194304 | tf_op jit(solution)/shard_map/rev | solution.py:40
  377.6 11.6 %rev.78 = f32[8,256,256]{2,1,0:T(8,128)} reverse(f32[8,256,256]{2,1,0:T(8,128)S(1)} %convolution_bitcast_fusion), dimensions={2} | reverse | bytes 4194304 | tf_op jit(solution)/shard_map/rev | solution.py:40
  389.6 11.8 %rev.79 = f32[8,256,256]{2,1,0:T(8,128)} reverse(f32[8,256,256]{2,1,0:T(8,128)S(1)} %fusion.81), dimensions={2} | reverse | bytes 4194304 | tf_op jit(solution)/shard_map/rev | solution.py:40
  405.8 7.1 reshape.447
  440.0 7.1 reshape.443
  457.1 7.3 reshape.441
  474.5 7.1 reshape.439
  491.6 7.1 reshape.437
  508.7 7.5 reshape.435
  629.1 7.3 reshape.421
  679.1 71.5 %all-reduce.65.cloned.1.call-done = f32[8,4096]{1,0:T(8,128)} async-done(((f32[8,4096]{1,0:T(8,128)}), f32[8,4096]{1,0:T(8,128)}) %all-reduce.65.cloned.1.call-update) | async-done | bytes 131088 | tf_op jit(solution)/shard_map/psum | solution.py:130
  1009.5 7.7 fusion.36
  1045.1 23.3 %all_to_all.81 = bf16[32,128,128]{2,1,0:T(8,128)(2,1)S(1)} all-to-all(bf16[32,128,128]{2,1,0:T(8,128)(2,1)S(1)} %get-tuple-element.60), channel_id=1, replica_groups=mesh['dp'=8,'ctx'=32] {'ctx'}, dimensions={0} | all-to-all | bytes 2097152 | tf_op jit(solution)/shard_map/all_to_all | solution.py:125
  1068.5 20.7 %all_to_all.82 = bf16[32,128,128]{2,1,0:T(8,128)(2,1)S(1)} all-to-all(bf16[32,128,128]{2,1,0:T(8,128)(2,1)S(1)} %get-tuple-element.61), channel_id=1, replica_groups=mesh['dp'=8,'ctx'=32] {'ctx'}, dimensions={0} | all-to-all | bytes 2097152 | tf_op jit(solution)/shard_map/all_to_all | solution.py:124
  1099.8 10.7 all-to-all-done.5
  (611 shorter events, 648.4 us)
Async XLA Ops:
  11.2 23.9 %all-to-all-start.1 = ((bf16[128,32,128]{2,0,1:T(8,128)(2,1)}), bf16[128,32,128]{2,0,1:T(8,128)(2,1)S(1)}, u32[]{:S(2)}, u32[]{:S(2)}) async-start(bf16[128,32,128]{2,0,1:T(8,128)(2,1)} %copy.207), calls=%async_computation.1 | async-start | bytes 2097152 | tf_op jit(solution)/shard_map/all_to_all | solution.py:110
  35.1 21.3 %all-to-all-start = ((bf16[128,32,128]{2,0,1:T(8,128)(2,1)}), bf16[128,32,128]{2,0,1:T(8,128)(2,1)S(1)}, u32[]{:S(2)}, u32[]{:S(2)}) async-start(bf16[128,32,128]{2,0,1:T(8,128)(2,1)} %copy.204), calls=%async_computation | async-start | bytes 2097152 | tf_op jit(solution)/shard_map/all_to_all | solution.py:111
  56.3 22.0 %all-to-all-start.3 = ((bf16[128,32,128]{2,0,1:T(8,128)(2,1)}), bf16[128,32,128]{2,0,1:T(8,128)(2,1)}, u32[]{:S(2)}, u32[]{:S(2)}) async-start(bf16[128,32,128]{2,0,1:T(8,128)(2,1)} %copy.243), calls=%async_computation.3 | async-start | bytes 2097152 | tf_op jit(solution)/shard_map/all_to_all | solution.py:112
  62.1 688.6 %all-reduce.65.cloned.1.call-start = ((), (), s32[]{:S(2)}) async-start(), calls=%async_computation.6 | async-start | bytes 262144 | tf_op jit(solution)/shard_map/psum | solution.py:130
  62.3 18.0 %copy-start.79 = (pred[32]{0:T(512)(128)(4,1)}, pred[32]{0:T(512)(128)(4,1)S(1)}, u32[]{:S(2)}) copy-start(pred[32]{0:T(512)(128)(4,1)S(1)} %compare_and_fusion.1) | copy-start | bytes 100
  67.2 13.7 %copy-start.2 = (bf16[32,128,128]{2,1,0:T(8,128)(2,1)}, bf16[32,128,128]{2,1,0:T(8,128)(2,1)S(1)}, u32[]{:S(2)}) copy-start(bf16[32,128,128]{2,1,0:T(8,128)(2,1)S(1)} %gather_fusion) | copy-start | bytes 3145732
  83.8 305.4 %copy-start.75 = (bf16[256,8,16]{0,2,1:T(8,128)(2,1)}, bf16[256,8,16]{0,2,1:T(8,128)(2,1)S(1)}, u32[]{:S(2)}) copy-start(bf16[256,8,16]{0,2,1:T(8,128)(2,1)S(1)} %reshape.414) | copy-start | bytes 196612
  85.1 279.9 %copy-start.60 = (bf16[3,256,8,16]{1,0,3,2:T(4,128)(2,1)}, bf16[3,256,8,16]{1,0,3,2:T(4,128)(2,1)S(1)}, u32[]{:S(2)}) copy-start(bf16[3,256,8,16]{1,0,3,2:T(4,128)(2,1)S(1)} %slice.794) | copy-start | bytes 589828
  104.0 62.8 %copy-start.31 = (bf16[16,256,8,16]{1,0,3,2:T(8,128)(2,1)}, bf16[16,256,8,16]{1,0,3,2:T(8,128)(2,1)S(1)}, u32[]{:S(2)}) copy-start(bf16[16,256,8,16]{1,0,3,2:T(8,128)(2,1)S(1)} %reshape_reshape.4) | copy-start | bytes 3145732
  141.7 25.1 %copy-start.32 = (bf16[16,256,8,16]{1,0,3,2:T(8,128)(2,1)}, bf16[16,256,8,16]{1,0,3,2:T(8,128)(2,1)S(1)}, u32[]{:S(2)}) copy-start(bf16[16,256,8,16]{1,0,3,2:T(8,128)(2,1)S(1)} %convert_element_type.227) | copy-start | bytes 3145732
  168.6 17.7 %copy-start.35 = (bf16[14,256,8,16]{1,0,3,2:T(8,128)(2,1)S(1)}, bf16[14,256,8,16]{1,0,3,2:T(8,128)(2,1)}, u32[]{:S(2)}) copy-start(bf16[14,256,8,16]{1,0,3,2:T(8,128)(2,1)} %slice.695) | copy-start | bytes 2752516
  168.6 17.7 %copy-start.37 = (bf16[14,256,8,16]{1,0,3,2:T(8,128)(2,1)S(1)}, bf16[14,256,8,16]{1,0,3,2:T(8,128)(2,1)}, u32[]{:S(2)}) copy-start(bf16[14,256,8,16]{1,0,3,2:T(8,128)(2,1)} %slice.822) | copy-start | bytes 2752516
  188.1 17.7 %copy-start.38 = (bf16[13,256,8,16]{1,0,3,2:T(8,128)(2,1)S(1)}, bf16[13,256,8,16]{1,0,3,2:T(8,128)(2,1)}, u32[]{:S(2)}) copy-start(bf16[13,256,8,16]{1,0,3,2:T(8,128)(2,1)} %slice.704) | copy-start | bytes 2555908
  188.1 17.7 %copy-start.40 = (bf16[13,256,8,16]{1,0,3,2:T(8,128)(2,1)S(1)}, bf16[13,256,8,16]{1,0,3,2:T(8,128)(2,1)}, u32[]{:S(2)}) copy-start(bf16[13,256,8,16]{1,0,3,2:T(8,128)(2,1)} %slice.824) | copy-start | bytes 2555908
  207.6 17.7 %copy-start.41 = (bf16[12,256,8,16]{1,0,3,2:T(8,128)(2,1)S(1)}, bf16[12,256,8,16]{1,0,3,2:T(8,128)(2,1)}, u32[]{:S(2)}) copy-start(bf16[12,256,8,16]{1,0,3,2:T(8,128)(2,1)} %slice.713) | copy-start | bytes 2359300
  207.6 17.7 %copy-start.43 = (bf16[12,256,8,16]{1,0,3,2:T(8,128)(2,1)S(1)}, bf16[12,256,8,16]{1,0,3,2:T(8,128)(2,1)}, u32[]{:S(2)}) copy-start(bf16[12,256,8,16]{1,0,3,2:T(8,128)(2,1)} %slice.826) | copy-start | bytes 2359300
  227.1 17.7 %copy-start.44 = (bf16[11,256,8,16]{1,0,3,2:T(8,128)(2,1)S(1)}, bf16[11,256,8,16]{1,0,3,2:T(8,128)(2,1)}, u32[]{:S(2)}) copy-start(bf16[11,256,8,16]{1,0,3,2:T(8,128)(2,1)} %slice.722) | copy-start | bytes 2162692
  227.1 17.7 %copy-start.46 = (bf16[11,256,8,16]{1,0,3,2:T(8,128)(2,1)S(1)}, bf16[11,256,8,16]{1,0,3,2:T(8,128)(2,1)}, u32[]{:S(2)}) copy-start(bf16[11,256,8,16]{1,0,3,2:T(8,128)(2,1)} %slice.828) | copy-start | bytes 2162692
  246.6 17.7 %copy-start.47 = (bf16[10,256,8,16]{1,0,3,2:T(8,128)(2,1)S(1)}, bf16[10,256,8,16]{1,0,3,2:T(8,128)(2,1)}, u32[]{:S(2)}) copy-start(bf16[10,256,8,16]{1,0,3,2:T(8,128)(2,1)} %slice.731) | copy-start | bytes 1966084
  246.6 17.7 %copy-start.49 = (bf16[10,256,8,16]{1,0,3,2:T(8,128)(2,1)S(1)}, bf16[10,256,8,16]{1,0,3,2:T(8,128)(2,1)}, u32[]{:S(2)}) copy-start(bf16[10,256,8,16]{1,0,3,2:T(8,128)(2,1)} %slice.830) | copy-start | bytes 1966084
  266.1 17.7 %copy-start.51 = (bf16[9,256,8,16]{1,0,3,2:T(8,128)(2,1)S(1)}, bf16[9,256,8,16]{1,0,3,2:T(8,128)(2,1)}, u32[]{:S(2)}) copy-start(bf16[9,256,8,16]{1,0,3,2:T(8,128)(2,1)} %slice.740) | copy-start | bytes 1769476
  266.1 17.7 %copy-start.53 = (bf16[9,256,8,16]{1,0,3,2:T(8,128)(2,1)S(1)}, bf16[9,256,8,16]{1,0,3,2:T(8,128)(2,1)}, u32[]{:S(2)}) copy-start(bf16[9,256,8,16]{1,0,3,2:T(8,128)(2,1)} %slice.832) | copy-start | bytes 1769476
  285.6 17.6 %copy-start.55 = (bf16[8,256,8,16]{1,0,3,2:T(8,128)(2,1)S(1)}, bf16[8,256,8,16]{1,0,3,2:T(8,128)(2,1)}, u32[]{:S(2)}) copy-start(bf16[8,256,8,16]{1,0,3,2:T(8,128)(2,1)} %slice.749) | copy-start | bytes 1572868
  285.6 17.6 %copy-start.57 = (bf16[8,256,8,16]{1,0,3,2:T(8,128)(2,1)S(1)}, bf16[8,256,8,16]{1,0,3,2:T(8,128)(2,1)}, u32[]{:S(2)}) copy-start(bf16[8,256,8,16]{1,0,3,2:T(8,128)(2,1)} %slice.834) | copy-start | bytes 1572868
  317.0 11.7 %copy-start.62 = (bf16[6,256,8,16]{1,0,3,2:T(8,128)(2,1)S(1)}, bf16[6,256,8,16]{1,0,3,2:T(8,128)(2,1)}, u32[]{:S(2)}) copy-start(bf16[6,256,8,16]{1,0,3,2:T(8,128)(2,1)} %slice.767) | copy-start | bytes 1179652
  317.0 11.6 %copy-start.64 = (bf16[6,256,8,16]{1,0,3,2:T(8,128)(2,1)S(1)}, bf16[6,256,8,16]{1,0,3,2:T(8,128)(2,1)}, u32[]{:S(2)}) copy-start(bf16[6,256,8,16]{1,0,3,2:T(8,128)(2,1)} %slice.838) | copy-start | bytes 1179652
  329.2 11.6 %copy-start.66 = (bf16[5,256,8,16]{1,0,3,2:T(8,128)(2,1)S(1)}, bf16[5,256,8,16]{1,0,3,2:T(8,128)(2,1)}, u32[]{:S(2)}) copy-start(bf16[5,256,8,16]{1,0,3,2:T(8,128)(2,1)} %slice.776) | copy-start | bytes 983044
  329.2 11.6 %copy-start.68 = (bf16[5,256,8,16]{1,0,3,2:T(8,128)(2,1)S(1)}, bf16[5,256,8,16]{1,0,3,2:T(8,128)(2,1)}, u32[]{:S(2)}) copy-start(bf16[5,256,8,16]{1,0,3,2:T(8,128)(2,1)} %slice.840) | copy-start | bytes 983044
  365.5 11.6 %copy-start.69 = (bf16[2,256,8,16]{1,0,3,2:T(2,128)(2,1)S(1)}, bf16[2,256,8,16]{1,0,3,2:T(2,128)(2,1)}, u32[]{:S(2)}) copy-start(bf16[2,256,8,16]{1,0,3,2:T(2,128)(2,1)} %slice.803) | copy-start | bytes 393220
  365.5 11.6 %copy-start.70 = (bf16[2,256,8,16]{1,0,3,2:T(2,128)(2,1)S(1)}, bf16[2,256,8,16]{1,0,3,2:T(2,128)(2,1)}, u32[]{:S(2)}) copy-start(bf16[2,256,8,16]{1,0,3,2:T(2,128)(2,1)} %slice.846) | copy-start | bytes 393220
  675.0 75.6 %copy-start.77 = (f32[8,4096]{1,0:T(8,128)S(1)}, f32[8,4096]{1,0:T(8,128)}, u32[]{:S(2)}) copy-start(f32[8,4096]{1,0:T(8,128)} %param.12) | copy-start | bytes 393220
  1089.1 21.3 %all-to-all-start.5 = ((bf16[32,128,128]{2,1,0:T(8,128)(2,1)}), bf16[32,128,128]{2,1,0:T(8,128)(2,1)S(1)}, u32[]{:S(2)}, u32[]{:S(2)}) async-start(bf16[32,128,128]{2,1,0:T(8,128)(2,1)} %get-tuple-element.59), calls=%async_computation.5 | async-start | bytes 2097152 | tf_op jit(solution)/shard_map/all_to_all | solution.py:126
  (87 other events, 313.8 us)
Sparse Core Ops, SparseCore 0:
  678.6 71.9 all-reduce.64
where the time goes:
time: 1150 us; the launch traced here: 1130 us
  local copies, waits for them, and re-layouts  770 us (67%)
  waiting for transfers between devices  121 us (11%)
  matrix products  92.7 us (8%)
  other arithmetic  61.6 us (5%)
  blocking collectives  44 us (4%)
  starting transfers between devices  23.8 us (2%)
  between operations  15.9 us (1%)
    rev x16, local copies, waits for them, and re-layouts, diagonal_sums(): flipped = square[:, :, ::-1]  234 us
    unnamed x256, local copies, waits for them, and re-layouts  117 us
    reshape x16, local copies, waits for them, and re-layouts, diagonal_sums(): padded.reshape(groups, block_rows * (2 * block_rows + 1))  114 us
    reshape x16, local copies, waits for them, and re-layouts, toeplitz_tables(): flat.reshape(groups, block_rows, 2 * block_rows - 1)[:, :, :block_rows]  81.9 us
    psum x1, waiting for transfers between devices, shards(): lag_total = lax.psum(lag_sums, 'dp')  71.5 us
    slice x16, local copies, waits for them, and re-layouts, diagonal_sums(): padded.reshape(groups, block_rows * (2 * block_rows + 1))  71.3 us
    pad x16, local copies, waits for them, and re-layouts, diagonal_sums(): padded = jnp.pad(flipped, ((0, 0), (0, 0), (0, block_rows + 1)))  45.8 us
    reduce_sum x16, other arithmetic, diagonal_sums(): return jnp.sum(flat.reshape(groups, block_rows, 2 * block_rows), axis=1)  42.4 us
  transfers between devices with their start and end apart: 5, of which 5 were waited for; matrix products, arithmetic and copies ran while one was open for 1% of the time, Pallas kernels for 0%

commit v1 on v0

v1 whole, which is shorter than its diff:
```python
import functools
import math

import jax
import jax.numpy as jnp
from jax import lax
from jax.experimental import pallas as pl
from jax.experimental.pallas import tpu as pltpu
from jax.sharding import PartitionSpec as P

EPSILON = 1e-06
BLOCK = 128
GROUP = 16
VMEM_LIMIT = 48 * 1024 * 1024

NN = (((1,), (0,)), ((), ()))
NT = (((1,), (1,)), ((), ()))
TN = (((0,), (0,)), ((), ()))


def dot(a, b, dims):
    return lax.dot_general(a, b, dims, preferred_element_type=jnp.float32)


def params():
    return pltpu.CompilerParams(vmem_limit_bytes=VMEM_LIMIT)


def product_of(a, b):
    return (a.astype(jnp.float32) * b.astype(jnp.float32)).astype(jnp.bfloat16)


def pre_kernel(tiles, a_ref, b_ref, out_ref):
    for i in range(tiles):
        cols = slice(i * BLOCK, (i + 1) * BLOCK)
        out_ref[i] = product_of(a_ref[0, :, cols], b_ref[0, :, cols]).T


def pre(a, b):
    _, rows, channels = a.shape
    pieces = channels // BLOCK
    tiles = 4
    spec = pl.BlockSpec((1, rows, tiles * BLOCK), lambda i: (0, 0, i))
    return pl.pallas_call(
        functools.partial(pre_kernel, tiles),
        grid=(pieces // tiles,),
        in_specs=[spec, spec],
        out_specs=pl.BlockSpec((tiles, BLOCK, rows), lambda i: (i, 0, 0)),
        out_shape=jax.ShapeDtypeStruct((pieces, BLOCK, rows), jnp.bfloat16),
        compiler_params=params(),
        cost_estimate=pl.CostEstimate(
            flops=a.size, bytes_accessed=6 * a.size, transcendentals=0
        ),
    )(a, b)


def strip_kernel(taps_ref, out_ref):
    g = pl.program_id(0)
    taps = taps_ref[pl.ds(g, 1), :]
    length = taps.shape[1]
    root = jnp.sqrt(jnp.mean(taps * taps, axis=1, keepdims=True) + EPSILON)
    row = taps * (1.0 / (math.sqrt(length) * root))
    width = length + BLOCK
    cur = jnp.concatenate([jnp.zeros((1, BLOCK), jnp.float32), row], axis=1)
    cur = jnp.broadcast_to(cur, (16, width))
    line = lax.broadcasted_iota(jnp.int32, (16, width), 0)
    for step in (1, 2, 4, 8):
        cur = jnp.where((line & step) != 0, pltpu.roll(cur, step, 1), cur)
    for q in range(BLOCK // 16):
        if q:
            cur = pltpu.roll(cur, 16, 1)
        out_ref[0, 16 * q : 16 * (q + 1), :] = cur.astype(jnp.bfloat16)
    out_ref[0, :, :BLOCK] = jnp.zeros((BLOCK, BLOCK), jnp.bfloat16)


def strips(taps):
    groups, length = taps.shape
    width = length + BLOCK
    return pl.pallas_call(
        strip_kernel,
        grid=(groups,),
        in_specs=[pl.BlockSpec((groups, length), lambda g: (0, 0))],
        out_specs=pl.BlockSpec((1, BLOCK, width), lambda g: (g, 0, 0)),
        out_shape=jax.ShapeDtypeStruct((groups, BLOCK, width), jnp.bfloat16),
        compiler_params=params(),
        cost_estimate=pl.CostEstimate(
            flops=4 * groups * BLOCK * width,
            bytes_accessed=2 * groups * BLOCK * width,
            transcendentals=0,
        ),
    )(taps)


def place(order_ref, from_ref, to_ref):
    for d in range(from_ref.shape[0]):
        b = order_ref[d]
        to_ref[b % 2, pl.ds(pl.multiple_of(GROUP * (b // 2), GROUP), GROUP), :] = from_ref[d]


def take(order_ref, from_ref, to_ref):
    for d in range(to_ref.shape[0]):
        b = order_ref[d]
        rows = pl.ds(pl.multiple_of(GROUP * (b // 2), GROUP), GROUP)
        to_ref[d] = from_ref[b % 2, rows, :].astype(jnp.bfloat16)


def conv_kernel(backward, order_ref, x_ref, strip_ref, out_ref, xs, acc):
    place(order_ref, x_ref, xs)
    rows = xs.shape[1]
    pairs = rows // GROUP
    for lag in range(pairs):
        at = BLOCK + 2 * BLOCK * lag
        weights = jnp.concatenate(
            [
                strip_ref[0, :, at : at + 2 * BLOCK],
                strip_ref[0, :, at - BLOCK : at + BLOCK],
            ],
            axis=0,
        )
        low, high = slice(0, rows - GROUP * lag), slice(GROUP * lag, rows)
        source, target = (high, low) if backward else (low, high)
        left = jnp.concatenate([xs[0, source, :], xs[1, source, :]], axis=1)
        part = dot(left, weights, NT if backward else NN)
        if lag == 0:
            acc[0] = part[:, :BLOCK]
            acc[1] = part[:, BLOCK:]
        else:
            acc[0, target, :] += part[:, :BLOCK]
            acc[1, target, :] += part[:, BLOCK:]
    take(order_ref, acc, out_ref)


def conv(order, x, strip, backward):
    pieces = x.shape[0]
    groups, _, width = strip.shape
    rows = GROUP * pieces // 2
    spec = pl.BlockSpec((pieces, GROUP, BLOCK), lambda g, order: (0, g, 0))
    return pl.pallas_call(
        functools.partial(conv_kernel, backward),
        grid_spec=pltpu.PrefetchScalarGridSpec(
            num_scalar_prefetch=1,
            grid=(groups,),
            in_specs=[
                spec,
                pl.BlockSpec((1, BLOCK, width), lambda g, order: (g, 0, 0)),
            ],
            out_specs=spec,
            scratch_shapes=[
                pltpu.VMEM((2, rows, BLOCK), jnp.bfloat16),
                pltpu.VMEM((2, rows, BLOCK), jnp.float32),
            ],
        ),
        out_shape=jax.ShapeDtypeStruct(x.shape, jnp.bfloat16),
        compiler_params=params(),
        cost_estimate=pl.CostEstimate(
            flops=groups * rows * rows * 16 * BLOCK,
            bytes_accessed=4 * x.size + 2 * strip.size,
            transcendentals=0,
        ),
    )(order, x, strip)


def lag_kernel(order_ref, x_ref, w_ref, out_ref, xs, ws, squares):
    pieces = x_ref.shape[0]
    total = GROUP * pieces
    for d in range(pieces):
        rows = pl.ds(pl.multiple_of(GROUP * order_ref[d], GROUP), GROUP)
        xs[rows, :] = x_ref[d]
        ws[rows, :] = w_ref[d]
    ws[total : total + GROUP, :] = jnp.zeros((GROUP, BLOCK), jnp.bfloat16)
    x_turned = xs[...].T
    for lag in range(0, pieces, 2):
        depth = total - GROUP * lag
        start = GROUP * lag
        right = jnp.concatenate(
            [ws[start : start + depth, :], ws[start + GROUP : start + GROUP + depth, :]],
            axis=1,
        )
        squares[:, lag * BLOCK : (lag + 2) * BLOCK] = dot(x_turned[:, :depth], right, NN)
    row = lax.broadcasted_iota(jnp.int32, (BLOCK, BLOCK), 0)
    col = lax.broadcasted_iota(jnp.int32, (BLOCK, BLOCK), 1)
    squares[:, :BLOCK] = jnp.where(col >= row, squares[:, :BLOCK], 0.0)
    width = squares.shape[1]
    cur = squares[BLOCK - 8 :, :]
    for q in range(BLOCK // 8 - 2, -1, -1):
        cur = pltpu.roll(cur, width - 8, 1) + squares[8 * q : 8 * (q + 1), :]
    line = lax.broadcasted_iota(jnp.int32, (8, width), 0)
    for step in (1, 2, 4):
        cur = jnp.where((line & step) != 0, pltpu.roll(cur, width - step, 1), cur)
    out_ref[pl.ds(pl.program_id(0), 1), :] = jnp.sum(cur, axis=0, keepdims=True)


def lag_sums_of(order, x, w, groups):
    pieces = x.shape[0]
    length = pieces * BLOCK
    rows = GROUP * pieces
    spec = pl.BlockSpec((pieces, GROUP, BLOCK), lambda g, order: (0, g, 0))
    return pl.pallas_call(
        lag_kernel,
        grid_spec=pltpu.PrefetchScalarGridSpec(
            num_scalar_prefetch=1,
            grid=(groups,),
            in_specs=[spec, spec],
            out_specs=pl.BlockSpec((groups, length), lambda g, order: (0, 0)),
            scratch_shapes=[
                pltpu.VMEM((rows, BLOCK), jnp.bfloat16),
                pltpu.VMEM((rows + GROUP, BLOCK), jnp.bfloat16),
                pltpu.VMEM((BLOCK, length), jnp.float32),
            ],
        ),
        out_shape=jax.ShapeDtypeStruct((groups, length), jnp.float32),
        compiler_params=params(),
        cost_estimate=pl.CostEstimate(
            flops=groups * rows * BLOCK * length,
            bytes_accessed=4 * x.size,
            transcendentals=0,
        ),
    )(order, x, w)


def post_kernel(tiles, r_ref, a_ref, b_ref, out_a_ref, out_b_ref):
    for i in range(tiles):
        cols = slice(i * BLOCK, (i + 1) * BLOCK)
        turned = r_ref[i].T
        out_a_ref[0, :, cols] = product_of(a_ref[0, :, cols], turned)
        out_b_ref[0, :, cols] = product_of(b_ref[0, :, cols], turned)


def post(r, a, b):
    _, rows, channels = a.shape
    pieces = channels // BLOCK
    tiles = 4
    spec = pl.BlockSpec((1, rows, tiles * BLOCK), lambda i: (0, 0, i))
    shape = jax.ShapeDtypeStruct(a.shape, a.dtype)
    return pl.pallas_call(
        functools.partial(post_kernel, tiles),
        grid=(pieces // tiles,),
        in_specs=[
            pl.BlockSpec((tiles, BLOCK, rows), lambda i: (i, 0, 0)),
            spec,
            spec,
        ],
        out_specs=[spec, spec],
        out_shape=[shape, shape],
        compiler_params=params(),
        cost_estimate=pl.CostEstimate(
            flops=2 * a.size, bytes_accessed=10 * a.size, transcendentals=0
        ),
    )(r, a, b)


def taps_kernel(sequences, taps_ref, lag_ref, out_ref):
    taps = taps_ref[...]
    length = taps.shape[1]
    root = jnp.sqrt(jnp.mean(taps * taps, axis=1, keepdims=True) + EPSILON)
    scale = 1.0 / (math.sqrt(length) * root)
    mean = lag_ref[...] / sequences
    projection = jnp.sum(mean * taps, axis=1, keepdims=True)
    out_ref[...] = scale * mean - taps * (scale * scale * scale) * projection


def taps_grad_of(taps, lag_total, sequences):
    return pl.pallas_call(
        functools.partial(taps_kernel, sequences),
        out_shape=jax.ShapeDtypeStruct(taps.shape, jnp.float32),
        compiler_params=params(),
    )(taps, lag_total)


def exchange(tiles):
    return lax.all_to_all(tiles, "ctx", split_axis=0, concat_axis=0, tiled=True)


def sum_over_dp(x):
    size = lax.axis_size("dp")
    step = 1
    while step < size:
        x = x + lax.ppermute(x, "dp", [(i, i ^ step) for i in range(size)])
        step *= 2
    return x


def shards(output_gate_input, key_input, value_input, upstream, filter_taps, order):
    groups = filter_taps.shape[0]
    product = exchange(pre(key_input, value_input))
    weighted = exchange(pre(upstream, output_gate_input))
    strip = strips(filter_taps)
    mixing = exchange(conv(order, product, strip, False))
    lag_sums = lag_sums_of(order, product, weighted, groups)
    returned = exchange(conv(order, weighted, strip, True))
    lag_total = sum_over_dp(lag_sums)
    mixed_out, gate_grad = post(mixing, output_gate_input, upstream)
    key_grad, value_grad = post(returned, value_input, key_input)
    taps_grad = taps_grad_of(filter_taps, lag_total, lax.axis_size("dp"))
    return mixed_out, gate_grad, key_grad, value_grad, taps_grad


def solution(mesh):
    rows = P("dp", "ctx", None)
    return jax.shard_map(
        shards,
        mesh=mesh,
        in_specs=(rows, rows, rows, rows, P("ctx", None), P()),
        out_specs=(rows, rows, rows, rows, P("ctx", None)),
        check_vma=False,
    )
```

time: 1150 us -> 149 us (0.13); the launches traced: 1130 us -> 148 us
  local copies, waits for them, and re-layouts: 770 us -> 11.7 us
  matrix products: 92.7 us -> 0 us
  waiting for transfers between devices: 121 us -> 30.3 us
  Pallas kernels: 0 us -> 67.5 us
  other arithmetic: 61.6 us -> 0.05 us
  blocking collectives: 44 us -> 0 us
  between operations: 15.9 us -> 0.77 us
  starting transfers between devices: 23.8 us -> 37.7 us
    rev x16 -> x0, local copies, waits for them, and re-layouts: 234 us -> none  [diagonal_sums(): flipped = square[:, :, ::-1]]
    reshape x32 -> x0, local copies, waits for them, and re-layouts: 196 us -> none  [the longest x16 114 us: diagonal_sums(): padded.reshape(groups, block_rows * (2 * block_rows + 1))]
    slice x166 -> x0, local copies, waits for them, and re-layouts: 141 us -> none  [the longest x16 71.3 us: diagonal_sums(): padded.reshape(groups, block_rows * (2 * block_rows + 1))]
    unnamed x256 -> x32, local copies, waits for them, and re-layouts: 117 us -> 11.7 us
    dot_general x48 -> x0, matrix products: 92.7 us -> none  [the longest x16 38.5 us: backward_part(): jnp.einsum('grs,jrgc->jsgc', tables[lag_block], later, preferred_element_...]
    psum x1 -> x0, waiting for transfers between devices: 71.5 us -> none  [shards(): lag_total = lax.psum(lag_sums, 'dp')]
    pallas_call x0 -> x9, Pallas kernels: none -> 67.5 us  [the longest x2 21.2 us: conv(): pl.pallas_call(functools.partial(conv_kernel, backward), grid_spec=pltpu....]
    pad x16 -> x0, local copies, waits for them, and re-layouts: 45.8 us -> none  [diagonal_sums(): padded = jnp.pad(flipped, ((0, 0), (0, 0), (0, block_rows + 1)))]
  transfers between devices with their start and end apart: 5 -> 7, of which waited for: 5 -> 5; matrix products, arithmetic and copies ran while one was open for 1% -> 0% of each run, Pallas kernels for 0% -> 40%
where the time goes in v1:
time: 149 us; the launch traced here: 148 us
  Pallas kernels  67.5 us (45%)
  starting transfers between devices  37.7 us (25%)
  waiting for transfers between devices  30.3 us (20%)
  local copies, waits for them, and re-layouts  11.7 us (8%)
    all_to_all x4, starting transfers between devices, exchange(): return lax.all_to_all(tiles, 'ctx', split_axis=0, concat_axis=0, tiled=True)  26.1 us
    pallas_call x2, Pallas kernels, conv(): pl.pallas_call(functools.partial(conv_kernel, backward), grid_spec=pltpu....  21.2 us
    pallas_call x1, Pallas kernels, lag_sums_of(): pl.pallas_call(lag_kernel, grid_spec=pltpu.PrefetchScalarGridSpec(num_sca...  16.5 us
    ppermute x3, waiting for transfers between devices, sum_over_dp(): x = x + lax.ppermute(x, 'dp', [(i, i ^ step) for i in range(size)])  15.8 us
    all_to_all x4, waiting for transfers between devices, exchange(): return lax.all_to_all(tiles, 'ctx', split_axis=0, concat_axis=0, tiled=True)  14.5 us
    unnamed x32, local copies, waits for them, and re-layouts  11.7 us
    ppermute x3, starting transfers between devices, sum_over_dp(): x = x + lax.ppermute(x, 'dp', [(i, i ^ step) for i in range(size)])  11.6 us
    pallas_call x2, Pallas kernels, post(): pl.pallas_call(functools.partial(post_kernel, tiles), grid=(pieces // til...  11.5 us
  transfers between devices with their start and end apart: 7, of which 5 were waited for; matrix products, arithmetic and copies ran while one was open for 0% of the time, Pallas kernels for 40%

profile of v1, /device:TPU:2, one launch (start us, length us, event | category | flops | bytes accessed | tf_op | source)
XLA Modules:
  0.0 148.1 jit_solution(5158504623793837228)
XLA Ops:
  0.6 0.0 copy-start.4
  0.6 1.2 copy-done.4
  1.9 1.2 copy-done.6
  3.1 3.2 %shard_map.105 = bf16[32,128,128]{2,1,0:T(8,128)(2,1)} custom-call(bf16[1,128,4096]{2,1,0:T(8,128)(2,1)S(1)} %copy-done.6, bf16[1,128,4096]{2,1,0:T(8,128)(2,1)S(1)} %copy-done.4), custom_call_target="tpu_custom_call" | custom-call | flops 524288 | bytes 3145728 | tf_op jit(solution)/shard_map/pallas_call | solution.py:44
  6.3 7.8 %all-to-all-start.2 = ((bf16[32,128,128]{2,1,0:T(8,128)(2,1)}), bf16[32,128,128]{2,1,0:T(8,128)(2,1)S(1)}, u32[]{:S(2)}, u32[]{:S(2)}) async-start(bf16[32,128,128]{2,1,0:T(8,128)(2,1)} %shard_map.105), calls=%async_computation.2 | async-start | bytes 2097152 | tf_op jit(solution)/shard_map/all_to_all | solution.py:271
  14.1 1.2 copy-done
  15.3 1.2 copy-done.2
  16.5 3.2 %shard_map.101 = bf16[32,128,128]{2,1,0:T(8,128)(2,1)} custom-call(bf16[1,128,4096]{2,1,0:T(8,128)(2,1)S(1)} %copy-done, bf16[1,128,4096]{2,1,0:T(8,128)(2,1)S(1)} %copy-done.2), custom_call_target="tpu_custom_call" | custom-call | flops 524288 | bytes 3145728 | tf_op jit(solution)/shard_map/pallas_call | solution.py:44
  19.7 10.5 %all-to-all-done.2.x_ref.w_ref = bf16[32,128,128]{2,1,0:T(8,128)(2,1)S(1)} async-done(((bf16[32,128,128]{2,1,0:T(8,128)(2,1)}), bf16[32,128,128]{2,1,0:T(8,128)(2,1)S(1)}, u32[]{:S(2)}, u32[]{:S(2)}) %all-to-all-start.2) | async-done | bytes 1048608 | tf_op jit(solution)/shard_map/all_to_all | solution.py:271
  30.2 5.0 %all-to-all-start = ((bf16[32,128,128]{2,1,0:T(8,128)(2,1)}), bf16[32,128,128]{2,1,0:T(8,128)(2,1)S(1)}, u32[]{:S(2)}, u32[]{:S(2)}) async-start(bf16[32,128,128]{2,1,0:T(8,128)(2,1)} %shard_map.101), calls=%async_computation | async-start | bytes 2097152 | tf_op jit(solution)/shard_map/all_to_all | solution.py:271
  35.2 11.1 %shard_map.102.strip_ref = bf16[8,128,4224]{2,1,0:T(8,128)(2,1)} custom-call(f32[8,4096]{1,0:T(8,128)S(1)} %copy-done.14), custom_call_target="tpu_custom_call" | custom-call | flops 17301504 | bytes 8650752 | tf_op jit(solution)/shard_map/pallas_call | solution.py:79
  46.3 11.3 %shard_map.106 = bf16[32,128,128]{2,1,0:T(8,128)(2,1)} custom-call(s32[32]{0:T(128)S(1)} %copy-done.15, bf16[32,128,128]{2,1,0:T(8,128)(2,1)S(1)} %all-to-all-done.2.x_ref.w_ref, bf16[8,128,4224]{2,1,0:T(8,128)(2,1)} %shard_map.102.strip_ref), custom_call_target="tpu_custom_call" | custom-call | flops 1073741824 | bytes 10747904 | tf_op jit(solution)/shard_map/pallas_call | solution.py:138
  57.7 1.0 copy-done.11
  58.6 7.5 %all-to-all-start.3 = ((bf16[32,128,128]{2,1,0:T(8,128)(2,1)}), bf16[32,128,128]{2,1,0:T(8,128)(2,1)}, u32[]{:S(2)}, u32[]{:S(2)}) async-start(bf16[32,128,128]{2,1,0:T(8,128)(2,1)} %shard_map.106), calls=%async_computation.3 | async-start | bytes 2097152 | tf_op jit(solution)/shard_map/all_to_all | solution.py:271
  66.2 1.2 copy-done.12
  67.4 9.9 %shard_map.103 = bf16[32,128,128]{2,1,0:T(8,128)(2,1)S(1)} custom-call(s32[32]{0:T(128)S(1)} %copy-done.15, bf16[32,128,128]{2,1,0:T(8,128)(2,1)S(1)} %copy-done.12, bf16[8,128,4224]{2,1,0:T(8,128)(2,1)} %shard_map.102.strip_ref), custom_call_target="tpu_custom_call" | custom-call | flops 1073741824 | bytes 10747904 | tf_op jit(solution)/shard_map/pallas_call | solution.py:138
  77.3 1.0 copy-done.8
  78.3 4.0 %all-to-all-done.3.r_ref = bf16[32,128,128]{2,1,0:T(8,128)(2,1)} async-done(((bf16[32,128,128]{2,1,0:T(8,128)(2,1)}), bf16[32,128,128]{2,1,0:T(8,128)(2,1)}, u32[]{:S(2)}, u32[]{:S(2)}) %all-to-all-start.3) | async-done | bytes 1048608 | tf_op jit(solution)/shard_map/all_to_all | solution.py:271
  82.3 5.7 %all-to-all-start.1 = ((bf16[32,128,128]{2,1,0:T(8,128)(2,1)}), bf16[32,128,128]{2,1,0:T(8,128)(2,1)}, u32[]{:S(2)}, u32[]{:S(2)}) async-start(bf16[32,128,128]{2,1,0:T(8,128)(2,1)} %copy-done.8), calls=%async_computation.1 | async-start | bytes 2097152 | tf_op jit(solution)/shard_map/all_to_all | solution.py:271
  88.1 1.2 copy-done.10
  89.3 1.2 copy-done.13
  90.5 16.5 %shard_map.108 = f32[8,4096]{1,0:T(8,128)S(1)} custom-call(s32[32]{0:T(128)S(1)} %copy-done.15, bf16[32,128,128]{2,1,0:T(8,128)(2,1)S(1)} %copy-done.13, bf16[32,128,128]{2,1,0:T(8,128)(2,1)S(1)} %copy-done.10), custom_call_target="tpu_custom_call" | custom-call | flops 2147483648 | bytes 2097152 | tf_op jit(solution)/shard_map/pallas_call | solution.py:198
  107.1 2.0 %collective-permute-start = (f32[8,4096]{1,0:T(8,128)S(1)}, f32[8,4096]{1,0:T(8,128)S(1)}, u32[]{:S(2)}, u32[]{:S(2)}) collective-permute-start(f32[8,4096]{1,0:T(8,128)S(1)} %shard_map.108), channel_id=1, source_target_pairs={{0,32},{32,0},{64,96},{96,64},{128,160},{160,128},{192,224},{224,1... | collective-permute-start | bytes 393224 | tf_op jit(solution)/shard_map/ppermute | solution.py:278
  109.1 3.8 %collective-permute-done = f32[8,4096]{1,0:T(8,128)S(1)} collective-permute-done((f32[8,4096]{1,0:T(8,128)S(1)}, f32[8,4096]{1,0:T(8,128)S(1)}, u32[]{:S(2)}, u32[]{:S(2)}) %collective-permute-start) | collective-permute-done | bytes 131104 | tf_op jit(solution)/shard_map/ppermute | solution.py:278
  112.9 3.4 %collective-permute-start.1 = (f32[8,4096]{1,0:T(8,128)S(1)}, f32[8,4096]{1,0:T(8,128)S(1)}, u32[]{:S(2)}, u32[]{:S(2)}) collective-permute-start(f32[8,4096]{1,0:T(8,128)S(1)} %add.9), channel_id=1, source_target_pairs={{0,64},{32,96},{64,0},{96,32},{128,192},{160,224},{192,128},{224,1... | collective-permute-start | bytes 393224 | tf_op jit(solution)/shard_map/ppermute | solution.py:278
  116.3 6.0 %collective-permute-done.1 = f32[8,4096]{1,0:T(8,128)S(1)} collective-permute-done((f32[8,4096]{1,0:T(8,128)S(1)}, f32[8,4096]{1,0:T(8,128)S(1)}, u32[]{:S(2)}, u32[]{:S(2)}) %collective-permute-start.1) | collective-permute-done | bytes 131104 | tf_op jit(solution)/shard_map/ppermute | solution.py:278
  122.3 6.3 %collective-permute-start.2 = (f32[8,4096]{1,0:T(8,128)S(1)}, f32[8,4096]{1,0:T(8,128)S(1)}, u32[]{:S(2)}, u32[]{:S(2)}) collective-permute-start(f32[8,4096]{1,0:T(8,128)S(1)} %add.10), channel_id=1, source_target_pairs={{0,128},{32,160},{64,192},{96,224},{128,0},{160,32},{192,64},{224,... | collective-permute-start | bytes 393224 | tf_op jit(solution)/shard_map/ppermute | solution.py:278
  128.5 6.0 %collective-permute-done.2 = f32[8,4096]{1,0:T(8,128)S(1)} collective-permute-done((f32[8,4096]{1,0:T(8,128)S(1)}, f32[8,4096]{1,0:T(8,128)S(1)}, u32[]{:S(2)}, u32[]{:S(2)}) %collective-permute-start.2) | collective-permute-done | bytes 131104 | tf_op jit(solution)/shard_map/ppermute | solution.py:278
  134.6 0.8 shard_map.109
  135.4 5.7 %shard_map.107 = (bf16[1,128,4096]{2,1,0:T(8,128)(2,1)}, bf16[1,128,4096]{2,1,0:T(8,128)(2,1)}) custom-call(bf16[32,128,128]{2,1,0:T(8,128)(2,1)} %all-to-all-done.3.r_ref, bf16[1,128,4096]{2,1,0:T(8,128)(2,1)S(1)} %copy-done.3, bf16[1,128,4096]{2,1,0:T(8,128)(2,1)S(1)} %copy-done.1), custom_call_target="tpu_custom_call" | custom-call | flops 1048576 | bytes 5242880 | tf_op jit(solution)/shard_map/pallas_call | solution.py:235
  141.1 1.2 copy-done.7
  142.4 5.7 %shard_map.104 = (bf16[1,128,4096]{2,1,0:T(8,128)(2,1)}, bf16[1,128,4096]{2,1,0:T(8,128)(2,1)}) custom-call(bf16[32,128,128]{2,1,0:T(8,128)(2,1)} %all-to-all-done.1.r_ref, bf16[1,128,4096]{2,1,0:T(8,128)(2,1)S(1)} %copy-done.5, bf16[1,128,4096]{2,1,0:T(8,128)(2,1)S(1)} %copy-done.7), custom_call_target="tpu_custom_call" | custom-call | flops 1048576 | bytes 5242880 | tf_op jit(solution)/shard_map/pallas_call | solution.py:235
  (26 shorter events, 0.1 us)
Async XLA Ops:
  0.6 1.2 copy-start.4
  1.9 1.2 copy-start.6
  3.1 32.1 %copy-start.14 = (f32[8,4096]{1,0:T(8,128)S(1)}, f32[8,4096]{1,0:T(8,128)}, u32[]{:S(2)}) copy-start(f32[8,4096]{1,0:T(8,128)} %taps_ref.3) | copy-start | bytes 393220
  6.3 40.0 %copy-start.15 = (s32[32]{0:T(128)S(1)}, s32[32]{0:T(128)}, u32[]{:S(2)}) copy-start(s32[32]{0:T(128)} %order_ref.5) | copy-start | bytes 388
  6.3 23.9 %all-to-all-start.2 = ((bf16[32,128,128]{2,1,0:T(8,128)(2,1)}), bf16[32,128,128]{2,1,0:T(8,128)(2,1)S(1)}, u32[]{:S(2)}, u32[]{:S(2)}) async-start(bf16[32,128,128]{2,1,0:T(8,128)(2,1)} %shard_map.105), calls=%async_computation.2 | async-start | bytes 2097152 | tf_op jit(solution)/shard_map/all_to_all | solution.py:271
  14.1 1.2 copy-start
  15.3 1.2 copy-start.2
  30.2 27.5 %copy-start.9 = (bf16[32,128,128]{2,1,0:T(8,128)(2,1)}, bf16[32,128,128]{2,1,0:T(8,128)(2,1)S(1)}, u32[]{:S(2)}) copy-start(bf16[32,128,128]{2,1,0:T(8,128)(2,1)S(1)} %all-to-all-done.2.x_ref.w_ref) | copy-start | bytes 3145732
  30.2 27.5 %all-to-all-start = ((bf16[32,128,128]{2,1,0:T(8,128)(2,1)}), bf16[32,128,128]{2,1,0:T(8,128)(2,1)S(1)}, u32[]{:S(2)}, u32[]{:S(2)}) async-start(bf16[32,128,128]{2,1,0:T(8,128)(2,1)} %shard_map.101), calls=%async_computation | async-start | bytes 2097152 | tf_op jit(solution)/shard_map/all_to_all | solution.py:271
  57.7 1.0 copy-start.11
  58.6 23.7 %all-to-all-start.3 = ((bf16[32,128,128]{2,1,0:T(8,128)(2,1)}), bf16[32,128,128]{2,1,0:T(8,128)(2,1)}, u32[]{:S(2)}, u32[]{:S(2)}) async-start(bf16[32,128,128]{2,1,0:T(8,128)(2,1)} %shard_map.106), calls=%async_computation.3 | async-start | bytes 2097152 | tf_op jit(solution)/shard_map/all_to_all | solution.py:271
  66.2 1.2 copy-start.12
  67.4 68.0 %copy-start.1 = (bf16[1,128,4096]{2,1,0:T(8,128)(2,1)S(1)}, bf16[1,128,4096]{2,1,0:T(8,128)(2,1)}, u32[]{:S(2)}) copy-start(bf16[1,128,4096]{2,1,0:T(8,128)(2,1)} %b_ref.7) | copy-start | bytes 3145732
  67.4 68.0 %copy-start.3 = (bf16[1,128,4096]{2,1,0:T(8,128)(2,1)S(1)}, bf16[1,128,4096]{2,1,0:T(8,128)(2,1)}, u32[]{:S(2)}) copy-start(bf16[1,128,4096]{2,1,0:T(8,128)(2,1)} %a_ref.7) | copy-start | bytes 3145732
  77.3 1.0 copy-start.8
  78.3 62.8 %copy-start.5 = (bf16[1,128,4096]{2,1,0:T(8,128)(2,1)S(1)}, bf16[1,128,4096]{2,1,0:T(8,128)(2,1)}, u32[]{:S(2)}) copy-start(bf16[1,128,4096]{2,1,0:T(8,128)(2,1)} %b_ref.6) | copy-start | bytes 3145732
  82.3 58.8 %all-to-all-start.1 = ((bf16[32,128,128]{2,1,0:T(8,128)(2,1)}), bf16[32,128,128]{2,1,0:T(8,128)(2,1)}, u32[]{:S(2)}, u32[]{:S(2)}) async-start(bf16[32,128,128]{2,1,0:T(8,128)(2,1)} %copy-done.8), calls=%async_computation.1 | async-start | bytes 2097152 | tf_op jit(solution)/shard_map/all_to_all | solution.py:271
  88.1 1.2 copy-start.10
  89.3 1.2 copy-start.13
  107.1 5.8 %collective-permute-start = (f32[8,4096]{1,0:T(8,128)S(1)}, f32[8,4096]{1,0:T(8,128)S(1)}, u32[]{:S(2)}, u32[]{:S(2)}) collective-permute-start(f32[8,4096]{1,0:T(8,128)S(1)} %shard_map.108), channel_id=1, source_target_pairs={{0,32},{32,0},{64,96},{96,64},{128,160},{160,128},{192,224},{224,1... | collective-permute-start | bytes 393224 | tf_op jit(solution)/shard_map/ppermute | solution.py:278
  112.9 9.3 %collective-permute-start.1 = (f32[8,4096]{1,0:T(8,128)S(1)}, f32[8,4096]{1,0:T(8,128)S(1)}, u32[]{:S(2)}, u32[]{:S(2)}) collective-permute-start(f32[8,4096]{1,0:T(8,128)S(1)} %add.9), channel_id=1, source_target_pairs={{0,64},{32,96},{64,0},{96,32},{128,192},{160,224},{192,128},{224,1... | collective-permute-start | bytes 393224 | tf_op jit(solution)/shard_map/ppermute | solution.py:278
  122.3 12.3 %collective-permute-start.2 = (f32[8,4096]{1,0:T(8,128)S(1)}, f32[8,4096]{1,0:T(8,128)S(1)}, u32[]{:S(2)}, u32[]{:S(2)}) collective-permute-start(f32[8,4096]{1,0:T(8,128)S(1)} %add.10), channel_id=1, source_target_pairs={{0,128},{32,160},{64,192},{96,224},{128,0},{160,32},{192,64},{224,... | collective-permute-start | bytes 393224 | tf_op jit(solution)/shard_map/ppermute | solution.py:278
  141.1 1.2 copy-start.7

commit v2 on v1

--- a/solution.py
+++ b/solution.py
@@ -11,7 +11,8 @@
 EPSILON = 1e-06
 BLOCK = 128
 GROUP = 16
-VMEM_LIMIT = 48 * 1024 * 1024
+MIB = 1024 * 1024
+SPAN = 4
 
 NN = (((1,), (0,)), ((), ()))
 NT = (((1,), (1,)), ((), ()))
@@ -22,12 +23,12 @@
     return lax.dot_general(a, b, dims, preferred_element_type=jnp.float32)
 
 
-def params():
-    return pltpu.CompilerParams(vmem_limit_bytes=VMEM_LIMIT)
+def params(mib=60):
+    return pltpu.CompilerParams(vmem_limit_bytes=mib * MIB)
 
 
 def product_of(a, b):
-    return (a.astype(jnp.float32) * b.astype(jnp.float32)).astype(jnp.bfloat16)
+    return a * b
 
 
 def pre_kernel(tiles, a_ref, b_ref, out_ref):
@@ -73,70 +74,100 @@
     out_ref[0, :, :BLOCK] = jnp.zeros((BLOCK, BLOCK), jnp.bfloat16)
 
 
-def strips(taps):
+def pre_strip_kernel(tiles, a_ref, b_ref, taps_ref, out_ref, strip_ref):
+    pre_kernel(tiles, a_ref, b_ref, out_ref)
+    strip_kernel(taps_ref, strip_ref)
+
+
+def pre_and_strips(a, b, taps):
+    _, rows, channels = a.shape
+    pieces = channels // BLOCK
     groups, length = taps.shape
+    tiles = pieces // groups
     width = length + BLOCK
-    return pl.pallas_call(
-        strip_kernel,
+    spec = pl.BlockSpec((1, rows, tiles * BLOCK), lambda i: (0, 0, i))
+    return pl.pallas_call(
+        functools.partial(pre_strip_kernel, tiles),
         grid=(groups,),
-        in_specs=[pl.BlockSpec((groups, length), lambda g: (0, 0))],
-        out_specs=pl.BlockSpec((1, BLOCK, width), lambda g: (g, 0, 0)),
-        out_shape=jax.ShapeDtypeStruct((groups, BLOCK, width), jnp.bfloat16),
+        in_specs=[spec, spec, pl.BlockSpec((groups, length), lambda i: (0, 0))],
+        out_specs=[
+            pl.BlockSpec((tiles, BLOCK, rows), lambda i: (i, 0, 0)),
+            pl.BlockSpec((1, BLOCK, width), lambda i: (i, 0, 0)),
+        ],
+        out_shape=[
+            jax.ShapeDtypeStruct((pieces, BLOCK, rows), jnp.bfloat16),
+            jax.ShapeDtypeStruct((groups, BLOCK, width), jnp.bfloat16),
+        ],
         compiler_params=params(),
         cost_estimate=pl.CostEstimate(
             flops=4 * groups * BLOCK * width,
-            bytes_accessed=2 * groups * BLOCK * width,
+            bytes_accessed=2 * groups * BLOCK * width + 6 * a.size,
             transcendentals=0,
         ),
-    )(taps)
-
-
-def place(order_ref, from_ref, to_ref):
-    for d in range(from_ref.shape[0]):
+    )(a, b, taps)
+
+
+def rows_of(block):
+    return pl.ds(pl.multiple_of(GROUP * block, GROUP), GROUP)
+
+
+def conv_kernel(backward, order_ref, x_ref, strip_ref, out_ref, xs, acc):
+    pieces = x_ref.shape[0]
+    rows = acc.shape[1]
+    spare = GROUP * (SPAN - 1)
+    first = 0 if backward else SPAN - 1
+    if backward:
+        xs[:, rows : rows + spare, :] = jnp.zeros((2, spare, BLOCK), jnp.bfloat16)
+    else:
+        xs[:, :spare, :] = jnp.zeros((2, spare, BLOCK), jnp.bfloat16)
+    for d in range(pieces):
         b = order_ref[d]
-        to_ref[b % 2, pl.ds(pl.multiple_of(GROUP * (b // 2), GROUP), GROUP), :] = from_ref[d]
-
-
-def take(order_ref, from_ref, to_ref):
-    for d in range(to_ref.shape[0]):
-        b = order_ref[d]
-        rows = pl.ds(pl.multiple_of(GROUP * (b // 2), GROUP), GROUP)
-        to_ref[d] = from_ref[b % 2, rows, :].astype(jnp.bfloat16)
-
-
-def conv_kernel(backward, order_ref, x_ref, strip_ref, out_ref, xs, acc):
-    place(order_ref, x_ref, xs)
-    rows = xs.shape[1]
-    pairs = rows // GROUP
-    for lag in range(pairs):
-        at = BLOCK + 2 * BLOCK * lag
-        weights = jnp.concatenate(
-            [
-                strip_ref[0, :, at : at + 2 * BLOCK],
-                strip_ref[0, :, at - BLOCK : at + BLOCK],
-            ],
-            axis=0,
-        )
-        low, high = slice(0, rows - GROUP * lag), slice(GROUP * lag, rows)
-        source, target = (high, low) if backward else (low, high)
-        left = jnp.concatenate([xs[0, source, :], xs[1, source, :]], axis=1)
-        part = dot(left, weights, NT if backward else NN)
+        xs[b % 2, rows_of(b // 2 + first), :] = x_ref[d]
+    wide = 2 * BLOCK
+    for lag in range(0, rows // GROUP, SPAN):
+        depth = rows - GROUP * lag
+        at = BLOCK + wide * lag
+        lefts, weights = [], []
+        for k in range(SPAN):
+            start = GROUP * (lag + k) if backward else GROUP * (SPAN - 1 - k)
+            lefts += [xs[0, start : start + depth, :], xs[1, start : start + depth, :]]
+            weights += [
+                strip_ref[0, :, at + wide * k : at + wide * (k + 1)],
+                strip_ref[0, :, at + wide * k - BLOCK : at + wide * k + BLOCK],
+            ]
+        left = jnp.concatenate(lefts, axis=1)
+        if backward:
+            weights = [
+                strip_ref[0, :, at : at + wide * SPAN],
+                strip_ref[0, :, at - BLOCK : at - BLOCK + wide * SPAN],
+            ]
+        part = dot(left, jnp.concatenate(weights, axis=0), NT if backward else NN)
         if lag == 0:
             acc[0] = part[:, :BLOCK]
             acc[1] = part[:, BLOCK:]
         else:
+            target = slice(0, depth) if backward else slice(rows - depth, rows)
             acc[0, target, :] += part[:, :BLOCK]
             acc[1, target, :] += part[:, BLOCK:]
-    take(order_ref, acc, out_ref)
-
-
-def conv(order, x, strip, backward):
+    for d in range(pieces):
+        b = order_ref[d]
+        out_ref[d] = acc[b % 2, rows_of(b // 2), :].astype(jnp.bfloat16)
+
+
+def conv_scratch(rows):
+    return [
+        pltpu.VMEM((2, rows + GROUP * (SPAN - 1), BLOCK), jnp.bfloat16),
+        pltpu.VMEM((2, rows, BLOCK), jnp.float32),
+    ]
+
+
+def forward(order, x, strip):
     pieces = x.shape[0]
     groups, _, width = strip.shape
     rows = GROUP * pieces // 2
     spec = pl.BlockSpec((pieces, GROUP, BLOCK), lambda g, order: (0, g, 0))
     return pl.pallas_call(
-        functools.partial(conv_kernel, backward),
+        functools.partial(conv_kernel, False),
         grid_spec=pltpu.PrefetchScalarGridSpec(
             num_scalar_prefetch=1,
             grid=(groups,),
@@ -145,10 +176,7 @@
                 pl.BlockSpec((1, BLOCK, width), lambda g, order: (g, 0, 0)),
             ],
             out_specs=spec,
-            scratch_shapes=[
-                pltpu.VMEM((2, rows, BLOCK), jnp.bfloat16),
-                pltpu.VMEM((2, rows, BLOCK), jnp.float32),
-            ],
+            scratch_shapes=conv_scratch(rows),
         ),
         out_shape=jax.ShapeDtypeStruct(x.shape, jnp.bfloat16),
         compiler_params=params(),
@@ -164,14 +192,16 @@
     pieces = x_ref.shape[0]
     total = GROUP * pieces
     for d in range(pieces):
-        rows = pl.ds(pl.multiple_of(GROUP * order_ref[d], GROUP), GROUP)
+        rows = rows_of(order_ref[d])
         xs[rows, :] = x_ref[d]
         ws[rows, :] = w_ref[d]
-    ws[total : total + GROUP, :] = jnp.zeros((GROUP, BLOCK), jnp.bfloat16)
+    ws[total:, :] = jnp.zeros((BLOCK, BLOCK), jnp.bfloat16)
     x_turned = xs[...].T
     for lag in range(0, pieces, 2):
-        depth = total - GROUP * lag
+        depth = total - GROUP * lag // BLOCK * BLOCK
         start = GROUP * lag
+        if start + GROUP + depth > total + BLOCK:
+            raise ValueError("spare rows")
         right = jnp.concatenate(
             [ws[start : start + depth, :], ws[start + GROUP : start + GROUP + depth, :]],
             axis=1,
@@ -190,32 +220,48 @@
     out_ref[pl.ds(pl.program_id(0), 1), :] = jnp.sum(cur, axis=0, keepdims=True)
 
 
-def lag_sums_of(order, x, w, groups):
+def back_kernel(
+    order_ref, x_ref, w_ref, strip_ref, out_ref, lag_ref, pairs, acc, xs, ws, squares
+):
+    conv_kernel(True, order_ref, w_ref, strip_ref, out_ref, pairs, acc)
+    lag_kernel(order_ref, x_ref, w_ref, lag_ref, xs, ws, squares)
+
+
+def back(order, x, w, strip):
     pieces = x.shape[0]
+    groups, _, width = strip.shape
     length = pieces * BLOCK
     rows = GROUP * pieces
     spec = pl.BlockSpec((pieces, GROUP, BLOCK), lambda g, order: (0, g, 0))
     return pl.pallas_call(
-        lag_kernel,
+        back_kernel,
         grid_spec=pltpu.PrefetchScalarGridSpec(
             num_scalar_prefetch=1,
             grid=(groups,),
-            in_specs=[spec, spec],
-            out_specs=pl.BlockSpec((groups, length), lambda g, order: (0, 0)),
-            scratch_shapes=[
+            in_specs=[
+                spec,
+                spec,
+                pl.BlockSpec((1, BLOCK, width), lambda g, order: (g, 0, 0)),
+            ],
+            out_specs=[spec, pl.BlockSpec((groups, length), lambda g, order: (0, 0))],
+            scratch_shapes=conv_scratch(rows // 2)
+            + [
                 pltpu.VMEM((rows, BLOCK), jnp.bfloat16),
-                pltpu.VMEM((rows + GROUP, BLOCK), jnp.bfloat16),
+                pltpu.VMEM((rows + BLOCK, BLOCK), jnp.bfloat16),
                 pltpu.VMEM((BLOCK, length), jnp.float32),
             ],
         ),
-        out_shape=jax.ShapeDtypeStruct((groups, length), jnp.float32),
-        compiler_params=params(),
-        cost_estimate=pl.CostEstimate(
-            flops=groups * rows * BLOCK * length,
-            bytes_accessed=4 * x.size,
+        out_shape=[
+            jax.ShapeDtypeStruct(x.shape, jnp.bfloat16),
+            jax.ShapeDtypeStruct((groups, length), jnp.float32),
+        ],
+        compiler_params=params(),
+        cost_estimate=pl.CostEstimate(
+            flops=2 * groups * rows * BLOCK * length,
+            bytes_accessed=6 * x.size + 2 * strip.size,
             transcendentals=0,
         ),
-    )(order, x, w)
+    )(order, x, w, strip)
 
 
 def post_kernel(tiles, r_ref, a_ref, b_ref, out_a_ref, out_b_ref):
@@ -242,7 +288,7 @@
         ],
         out_specs=[spec, spec],
         out_shape=[shape, shape],
-        compiler_params=params(),
+        compiler_params=params(32),
         cost_estimate=pl.CostEstimate(
             flops=2 * a.size, bytes_accessed=10 * a.size, transcendentals=0
         ),
@@ -281,17 +327,17 @@
 
 
 def shards(output_gate_input, key_input, value_input, upstream, filter_taps, order):
-    groups = filter_taps.shape[0]
-    product = exchange(pre(key_input, value_input))
-    weighted = exchange(pre(upstream, output_gate_input))
-    strip = strips(filter_taps)
-    mixing = exchange(conv(order, product, strip, False))
-    lag_sums = lag_sums_of(order, product, weighted, groups)
-    returned = exchange(conv(order, weighted, strip, True))
+    product_tiles = pre(key_input, value_input)
+    product = exchange(product_tiles)
+    weighted_tiles, strip = pre_and_strips(upstream, output_gate_input, filter_taps)
+    weighted = exchange(weighted_tiles)
+    mixing = exchange(forward(order, product, strip))
+    returned_tiles, lag_sums = back(order, product, weighted, strip)
+    returned = exchange(returned_tiles)
     lag_total = sum_over_dp(lag_sums)
     mixed_out, gate_grad = post(mixing, output_gate_input, upstream)
+    taps_grad = taps_grad_of(filter_taps, lag_total, lax.axis_size("dp"))
     key_grad, value_grad = post(returned, value_input, key_input)
-    taps_grad = taps_grad_of(filter_taps, lag_total, lax.axis_size("dp"))
     return mixed_out, gate_grad, key_grad, value_grad, taps_grad
 
 

time: 149 us -> 136 us (0.913)
  local copies, waits for them, and re-layouts: 11.7 us -> 2.22 us
  waiting for transfers between devices: 30.3 us -> 25 us
  other arithmetic: 0.05 us -> 1.61 us
    unnamed x32 -> x12, local copies, waits for them, and re-layouts: 11.7 us -> 2.22 us
    all_to_all x4, waiting for transfers between devices: 14.5 us -> 8.87 us  [exchange(): return lax.all_to_all(tiles, 'ctx', split_axis=0, concat_axis=0, tiled=True)]
    add x3, other arithmetic: 0.05 us -> 1.61 us  [sum_over_dp(): x = x + lax.ppermute(x, 'dp', [(i, i ^ step) for i in range(size)])]
    pallas_call x4 -> x3, Pallas kernels: 48.9 us -> 48.1 us  [the longest x1 24.6 us: back(): pl.pallas_call(back_kernel, grid_spec=pltpu.PrefetchScalarGridSpec(num_sc...]
    pallas_call x2 -> x1, Pallas kernels: 6.41 us -> 5.79 us  [pre(): pl.pallas_call(functools.partial(pre_kernel, tiles), grid=(pieces // tile...]
  transfers between devices with their start and end apart: 7 -> 7, of which waited for: 5 -> 5; matrix products, arithmetic and copies ran while one was open for 0% -> 1% of each run, Pallas kernels for 40% -> 41%
where the time goes in v2:
time: 136 us; the launch traced here: 134 us
  Pallas kernels  67 us (49%)
  starting transfers between devices  37.6 us (28%)
  waiting for transfers between devices  25 us (18%)
  local copies, waits for them, and re-layouts  2.22 us (2%)
  other arithmetic  1.61 us (1%)
    all_to_all x4, starting transfers between devices, exchange(): return lax.all_to_all(tiles, 'ctx', split_axis=0, concat_axis=0, tiled=True)  25.9 us
    pallas_call x1, Pallas kernels, back(): pl.pallas_call(back_kernel, grid_spec=pltpu.PrefetchScalarGridSpec(num_sc...  24.6 us
    ppermute x3, waiting for transfers between devices, sum_over_dp(): x = x + lax.ppermute(x, 'dp', [(i, i ^ step) for i in range(size)])  16.1 us
    pallas_call x1, Pallas kernels, pre_and_strips(): pl.pallas_call(functools.partial(pre_strip_kernel, tiles), grid=(groups,)...  12.4 us
    ppermute x3, starting transfers between devices, sum_over_dp(): x = x + lax.ppermute(x, 'dp', [(i, i ^ step) for i in range(size)])  11.6 us
    pallas_call x2, Pallas kernels, post(): pl.pallas_call(functools.partial(post_kernel, tiles), grid=(pieces // til...  11.4 us
    pallas_call x1, Pallas kernels, forward(): pl.pallas_call(functools.partial(conv_kernel, False), grid_spec=pltpu.Pre...  11.1 us
    all_to_all x4, waiting for transfers between devices, exchange(): return lax.all_to_all(tiles, 'ctx', split_axis=0, concat_axis=0, tiled=True)  8.87 us
  transfers between devices with their start and end apart: 7, of which 5 were waited for; matrix products, arithmetic and copies ran while one was open for 1% of the time, Pallas kernels for 41%

profile of v2, /device:TPU:2, one launch (start us, length us, event | category | flops | bytes accessed | tf_op | source)
XLA Modules:
  0.0 134.1 jit_solution(3183682802700656527)
XLA Ops:
  0.6 5.8 %shard_map.101 = bf16[32,128,128]{2,1,0:T(8,128)(2,1)} custom-call(bf16[1,128,4096]{2,1,0:T(8,128)(2,1)} %b_ref.7, bf16[1,128,4096]{2,1,0:T(8,128)(2,1)} %a_ref.7), custom_call_target="tpu_custom_call" | custom-call | flops 524288 | bytes 3145728 | tf_op jit(solution)/shard_map/pallas_call | solution.py:45
  6.4 7.6 %all-to-all-start = ((bf16[32,128,128]{2,1,0:T(8,128)(2,1)}), bf16[32,128,128]{2,1,0:T(8,128)(2,1)S(1)}, u32[]{:S(2)}, u32[]{:S(2)}) async-start(bf16[32,128,128]{2,1,0:T(8,128)(2,1)} %shard_map.101), calls=%async_computation | async-start | bytes 2097152 | tf_op jit(solution)/shard_map/all_to_all | solution.py:317
  14.0 12.4 %shard_map.102 = (bf16[32,128,128]{2,1,0:T(8,128)(2,1)}, bf16[8,128,4224]{2,1,0:T(8,128)(2,1)}) custom-call(bf16[1,128,4096]{2,1,0:T(8,128)(2,1)} %b_ref.6, bf16[1,128,4096]{2,1,0:T(8,128)(2,1)} %a_ref.6, f32[8,4096]{1,0:T(8,128)} %taps_ref.3), custom_call_target="tpu_custom_call" | custom-call | flops 17301504 | bytes 11796480 | tf_op jit(solution)/shard_map/pallas_call | solution.py:89
  26.4 3.7 %all-to-all-done.x_ref = bf16[32,128,128]{2,1,0:T(8,128)(2,1)S(1)} async-done(((bf16[32,128,128]{2,1,0:T(8,128)(2,1)}), bf16[32,128,128]{2,1,0:T(8,128)(2,1)S(1)}, u32[]{:S(2)}, u32[]{:S(2)}) %all-to-all-start) | async-done | bytes 1048608 | tf_op jit(solution)/shard_map/all_to_all | solution.py:317
  30.2 5.0 %all-to-all-start.2 = ((bf16[32,128,128]{2,1,0:T(8,128)(2,1)}), bf16[32,128,128]{2,1,0:T(8,128)(2,1)S(1)}, u32[]{:S(2)}, u32[]{:S(2)}) async-start(bf16[32,128,128]{2,1,0:T(8,128)(2,1)} %get-tuple-element.16), calls=%async_computation.2 | async-start | bytes 2097152 | tf_op jit(solution)/shard_map/all_to_all | solution.py:317
  35.2 0.0 copy-done.4
  35.2 11.1 %shard_map.103 = bf16[32,128,128]{2,1,0:T(8,128)(2,1)} custom-call(s32[32]{0:T(128)} %order_ref.3, bf16[32,128,128]{2,1,0:T(8,128)(2,1)} %copy-done.4, bf16[8,128,4224]{2,1,0:T(8,128)(2,1)} %get-tuple-element.13.strip_ref), custom_call_target="tpu_custom_call" | custom-call | flops 1073741824 | bytes 10747904 | tf_op jit(solution)/shard_map/pallas_call | solution.py:169
  46.3 5.1 %all-to-all-done.2.w_ref = bf16[32,128,128]{2,1,0:T(8,128)(2,1)S(1)} async-done(((bf16[32,128,128]{2,1,0:T(8,128)(2,1)}), bf16[32,128,128]{2,1,0:T(8,128)(2,1)S(1)}, u32[]{:S(2)}, u32[]{:S(2)}) %all-to-all-start.2) | async-done | bytes 1048608 | tf_op jit(solution)/shard_map/all_to_all | solution.py:317
  51.4 1.0 copy-done.5
  52.4 5.7 %all-to-all-start.1 = ((bf16[32,128,128]{2,1,0:T(8,128)(2,1)}), bf16[32,128,128]{2,1,0:T(8,128)(2,1)}, u32[]{:S(2)}, u32[]{:S(2)}) async-start(bf16[32,128,128]{2,1,0:T(8,128)(2,1)} %shard_map.103), calls=%async_computation.1 | async-start | bytes 2097152 | tf_op jit(solution)/shard_map/all_to_all | solution.py:317
  58.1 0.0 copy-start.2
  58.1 0.0 copy-start
  58.2 0.0 copy-start.1
  58.2 24.6 %shard_map.105 = (bf16[32,128,128]{2,1,0:T(8,128)(2,1)}, f32[8,4096]{1,0:T(8,128)}) custom-call(s32[32]{0:T(128)} %order_ref.3, bf16[32,128,128]{2,1,0:T(8,128)(2,1)} %copy-done.4, bf16[32,128,128]{2,1,0:T(8,128)(2,1)} %copy-done.5, bf16[8,128,4224]{2,1,0:T(8,128)(2,1)} %get-tuple-element.13.strip_ref), custom_call_target="tpu_custom_call" | custom-call | flops 4294967296 | bytes 11796480 | tf_op jit(solution)/shard_map/pallas_call | solution.py:236
  82.8 0.0 all-to-all-done.1.r_ref
  82.8 7.5 %all-to-all-start.3 = ((bf16[32,128,128]{2,1,0:T(8,128)(2,1)}), bf16[32,128,128]{2,1,0:T(8,128)(2,1)}, u32[]{:S(2)}, u32[]{:S(2)}) async-start(bf16[32,128,128]{2,1,0:T(8,128)(2,1)} %get-tuple-element.17), calls=%async_computation.3 | async-start | bytes 2097152 | tf_op jit(solution)/shard_map/all_to_all | solution.py:317
  90.3 2.0 %collective-permute-start = (f32[8,4096]{1,0:T(8,128)}, f32[8,4096]{1,0:T(8,128)S(1)}, u32[]{:S(2)}, u32[]{:S(2)}) collective-permute-start(f32[8,4096]{1,0:T(8,128)} %get-tuple-element.20), channel_id=1, source_target_pairs={{0,32},{32,0},{64,96},{96,64},{128,160},{160,128},{192,224},{224,1... | collective-permute-start | bytes 393224 | tf_op jit(solution)/shard_map/ppermute | solution.py:324
  92.3 4.0 %collective-permute-done = f32[8,4096]{1,0:T(8,128)S(1)} collective-permute-done((f32[8,4096]{1,0:T(8,128)}, f32[8,4096]{1,0:T(8,128)S(1)}, u32[]{:S(2)}, u32[]{:S(2)}) %collective-permute-start) | collective-permute-done | bytes 131104 | tf_op jit(solution)/shard_map/ppermute | solution.py:324
  96.4 0.9 add.9
  97.3 3.4 %collective-permute-start.1 = (f32[8,4096]{1,0:T(8,128)S(1)}, f32[8,4096]{1,0:T(8,128)S(1)}, u32[]{:S(2)}, u32[]{:S(2)}) collective-permute-start(f32[8,4096]{1,0:T(8,128)S(1)} %add.9), channel_id=1, source_target_pairs={{0,64},{32,96},{64,0},{96,32},{128,192},{160,224},{192,128},{224,1... | collective-permute-start | bytes 393224 | tf_op jit(solution)/shard_map/ppermute | solution.py:324
  100.6 6.1 %collective-permute-done.1 = f32[8,4096]{1,0:T(8,128)S(1)} collective-permute-done((f32[8,4096]{1,0:T(8,128)S(1)}, f32[8,4096]{1,0:T(8,128)S(1)}, u32[]{:S(2)}, u32[]{:S(2)}) %collective-permute-start.1) | collective-permute-done | bytes 131104 | tf_op jit(solution)/shard_map/ppermute | solution.py:324
  106.8 6.3 %collective-permute-start.2 = (f32[8,4096]{1,0:T(8,128)S(1)}, f32[8,4096]{1,0:T(8,128)S(1)}, u32[]{:S(2)}, u32[]{:S(2)}) collective-permute-start(f32[8,4096]{1,0:T(8,128)S(1)} %add.10), channel_id=1, source_target_pairs={{0,128},{32,160},{64,192},{96,224},{128,0},{160,32},{192,64},{224,... | collective-permute-start | bytes 393224 | tf_op jit(solution)/shard_map/ppermute | solution.py:324
  113.0 6.0 %collective-permute-done.2 = f32[8,4096]{1,0:T(8,128)S(1)} collective-permute-done((f32[8,4096]{1,0:T(8,128)S(1)}, f32[8,4096]{1,0:T(8,128)S(1)}, u32[]{:S(2)}, u32[]{:S(2)}) %collective-permute-start.2) | collective-permute-done | bytes 131104 | tf_op jit(solution)/shard_map/ppermute | solution.py:324
  119.0 0.7 add.11.lag_ref
  119.7 1.8 %shard_map.107 = f32[8,4096]{1,0:T(8,128)} custom-call(f32[8,4096]{1,0:T(8,128)} %taps_ref.3, f32[8,4096]{1,0:T(8,128)} %add.11.lag_ref), custom_call_target="tpu_custom_call" | custom-call | tf_op jit(solution)/shard_map/pallas_call | solution.py:309
  121.5 0.0 copy-done.2
  121.5 1.2 copy-done.3
  122.7 5.7 %shard_map.104 = (bf16[1,128,4096]{2,1,0:T(8,128)(2,1)}, bf16[1,128,4096]{2,1,0:T(8,128)(2,1)}) custom-call(bf16[32,128,128]{2,1,0:T(8,128)(2,1)} %all-to-all-done.1.r_ref, bf16[1,128,4096]{2,1,0:T(8,128)(2,1)S(1)} %copy-done.3, bf16[1,128,4096]{2,1,0:T(8,128)(2,1)S(1)} %copy-done.2), custom_call_target="tpu_custom_call" | custom-call | flops 1048576 | bytes 5242880 | tf_op jit(solution)/shard_map/pallas_call | solution.py:281
  128.4 0.0 all-to-all-done.3.r_ref
  128.4 0.0 copy-done
  128.4 0.0 copy-done.1
  128.4 5.7 %shard_map.106 = (bf16[1,128,4096]{2,1,0:T(8,128)(2,1)}, bf16[1,128,4096]{2,1,0:T(8,128)(2,1)}) custom-call(bf16[32,128,128]{2,1,0:T(8,128)(2,1)} %all-to-all-done.3.r_ref, bf16[1,128,4096]{2,1,0:T(8,128)(2,1)S(1)} %copy-done.1, bf16[1,128,4096]{2,1,0:T(8,128)(2,1)S(1)} %copy-done), custom_call_target="tpu_custom_call" | custom-call | flops 1048576 | bytes 5242880 | tf_op jit(solution)/shard_map/pallas_call | solution.py:281
  (4 shorter events, 0.0 us)
Async XLA Ops:
  6.4 23.7 %all-to-all-start = ((bf16[32,128,128]{2,1,0:T(8,128)(2,1)}), bf16[32,128,128]{2,1,0:T(8,128)(2,1)S(1)}, u32[]{:S(2)}, u32[]{:S(2)}) async-start(bf16[32,128,128]{2,1,0:T(8,128)(2,1)} %shard_map.101), calls=%async_computation | async-start | bytes 2097152 | tf_op jit(solution)/shard_map/all_to_all | solution.py:317
  30.2 5.1 %copy-start.4 = (bf16[32,128,128]{2,1,0:T(8,128)(2,1)}, bf16[32,128,128]{2,1,0:T(8,128)(2,1)S(1)}, u32[]{:S(2)}) copy-start(bf16[32,128,128]{2,1,0:T(8,128)(2,1)S(1)} %all-to-all-done.x_ref) | copy-start | bytes 3145732
  30.2 21.3 %all-to-all-start.2 = ((bf16[32,128,128]{2,1,0:T(8,128)(2,1)}), bf16[32,128,128]{2,1,0:T(8,128)(2,1)S(1)}, u32[]{:S(2)}, u32[]{:S(2)}) async-start(bf16[32,128,128]{2,1,0:T(8,128)(2,1)} %get-tuple-element.16), calls=%async_computation.2 | async-start | bytes 2097152 | tf_op jit(solution)/shard_map/all_to_all | solution.py:317
  51.4 1.0 copy-start.5
  52.4 30.4 %all-to-all-start.1 = ((bf16[32,128,128]{2,1,0:T(8,128)(2,1)}), bf16[32,128,128]{2,1,0:T(8,128)(2,1)}, u32[]{:S(2)}, u32[]{:S(2)}) async-start(bf16[32,128,128]{2,1,0:T(8,128)(2,1)} %shard_map.103), calls=%async_computation.1 | async-start | bytes 2097152 | tf_op jit(solution)/shard_map/all_to_all | solution.py:317
  58.1 63.3 %copy-start.2 = (bf16[1,128,4096]{2,1,0:T(8,128)(2,1)S(1)}, bf16[1,128,4096]{2,1,0:T(8,128)(2,1)}, u32[]{:S(2)}) copy-start(bf16[1,128,4096]{2,1,0:T(8,128)(2,1)} %b_ref.6) | copy-start | bytes 3145732
  58.1 70.3 %copy-start = (bf16[1,128,4096]{2,1,0:T(8,128)(2,1)S(1)}, bf16[1,128,4096]{2,1,0:T(8,128)(2,1)}, u32[]{:S(2)}) copy-start(bf16[1,128,4096]{2,1,0:T(8,128)(2,1)} %b_ref.7) | copy-start | bytes 3145732
  58.2 70.2 %copy-start.1 = (bf16[1,128,4096]{2,1,0:T(8,128)(2,1)S(1)}, bf16[1,128,4096]{2,1,0:T(8,128)(2,1)}, u32[]{:S(2)}) copy-start(bf16[1,128,4096]{2,1,0:T(8,128)(2,1)} %a_ref.7) | copy-start | bytes 3145732
  82.8 45.6 %all-to-all-start.3 = ((bf16[32,128,128]{2,1,0:T(8,128)(2,1)}), bf16[32,128,128]{2,1,0:T(8,128)(2,1)}, u32[]{:S(2)}, u32[]{:S(2)}) async-start(bf16[32,128,128]{2,1,0:T(8,128)(2,1)} %get-tuple-element.17), calls=%async_computation.3 | async-start | bytes 2097152 | tf_op jit(solution)/shard_map/all_to_all | solution.py:317
  90.3 6.0 %collective-permute-start = (f32[8,4096]{1,0:T(8,128)}, f32[8,4096]{1,0:T(8,128)S(1)}, u32[]{:S(2)}, u32[]{:S(2)}) collective-permute-start(f32[8,4096]{1,0:T(8,128)} %get-tuple-element.20), channel_id=1, source_target_pairs={{0,32},{32,0},{64,96},{96,64},{128,160},{160,128},{192,224},{224,1... | collective-permute-start | bytes 393224 | tf_op jit(solution)/shard_map/ppermute | solution.py:324
  97.3 9.4 %collective-permute-start.1 = (f32[8,4096]{1,0:T(8,128)S(1)}, f32[8,4096]{1,0:T(8,128)S(1)}, u32[]{:S(2)}, u32[]{:S(2)}) collective-permute-start(f32[8,4096]{1,0:T(8,128)S(1)} %add.9), channel_id=1, source_target_pairs={{0,64},{32,96},{64,0},{96,32},{128,192},{160,224},{192,128},{224,1... | collective-permute-start | bytes 393224 | tf_op jit(solution)/shard_map/ppermute | solution.py:324
  106.8 12.3 %collective-permute-start.2 = (f32[8,4096]{1,0:T(8,128)S(1)}, f32[8,4096]{1,0:T(8,128)S(1)}, u32[]{:S(2)}, u32[]{:S(2)}) collective-permute-start(f32[8,4096]{1,0:T(8,128)S(1)} %add.10), channel_id=1, source_target_pairs={{0,128},{32,160},{64,192},{96,224},{128,0},{160,32},{192,64},{224,... | collective-permute-start | bytes 393224 | tf_op jit(solution)/shard_map/ppermute | solution.py:324
  121.5 1.2 copy-start.3

commit v3 on v2

--- a/solution.py
+++ b/solution.py
@@ -13,6 +13,7 @@
 GROUP = 16
 MIB = 1024 * 1024
 SPAN = 4
+CHUNKS = 4
 
 NN = (((1,), (0,)), ((), ()))
 NT = (((1,), (1,)), ((), ()))
@@ -31,23 +32,61 @@
     return a * b
 
 
-def pre_kernel(tiles, a_ref, b_ref, out_ref):
-    for i in range(tiles):
-        cols = slice(i * BLOCK, (i + 1) * BLOCK)
-        out_ref[i] = product_of(a_ref[0, :, cols], b_ref[0, :, cols]).T
+def copies(source, target, sems, chunks):
+    step = source.shape[-1] // chunks
+    made = []
+    for i in range(chunks):
+        cols = pl.ds(i * step, step)
+        made.append(
+            pltpu.make_async_copy(source.at[0, :, cols], target.at[0, :, cols], sems.at[i])
+        )
+    return made
+
+
+def tile_copies(source, target, sems, chunks):
+    step = source.shape[0] // chunks
+    made = []
+    for i in range(chunks):
+        part = pl.ds(i * step, step)
+        made.append(pltpu.make_async_copy(source.at[part], target.at[part], sems.at[i]))
+    return made
+
+
+def pre_kernel(a_hbm, b_hbm, out_hbm, a, b, out, a_sem, b_sem, out_sem):
+    into = list(
+        zip(copies(a_hbm, a, a_sem, CHUNKS), copies(b_hbm, b, b_sem, CHUNKS), strict=True)
+    )
+    back = tile_copies(out, out_hbm, out_sem, CHUNKS)
+    for pair in into:
+        for copy in pair:
+            copy.start()
+    tiles = out.shape[0] // CHUNKS
+    for i in range(CHUNKS):
+        for copy in into[i]:
+            copy.wait()
+        for t in range(i * tiles, (i + 1) * tiles):
+            cols = slice(t * BLOCK, (t + 1) * BLOCK)
+            out[t] = product_of(a[0, :, cols], b[0, :, cols]).T
+        back[i].start()
+    for copy in back:
+        copy.wait()
 
 
 def pre(a, b):
     _, rows, channels = a.shape
-    pieces = channels // BLOCK
-    tiles = 4
-    spec = pl.BlockSpec((1, rows, tiles * BLOCK), lambda i: (0, 0, i))
-    return pl.pallas_call(
-        functools.partial(pre_kernel, tiles),
-        grid=(pieces // tiles,),
-        in_specs=[spec, spec],
-        out_specs=pl.BlockSpec((tiles, BLOCK, rows), lambda i: (i, 0, 0)),
-        out_shape=jax.ShapeDtypeStruct((pieces, BLOCK, rows), jnp.bfloat16),
+    tiles = (channels // BLOCK, BLOCK, rows)
+    anywhere = pl.BlockSpec(memory_space=pl.ANY)
+    return pl.pallas_call(
+        pre_kernel,
+        in_specs=[anywhere, anywhere],
+        out_specs=anywhere,
+        out_shape=jax.ShapeDtypeStruct(tiles, jnp.bfloat16),
+        scratch_shapes=[
+            pltpu.VMEM(a.shape, jnp.bfloat16),
+            pltpu.VMEM(b.shape, jnp.bfloat16),
+            pltpu.VMEM(tiles, jnp.bfloat16),
+        ]
+        + [pltpu.SemaphoreType.DMA((CHUNKS,))] * 3,
         compiler_params=params(),
         cost_estimate=pl.CostEstimate(
             flops=a.size, bytes_accessed=6 * a.size, transcendentals=0
@@ -75,7 +114,9 @@
 
 
 def pre_strip_kernel(tiles, a_ref, b_ref, taps_ref, out_ref, strip_ref):
-    pre_kernel(tiles, a_ref, b_ref, out_ref)
+    for i in range(tiles):
+        cols = slice(i * BLOCK, (i + 1) * BLOCK)
+        out_ref[i] = product_of(a_ref[0, :, cols], b_ref[0, :, cols]).T
     strip_kernel(taps_ref, strip_ref)
 
 
@@ -122,7 +163,7 @@
         xs[:, :spare, :] = jnp.zeros((2, spare, BLOCK), jnp.bfloat16)
     for d in range(pieces):
         b = order_ref[d]
-        xs[b % 2, rows_of(b // 2 + first), :] = x_ref[d]
+        xs[b % 2, rows_of(b // 2 + first), :] = x_ref[d, rows_of(pl.program_id(0)), :]
     wide = 2 * BLOCK
     for lag in range(0, rows // GROUP, SPAN):
         depth = rows - GROUP * lag
@@ -172,7 +213,7 @@
             num_scalar_prefetch=1,
             grid=(groups,),
             in_specs=[
-                spec,
+                pl.BlockSpec(x.shape, lambda g, order: (0, 0, 0)),
                 pl.BlockSpec((1, BLOCK, width), lambda g, order: (g, 0, 0)),
             ],
             out_specs=spec,
@@ -188,43 +229,51 @@
     )(order, x, strip)
 
 
-def lag_kernel(order_ref, x_ref, w_ref, out_ref, xs, ws, squares):
+def lag_kernel(order_ref, x_ref, w_ref, out_ref, xs, ws, squares, sums):
     pieces = x_ref.shape[0]
     total = GROUP * pieces
+    last = BLOCK - 1
+    g = pl.program_id(0)
     for d in range(pieces):
         rows = rows_of(order_ref[d])
-        xs[rows, :] = x_ref[d]
-        ws[rows, :] = w_ref[d]
+        xs[rows, :] = x_ref[d, rows_of(g), :]
+        ws[rows, :] = w_ref[d, rows_of(g), :]
     ws[total:, :] = jnp.zeros((BLOCK, BLOCK), jnp.bfloat16)
-    x_turned = xs[...].T
+    row = lax.broadcasted_iota(jnp.int32, (BLOCK, BLOCK), 0)
+    col = lax.broadcasted_iota(jnp.int32, (BLOCK, BLOCK), 1)
+    mirror = jnp.where(row + col == last, 1.0, 0.0).astype(jnp.bfloat16)
+    x_turned = dot(mirror, xs[...], NT).astype(jnp.bfloat16)
     for lag in range(0, pieces, 2):
         depth = total - GROUP * lag // BLOCK * BLOCK
         start = GROUP * lag
-        if start + GROUP + depth > total + BLOCK:
-            raise ValueError("spare rows")
         right = jnp.concatenate(
             [ws[start : start + depth, :], ws[start + GROUP : start + GROUP + depth, :]],
             axis=1,
         )
         squares[:, lag * BLOCK : (lag + 2) * BLOCK] = dot(x_turned[:, :depth], right, NN)
-    row = lax.broadcasted_iota(jnp.int32, (BLOCK, BLOCK), 0)
-    col = lax.broadcasted_iota(jnp.int32, (BLOCK, BLOCK), 1)
-    squares[:, :BLOCK] = jnp.where(col >= row, squares[:, :BLOCK], 0.0)
-    width = squares.shape[1]
-    cur = squares[BLOCK - 8 :, :]
-    for q in range(BLOCK // 8 - 2, -1, -1):
-        cur = pltpu.roll(cur, width - 8, 1) + squares[8 * q : 8 * (q + 1), :]
-    line = lax.broadcasted_iota(jnp.int32, (8, width), 0)
-    for step in (1, 2, 4):
-        cur = jnp.where((line & step) != 0, pltpu.roll(cur, width - step, 1), cur)
-    out_ref[pl.ds(pl.program_id(0), 1), :] = jnp.sum(cur, axis=0, keepdims=True)
+    squares[:, pieces * BLOCK :] = jnp.zeros((BLOCK, BLOCK), jnp.float32)
+    step = 8
+    for t in range(0, pieces, step):
+        cols = slice(t * BLOCK, (t + step + 1) * BLOCK)
+        added = None
+        for q in range(BLOCK // 8):
+            moved = pltpu.roll(squares[8 * q : 8 * q + 8, cols], 8 * q, 1, stride=1, stride_axis=0)
+            added = moved if added is None else added + moved
+        added = jnp.sum(added, axis=0, keepdims=True)
+        skip = BLOCK if t else 0
+        sums[pl.ds(g, 1), t * BLOCK + skip : (t + step + 1) * BLOCK] = added[:, skip:]
+
+    @pl.when(g == pl.num_programs(0) - 1)
+    def _():
+        width = sums.shape[1]
+        out_ref[...] = pltpu.roll(sums[...], width - last, 1)[:, : pieces * BLOCK]
 
 
 def back_kernel(
-    order_ref, x_ref, w_ref, strip_ref, out_ref, lag_ref, pairs, acc, xs, ws, squares
+    order_ref, x_ref, w_ref, strip_ref, out_ref, lag_ref, pairs, acc, xs, ws, squares, sums
 ):
     conv_kernel(True, order_ref, w_ref, strip_ref, out_ref, pairs, acc)
-    lag_kernel(order_ref, x_ref, w_ref, lag_ref, xs, ws, squares)
+    lag_kernel(order_ref, x_ref, w_ref, lag_ref, xs, ws, squares, sums)
 
 
 def back(order, x, w, strip):
@@ -239,8 +288,8 @@
             num_scalar_prefetch=1,
             grid=(groups,),
             in_specs=[
-                spec,
-                spec,
+                pl.BlockSpec(x.shape, lambda g, order: (0, 0, 0)),
+                pl.BlockSpec(x.shape, lambda g, order: (0, 0, 0)),
                 pl.BlockSpec((1, BLOCK, width), lambda g, order: (g, 0, 0)),
             ],
             out_specs=[spec, pl.BlockSpec((groups, length), lambda g, order: (0, 0))],
@@ -248,7 +297,8 @@
             + [
                 pltpu.VMEM((rows, BLOCK), jnp.bfloat16),
                 pltpu.VMEM((rows + BLOCK, BLOCK), jnp.bfloat16),
-                pltpu.VMEM((BLOCK, length), jnp.float32),
+                pltpu.VMEM((BLOCK, length + BLOCK), jnp.float32),
+                pltpu.VMEM((groups, length + BLOCK), jnp.float32),
             ],
         ),
         out_shape=[
@@ -264,31 +314,51 @@
     )(order, x, w, strip)
 
 
-def post_kernel(tiles, r_ref, a_ref, b_ref, out_a_ref, out_b_ref):
-    for i in range(tiles):
-        cols = slice(i * BLOCK, (i + 1) * BLOCK)
-        turned = r_ref[i].T
-        out_a_ref[0, :, cols] = product_of(a_ref[0, :, cols], turned)
-        out_b_ref[0, :, cols] = product_of(b_ref[0, :, cols], turned)
+def post_kernel(
+    r_hbm, a_hbm, b_hbm, x_hbm, y_hbm, r, a, b, x, y, r_sem, a_sem, b_sem, x_sem, y_sem
+):
+    into = list(
+        zip(
+            tile_copies(r_hbm, r, r_sem, CHUNKS),
+            copies(a_hbm, a, a_sem, CHUNKS),
+            copies(b_hbm, b, b_sem, CHUNKS),
+            strict=True,
+        )
+    )
+    back = list(
+        zip(copies(x, x_hbm, x_sem, CHUNKS), copies(y, y_hbm, y_sem, CHUNKS), strict=True)
+    )
+    for group in into:
+        for copy in group:
+            copy.start()
+    tiles = r.shape[0] // CHUNKS
+    for i in range(CHUNKS):
+        for copy in into[i]:
+            copy.wait()
+        for t in range(i * tiles, (i + 1) * tiles):
+            cols = slice(t * BLOCK, (t + 1) * BLOCK)
+            turned = r[t].T
+            x[0, :, cols] = product_of(a[0, :, cols], turned)
+            y[0, :, cols] = product_of(b[0, :, cols], turned)
+        for copy in back[i]:
+            copy.start()
+    for group in back:
+        for copy in group:
+            copy.wait()
 
 
 def post(r, a, b):
-    _, rows, channels = a.shape
-    pieces = channels // BLOCK
-    tiles = 4
-    spec = pl.BlockSpec((1, rows, tiles * BLOCK), lambda i: (0, 0, i))
+    anywhere = pl.BlockSpec(memory_space=pl.ANY)
     shape = jax.ShapeDtypeStruct(a.shape, a.dtype)
     return pl.pallas_call(
-        functools.partial(post_kernel, tiles),
-        grid=(pieces // tiles,),
-        in_specs=[
-            pl.BlockSpec((tiles, BLOCK, rows), lambda i: (i, 0, 0)),
-            spec,
-            spec,
-        ],
-        out_specs=[spec, spec],
+        post_kernel,
+        in_specs=[anywhere] * 3,
+        out_specs=[anywhere] * 2,
         out_shape=[shape, shape],
-        compiler_params=params(32),
+        scratch_shapes=[pltpu.VMEM(r.shape, r.dtype)]
+        + [pltpu.VMEM(a.shape, a.dtype)] * 4
+        + [pltpu.SemaphoreType.DMA((CHUNKS,))] * 5,
+        compiler_params=params(),
         cost_estimate=pl.CostEstimate(
             flops=2 * a.size, bytes_accessed=10 * a.size, transcendentals=0
         ),

time: 136 us -> 117 us (0.86)
  Pallas kernels: 67 us -> 50.5 us
    pallas_call x3, Pallas kernels: 17.2 us -> 8.36 us  [the longest x2 5.91 us: post(): pl.pallas_call(post_kernel, in_specs=[anywhere] * 3, out_specs=[anywhere]...]
    pallas_call x1, Pallas kernels: 24.6 us -> 16.8 us  [back(): pl.pallas_call(back_kernel, grid_spec=pltpu.PrefetchScalarGridSpec(num_sc...]
  transfers between devices with their start and end apart: 7 -> 7, of which waited for: 5 -> 5; matrix products, arithmetic and copies ran while one was open for 1% -> 1% of each run, Pallas kernels for 41% -> 39%
where the time goes in v3:
time: 117 us; the launch traced here: 115 us
  Pallas kernels  50.5 us (43%)
  starting transfers between devices  36.9 us (32%)
  waiting for transfers between devices  24.8 us (21%)
  other arithmetic  1.61 us (1%)
    all_to_all x4, starting transfers between devices, exchange(): return lax.all_to_all(tiles, 'ctx', split_axis=0, concat_axis=0, tiled=True)  25.2 us
    pallas_call x1, Pallas kernels, back(): pl.pallas_call(back_kernel, grid_spec=pltpu.PrefetchScalarGridSpec(num_sc...  16.8 us
    ppermute x3, waiting for transfers between devices, sum_over_dp(): x = x + lax.ppermute(x, 'dp', [(i, i ^ step) for i in range(size)])  16 us
    pallas_call x1, Pallas kernels, pre_and_strips(): pl.pallas_call(functools.partial(pre_strip_kernel, tiles), grid=(groups,)...  12.4 us
    ppermute x3, starting transfers between devices, sum_over_dp(): x = x + lax.ppermute(x, 'dp', [(i, i ^ step) for i in range(size)])  11.6 us
    pallas_call x1, Pallas kernels, forward(): pl.pallas_call(functools.partial(conv_kernel, False), grid_spec=pltpu.Pre...  11.2 us
    all_to_all x4, waiting for transfers between devices, exchange(): return lax.all_to_all(tiles, 'ctx', split_axis=0, concat_axis=0, tiled=True)  8.79 us
    pallas_call x2, Pallas kernels, post(): pl.pallas_call(post_kernel, in_specs=[anywhere] * 3, out_specs=[anywhere]...  5.91 us
  transfers between devices with their start and end apart: 7, of which 5 were waited for; matrix products, arithmetic and copies ran while one was open for 1% of the time, Pallas kernels for 39%

profile of v3, /device:TPU:2, one launch (start us, length us, event | category | flops | bytes accessed | tf_op | source)
XLA Modules:
  0.0 115.5 jit_solution(5722140776734983425)
XLA Ops:
  0.6 2.4 %shard_map.101 = bf16[32,128,128]{2,1,0:T(8,128)(2,1)} custom-call(bf16[1,128,4096]{2,1,0:T(8,128)(2,1)} %b_hbm.5, bf16[1,128,4096]{2,1,0:T(8,128)(2,1)} %a_hbm.5), custom_call_target="tpu_custom_call" | custom-call | flops 524288 | bytes 3145728 | tf_op jit(solution)/shard_map/pallas_call | solution.py:79
  3.1 7.6 %all-to-all-start = ((bf16[32,128,128]{2,1,0:T(8,128)(2,1)}), bf16[32,128,128]{2,1,0:T(8,128)(2,1)S(1)}, u32[]{:S(2)}, u32[]{:S(2)}) async-start(bf16[32,128,128]{2,1,0:T(8,128)(2,1)} %shard_map.101), calls=%async_computation | async-start | bytes 2097152 | tf_op jit(solution)/shard_map/all_to_all | solution.py:387
  10.7 12.4 %shard_map.102 = (bf16[32,128,128]{2,1,0:T(8,128)(2,1)}, bf16[8,128,4224]{2,1,0:T(8,128)(2,1)}) custom-call(bf16[1,128,4096]{2,1,0:T(8,128)(2,1)} %b_hbm.4, bf16[1,128,4096]{2,1,0:T(8,128)(2,1)} %a_hbm.4, f32[8,4096]{1,0:T(8,128)} %taps_ref.3), custom_call_target="tpu_custom_call" | custom-call | flops 17301504 | bytes 11796480 | tf_op jit(solution)/shard_map/pallas_call | solution.py:130
  23.1 3.7 %all-to-all-done.x_ref = bf16[32,128,128]{2,1,0:T(8,128)(2,1)S(1)} async-done(((bf16[32,128,128]{2,1,0:T(8,128)(2,1)}), bf16[32,128,128]{2,1,0:T(8,128)(2,1)S(1)}, u32[]{:S(2)}, u32[]{:S(2)}) %all-to-all-start) | async-done | bytes 1048608 | tf_op jit(solution)/shard_map/all_to_all | solution.py:387
  26.8 0.0 copy-start.2
  26.8 5.0 %all-to-all-start.2 = ((bf16[32,128,128]{2,1,0:T(8,128)(2,1)}), bf16[32,128,128]{2,1,0:T(8,128)(2,1)S(1)}, u32[]{:S(2)}, u32[]{:S(2)}) async-start(bf16[32,128,128]{2,1,0:T(8,128)(2,1)} %get-tuple-element.16), calls=%async_computation.2 | async-start | bytes 2097152 | tf_op jit(solution)/shard_map/all_to_all | solution.py:387
  31.9 0.0 copy-done.2
  31.9 11.2 %shard_map.103 = bf16[32,128,128]{2,1,0:T(8,128)(2,1)} custom-call(s32[32]{0:T(128)} %order_ref.3, bf16[32,128,128]{2,1,0:T(8,128)(2,1)} %copy-done.2, bf16[8,128,4224]{2,1,0:T(8,128)(2,1)} %get-tuple-element.13.strip_ref), custom_call_target="tpu_custom_call" | custom-call | flops 1073741824 | bytes 10747904 | tf_op jit(solution)/shard_map/pallas_call | solution.py:210
  43.1 5.0 %all-to-all-done.2.w_ref = bf16[32,128,128]{2,1,0:T(8,128)(2,1)S(1)} async-done(((bf16[32,128,128]{2,1,0:T(8,128)(2,1)}), bf16[32,128,128]{2,1,0:T(8,128)(2,1)S(1)}, u32[]{:S(2)}, u32[]{:S(2)}) %all-to-all-start.2) | async-done | bytes 1048608 | tf_op jit(solution)/shard_map/all_to_all | solution.py:387
  48.1 0.0 copy-start.3
  48.1 5.0 %all-to-all-start.1 = ((bf16[32,128,128]{2,1,0:T(8,128)(2,1)}), bf16[32,128,128]{2,1,0:T(8,128)(2,1)S(1)}, u32[]{:S(2)}, u32[]{:S(2)}) async-start(bf16[32,128,128]{2,1,0:T(8,128)(2,1)} %shard_map.103), calls=%async_computation.1 | async-start | bytes 2097152 | tf_op jit(solution)/shard_map/all_to_all | solution.py:387
  53.2 0.0 copy-done.3
  53.2 16.8 %shard_map.105 = (bf16[32,128,128]{2,1,0:T(8,128)(2,1)}, f32[8,4096]{1,0:T(8,128)}) custom-call(s32[32]{0:T(128)} %order_ref.3, bf16[32,128,128]{2,1,0:T(8,128)(2,1)} %copy-done.2, bf16[32,128,128]{2,1,0:T(8,128)(2,1)} %copy-done.3, bf16[8,128,4224]{2,1,0:T(8,128)(2,1)} %get-tuple-element.13.strip_ref), custom_call_target="tpu_custom_call" | custom-call | flops 4294967296 | bytes 11796480 | tf_op jit(solution)/shard_map/pallas_call | solution.py:285
  70.0 0.0 all-to-all-done.1.r_hbm
  70.0 0.0 copy-start
  70.0 7.5 %all-to-all-start.3 = ((bf16[32,128,128]{2,1,0:T(8,128)(2,1)}), bf16[32,128,128]{2,1,0:T(8,128)(2,1)S(1)}, u32[]{:S(2)}, u32[]{:S(2)}) async-start(bf16[32,128,128]{2,1,0:T(8,128)(2,1)} %get-tuple-element.17), calls=%async_computation.3 | async-start | bytes 2097152 | tf_op jit(solution)/shard_map/all_to_all | solution.py:387
  77.5 2.0 %collective-permute-start = (f32[8,4096]{1,0:T(8,128)}, f32[8,4096]{1,0:T(8,128)S(1)}, u32[]{:S(2)}, u32[]{:S(2)}) collective-permute-start(f32[8,4096]{1,0:T(8,128)} %get-tuple-element.20), channel_id=1, source_target_pairs={{0,32},{32,0},{64,96},{96,64},{128,160},{160,128},{192,224},{224,1... | collective-permute-start | bytes 393224 | tf_op jit(solution)/shard_map/ppermute | solution.py:394
  79.5 4.0 %collective-permute-done = f32[8,4096]{1,0:T(8,128)S(1)} collective-permute-done((f32[8,4096]{1,0:T(8,128)}, f32[8,4096]{1,0:T(8,128)S(1)}, u32[]{:S(2)}, u32[]{:S(2)}) %collective-permute-start) | collective-permute-done | bytes 131104 | tf_op jit(solution)/shard_map/ppermute | solution.py:394
  83.5 0.9 add.9
  84.5 3.4 %collective-permute-start.1 = (f32[8,4096]{1,0:T(8,128)S(1)}, f32[8,4096]{1,0:T(8,128)S(1)}, u32[]{:S(2)}, u32[]{:S(2)}) collective-permute-start(f32[8,4096]{1,0:T(8,128)S(1)} %add.9), channel_id=1, source_target_pairs={{0,64},{32,96},{64,0},{96,32},{128,192},{160,224},{192,128},{224,1... | collective-permute-start | bytes 393224 | tf_op jit(solution)/shard_map/ppermute | solution.py:394
  87.8 6.0 %collective-permute-done.1 = f32[8,4096]{1,0:T(8,128)S(1)} collective-permute-done((f32[8,4096]{1,0:T(8,128)S(1)}, f32[8,4096]{1,0:T(8,128)S(1)}, u32[]{:S(2)}, u32[]{:S(2)}) %collective-permute-start.1) | collective-permute-done | bytes 131104 | tf_op jit(solution)/shard_map/ppermute | solution.py:394
  93.8 6.3 %collective-permute-start.2 = (f32[8,4096]{1,0:T(8,128)S(1)}, f32[8,4096]{1,0:T(8,128)S(1)}, u32[]{:S(2)}, u32[]{:S(2)}) collective-permute-start(f32[8,4096]{1,0:T(8,128)S(1)} %add.10), channel_id=1, source_target_pairs={{0,128},{32,160},{64,192},{96,224},{128,0},{160,32},{192,64},{224,... | collective-permute-start | bytes 393224 | tf_op jit(solution)/shard_map/ppermute | solution.py:394
  100.1 6.0 %collective-permute-done.2 = f32[8,4096]{1,0:T(8,128)S(1)} collective-permute-done((f32[8,4096]{1,0:T(8,128)S(1)}, f32[8,4096]{1,0:T(8,128)S(1)}, u32[]{:S(2)}, u32[]{:S(2)}) %collective-permute-start.2) | collective-permute-done | bytes 131104 | tf_op jit(solution)/shard_map/ppermute | solution.py:394
  106.1 0.7 add.11.lag_ref
  106.8 1.8 %shard_map.107 = f32[8,4096]{1,0:T(8,128)} custom-call(f32[8,4096]{1,0:T(8,128)} %taps_ref.3, f32[8,4096]{1,0:T(8,128)} %add.11.lag_ref), custom_call_target="tpu_custom_call" | custom-call | tf_op jit(solution)/shard_map/pallas_call | solution.py:379
  108.5 0.0 copy-done
  108.5 3.0 %shard_map.104 = (bf16[1,128,4096]{2,1,0:T(8,128)(2,1)}, bf16[1,128,4096]{2,1,0:T(8,128)(2,1)}) custom-call(bf16[32,128,128]{2,1,0:T(8,128)(2,1)} %copy-done, bf16[1,128,4096]{2,1,0:T(8,128)(2,1)} %a_hbm.4, bf16[1,128,4096]{2,1,0:T(8,128)(2,1)} %b_hbm.4), custom_call_target="tpu_custom_call" | custom-call | flops 1048576 | bytes 5242880 | tf_op jit(solution)/shard_map/pallas_call | solution.py:353
  111.5 0.0 all-to-all-done.3.r_hbm
  111.5 0.0 copy-start.1
  111.5 1.0 copy-done.1
  112.5 3.0 %shard_map.106 = (bf16[1,128,4096]{2,1,0:T(8,128)(2,1)}, bf16[1,128,4096]{2,1,0:T(8,128)(2,1)}) custom-call(bf16[32,128,128]{2,1,0:T(8,128)(2,1)} %copy-done.1, bf16[1,128,4096]{2,1,0:T(8,128)(2,1)} %a_hbm.5, bf16[1,128,4096]{2,1,0:T(8,128)(2,1)} %b_hbm.5), custom_call_target="tpu_custom_call" | custom-call | flops 1048576 | bytes 5242880 | tf_op jit(solution)/shard_map/pallas_call | solution.py:353
  (1 shorter events, 0.0 us)
Async XLA Ops:
  3.1 23.8 %all-to-all-start = ((bf16[32,128,128]{2,1,0:T(8,128)(2,1)}), bf16[32,128,128]{2,1,0:T(8,128)(2,1)S(1)}, u32[]{:S(2)}, u32[]{:S(2)}) async-start(bf16[32,128,128]{2,1,0:T(8,128)(2,1)} %shard_map.101), calls=%async_computation | async-start | bytes 2097152 | tf_op jit(solution)/shard_map/all_to_all | solution.py:387
  26.8 5.1 %copy-start.2 = (bf16[32,128,128]{2,1,0:T(8,128)(2,1)}, bf16[32,128,128]{2,1,0:T(8,128)(2,1)S(1)}, u32[]{:S(2)}) copy-start(bf16[32,128,128]{2,1,0:T(8,128)(2,1)S(1)} %all-to-all-done.x_ref) | copy-start | bytes 3145732
  26.8 21.3 %all-to-all-start.2 = ((bf16[32,128,128]{2,1,0:T(8,128)(2,1)}), bf16[32,128,128]{2,1,0:T(8,128)(2,1)S(1)}, u32[]{:S(2)}, u32[]{:S(2)}) async-start(bf16[32,128,128]{2,1,0:T(8,128)(2,1)} %get-tuple-element.16), calls=%async_computation.2 | async-start | bytes 2097152 | tf_op jit(solution)/shard_map/all_to_all | solution.py:387
  48.1 5.1 %copy-start.3 = (bf16[32,128,128]{2,1,0:T(8,128)(2,1)}, bf16[32,128,128]{2,1,0:T(8,128)(2,1)S(1)}, u32[]{:S(2)}) copy-start(bf16[32,128,128]{2,1,0:T(8,128)(2,1)S(1)} %all-to-all-done.2.w_ref) | copy-start | bytes 3145732
  48.1 21.9 %all-to-all-start.1 = ((bf16[32,128,128]{2,1,0:T(8,128)(2,1)}), bf16[32,128,128]{2,1,0:T(8,128)(2,1)S(1)}, u32[]{:S(2)}, u32[]{:S(2)}) async-start(bf16[32,128,128]{2,1,0:T(8,128)(2,1)} %shard_map.103), calls=%async_computation.1 | async-start | bytes 2097152 | tf_op jit(solution)/shard_map/all_to_all | solution.py:387
  70.0 38.5 %copy-start = (bf16[32,128,128]{2,1,0:T(8,128)(2,1)}, bf16[32,128,128]{2,1,0:T(8,128)(2,1)S(1)}, u32[]{:S(2)}) copy-start(bf16[32,128,128]{2,1,0:T(8,128)(2,1)S(1)} %all-to-all-done.1.r_hbm) | copy-start | bytes 3145732
  70.0 41.5 %all-to-all-start.3 = ((bf16[32,128,128]{2,1,0:T(8,128)(2,1)}), bf16[32,128,128]{2,1,0:T(8,128)(2,1)S(1)}, u32[]{:S(2)}, u32[]{:S(2)}) async-start(bf16[32,128,128]{2,1,0:T(8,128)(2,1)} %get-tuple-element.17), calls=%async_computation.3 | async-start | bytes 2097152 | tf_op jit(solution)/shard_map/all_to_all | solution.py:387
  77.5 6.0 %collective-permute-start = (f32[8,4096]{1,0:T(8,128)}, f32[8,4096]{1,0:T(8,128)S(1)}, u32[]{:S(2)}, u32[]{:S(2)}) collective-permute-start(f32[8,4096]{1,0:T(8,128)} %get-tuple-element.20), channel_id=1, source_target_pairs={{0,32},{32,0},{64,96},{96,64},{128,160},{160,128},{192,224},{224,1... | collective-permute-start | bytes 393224 | tf_op jit(solution)/shard_map/ppermute | solution.py:394
  84.5 9.3 %collective-permute-start.1 = (f32[8,4096]{1,0:T(8,128)S(1)}, f32[8,4096]{1,0:T(8,128)S(1)}, u32[]{:S(2)}, u32[]{:S(2)}) collective-permute-start(f32[8,4096]{1,0:T(8,128)S(1)} %add.9), channel_id=1, source_target_pairs={{0,64},{32,96},{64,0},{96,32},{128,192},{160,224},{192,128},{224,1... | collective-permute-start | bytes 393224 | tf_op jit(solution)/shard_map/ppermute | solution.py:394
  93.8 12.3 %collective-permute-start.2 = (f32[8,4096]{1,0:T(8,128)S(1)}, f32[8,4096]{1,0:T(8,128)S(1)}, u32[]{:S(2)}, u32[]{:S(2)}) collective-permute-start(f32[8,4096]{1,0:T(8,128)S(1)} %add.10), channel_id=1, source_target_pairs={{0,128},{32,160},{64,192},{96,224},{128,0},{160,32},{192,64},{224,... | collective-permute-start | bytes 393224 | tf_op jit(solution)/shard_map/ppermute | solution.py:394
  111.5 1.0 copy-start.1

commit v4 on v3

--- a/solution.py
+++ b/solution.py
@@ -14,6 +14,9 @@
 MIB = 1024 * 1024
 SPAN = 4
 CHUNKS = 4
+
+SHORT = pl.CostEstimate(flops=1000, bytes_accessed=1000, transcendentals=0)
+LONG = pl.CostEstimate(flops=10**10, bytes_accessed=1000, transcendentals=0)
 
 NN = (((1,), (0,)), ((), ()))
 NT = (((1,), (1,)), ((), ()))
@@ -202,13 +205,13 @@
     ]
 
 
-def forward(order, x, strip):
+def conv(order, x, strip, backward):
     pieces = x.shape[0]
     groups, _, width = strip.shape
     rows = GROUP * pieces // 2
     spec = pl.BlockSpec((pieces, GROUP, BLOCK), lambda g, order: (0, g, 0))
     return pl.pallas_call(
-        functools.partial(conv_kernel, False),
+        functools.partial(conv_kernel, backward),
         grid_spec=pltpu.PrefetchScalarGridSpec(
             num_scalar_prefetch=1,
             grid=(groups,),
@@ -221,11 +224,7 @@
         ),
         out_shape=jax.ShapeDtypeStruct(x.shape, jnp.bfloat16),
         compiler_params=params(),
-        cost_estimate=pl.CostEstimate(
-            flops=groups * rows * rows * 16 * BLOCK,
-            bytes_accessed=4 * x.size + 2 * strip.size,
-            transcendentals=0,
-        ),
+        cost_estimate=LONG if backward else SHORT,
     )(order, x, strip)
 
 
@@ -269,49 +268,29 @@
         out_ref[...] = pltpu.roll(sums[...], width - last, 1)[:, : pieces * BLOCK]
 
 
-def back_kernel(
-    order_ref, x_ref, w_ref, strip_ref, out_ref, lag_ref, pairs, acc, xs, ws, squares, sums
-):
-    conv_kernel(True, order_ref, w_ref, strip_ref, out_ref, pairs, acc)
-    lag_kernel(order_ref, x_ref, w_ref, lag_ref, xs, ws, squares, sums)
-
-
-def back(order, x, w, strip):
+def lag_sums_of(order, x, w, groups):
     pieces = x.shape[0]
-    groups, _, width = strip.shape
     length = pieces * BLOCK
     rows = GROUP * pieces
-    spec = pl.BlockSpec((pieces, GROUP, BLOCK), lambda g, order: (0, g, 0))
-    return pl.pallas_call(
-        back_kernel,
+    whole = pl.BlockSpec(x.shape, lambda g, order: (0, 0, 0))
+    return pl.pallas_call(
+        lag_kernel,
         grid_spec=pltpu.PrefetchScalarGridSpec(
             num_scalar_prefetch=1,
             grid=(groups,),
-            in_specs=[
-                pl.BlockSpec(x.shape, lambda g, order: (0, 0, 0)),
-                pl.BlockSpec(x.shape, lambda g, order: (0, 0, 0)),
-                pl.BlockSpec((1, BLOCK, width), lambda g, order: (g, 0, 0)),
-            ],
-            out_specs=[spec, pl.BlockSpec((groups, length), lambda g, order: (0, 0))],
-            scratch_shapes=conv_scratch(rows // 2)
-            + [
+            in_specs=[whole, whole],
+            out_specs=pl.BlockSpec((groups, length), lambda g, order: (0, 0)),
+            scratch_shapes=[
                 pltpu.VMEM((rows, BLOCK), jnp.bfloat16),
                 pltpu.VMEM((rows + BLOCK, BLOCK), jnp.bfloat16),
                 pltpu.VMEM((BLOCK, length + BLOCK), jnp.float32),
                 pltpu.VMEM((groups, length + BLOCK), jnp.float32),
             ],
         ),
-        out_shape=[
-            jax.ShapeDtypeStruct(x.shape, jnp.bfloat16),
-            jax.ShapeDtypeStruct((groups, length), jnp.float32),
-        ],
+        out_shape=jax.ShapeDtypeStruct((groups, length), jnp.float32),
         compiler_params=params(),
-        cost_estimate=pl.CostEstimate(
-            flops=2 * groups * rows * BLOCK * length,
-            bytes_accessed=6 * x.size + 2 * strip.size,
-            transcendentals=0,
-        ),
-    )(order, x, w, strip)
+        cost_estimate=SHORT,
+    )(order, x, w)
 
 
 def post_kernel(
@@ -358,55 +337,60 @@
         scratch_shapes=[pltpu.VMEM(r.shape, r.dtype)]
         + [pltpu.VMEM(a.shape, a.dtype)] * 4
         + [pltpu.SemaphoreType.DMA((CHUNKS,))] * 5,
-        compiler_params=params(),
+        compiler_params=params(24),
         cost_estimate=pl.CostEstimate(
             flops=2 * a.size, bytes_accessed=10 * a.size, transcendentals=0
         ),
     )(r, a, b)
 
 
-def taps_kernel(sequences, taps_ref, lag_ref, out_ref):
+def taps_kernel(sequences, taps_ref, mine_ref, others_ref, out_ref):
     taps = taps_ref[...]
     length = taps.shape[1]
     root = jnp.sqrt(jnp.mean(taps * taps, axis=1, keepdims=True) + EPSILON)
     scale = 1.0 / (math.sqrt(length) * root)
-    mean = lag_ref[...] / sequences
+    mean = (mine_ref[...] + others_ref[...]) / sequences
     projection = jnp.sum(mean * taps, axis=1, keepdims=True)
     out_ref[...] = scale * mean - taps * (scale * scale * scale) * projection
 
 
-def taps_grad_of(taps, lag_total, sequences):
+def taps_grad_of(taps, mine, others, sequences):
     return pl.pallas_call(
         functools.partial(taps_kernel, sequences),
         out_shape=jax.ShapeDtypeStruct(taps.shape, jnp.float32),
         compiler_params=params(),
-    )(taps, lag_total)
+    )(taps, mine, others)
 
 
 def exchange(tiles):
     return lax.all_to_all(tiles, "ctx", split_axis=0, concat_axis=0, tiled=True)
 
 
-def sum_over_dp(x):
-    size = lax.axis_size("dp")
-    step = 1
-    while step < size:
-        x = x + lax.ppermute(x, "dp", [(i, i ^ step) for i in range(size)])
-        step *= 2
-    return x
+def from_partner(x, step):
+    return lax.ppermute(x, "dp", [(i, i ^ step) for i in range(lax.axis_size("dp"))])
 
 
 def shards(output_gate_input, key_input, value_input, upstream, filter_taps, order):
+    groups = filter_taps.shape[0]
+    sequences = lax.axis_size("dp")
     product_tiles = pre(key_input, value_input)
     product = exchange(product_tiles)
     weighted_tiles, strip = pre_and_strips(upstream, output_gate_input, filter_taps)
     weighted = exchange(weighted_tiles)
-    mixing = exchange(forward(order, product, strip))
-    returned_tiles, lag_sums = back(order, product, weighted, strip)
+    mixing_tiles = conv(order, product, strip, False)
+    mixing = exchange(mixing_tiles)
+    product, _ = lax.optimization_barrier((product, mixing_tiles))
+    lag_sums = lag_sums_of(order, product, weighted, groups)
+    later, lag_sums = lax.optimization_barrier((weighted, lag_sums))
+    near = [from_partner(lag_sums, step) for step in range(1, sequences // 2)]
+    returned_tiles = conv(order, later, strip, True)
+    half = sum(near, lag_sums)
+    returned_tiles, half = lax.optimization_barrier((returned_tiles, half))
     returned = exchange(returned_tiles)
-    lag_total = sum_over_dp(lag_sums)
+    far = from_partner(half, sequences // 2)
     mixed_out, gate_grad = post(mixing, output_gate_input, upstream)
-    taps_grad = taps_grad_of(filter_taps, lag_total, lax.axis_size("dp"))
+    half, mixed_out = lax.optimization_barrier((half, mixed_out))
+    taps_grad = taps_grad_of(filter_taps, half, far, sequences)
     key_grad, value_grad = post(returned, value_input, key_input)
     return mixed_out, gate_grad, key_grad, value_grad, taps_grad
 

time: 117 us -> 113 us (0.966)
  the two profiles are of different devices: /device:TPU:2 before, /device:TPU:1 now
where the time goes in v4:
time: 113 us; the launch traced here: 111 us
  Pallas kernels  56.8 us (50%)
  starting transfers between devices  36.2 us (32%)
  waiting for transfers between devices  15.7 us (14%)
  local copies, waits for them, and re-layouts  1.9 us (2%)
    all_to_all x4, starting transfers between devices, exchange(): return lax.all_to_all(tiles, 'ctx', split_axis=0, concat_axis=0, tiled=True)  25.3 us
    pallas_call x2, Pallas kernels, conv(): pl.pallas_call(functools.partial(conv_kernel, backward), grid_spec=pltpu....  22.9 us
    all_to_all x4, waiting for transfers between devices, exchange(): return lax.all_to_all(tiles, 'ctx', split_axis=0, concat_axis=0, tiled=True)  15.6 us
    pallas_call x1, Pallas kernels, pre_and_strips(): pl.pallas_call(functools.partial(pre_strip_kernel, tiles), grid=(groups,)...  12.4 us
    pallas_call x1, Pallas kernels, lag_sums_of(): pl.pallas_call(lag_kernel, grid_spec=pltpu.PrefetchScalarGridSpec(num_sca...  11.9 us
    ppermute x4, starting transfers between devices, from_partner(): lax.ppermute(x, 'dp', [(i, i ^ step) for i in range(lax.axis_size('dp'))])  10.9 us
    pallas_call x2, Pallas kernels, post(): pl.pallas_call(post_kernel, in_specs=[anywhere] * 3, out_specs=[anywhere]...  5.25 us
    pallas_call x1, Pallas kernels, pre(): pl.pallas_call(pre_kernel, in_specs=[anywhere, anywhere], out_specs=anywh...  2.44 us
  transfers between devices with their start and end apart: 8, of which 3 were waited for; matrix products, arithmetic and copies ran while one was open for 0% of the time, Pallas kernels for 46%

profile of v4, /device:TPU:1, one launch (start us, length us, event | category | flops | bytes accessed | tf_op | source)
XLA Modules:
  0.0 111.4 jit_solution(8355589563734547977)
XLA Ops:
  0.6 2.4 %shard_map.102 = bf16[32,128,128]{2,1,0:T(8,128)(2,1)} custom-call(bf16[1,128,4096]{2,1,0:T(8,128)(2,1)} %b_hbm.5, bf16[1,128,4096]{2,1,0:T(8,128)(2,1)} %a_hbm.5), custom_call_target="tpu_custom_call" | custom-call | flops 524288 | bytes 3145728 | tf_op jit(solution)/shard_map/pallas_call | solution.py:82
  3.1 8.6 %all-to-all-start.1 = ((bf16[32,128,128]{2,1,0:T(8,128)(2,1)}), bf16[32,128,128]{2,1,0:T(8,128)(2,1)S(1)}, u32[]{:S(2)}, u32[]{:S(2)}) async-start(bf16[32,128,128]{2,1,0:T(8,128)(2,1)} %shard_map.102), calls=%async_computation.1 | async-start | bytes 2097152 | tf_op jit(solution)/shard_map/all_to_all | solution.py:366
  11.7 12.4 %shard_map.101 = (bf16[32,128,128]{2,1,0:T(8,128)(2,1)}, bf16[8,128,4224]{2,1,0:T(8,128)(2,1)}) custom-call(bf16[1,128,4096]{2,1,0:T(8,128)(2,1)} %b_hbm.4, bf16[1,128,4096]{2,1,0:T(8,128)(2,1)} %a_hbm.4, f32[8,4096]{1,0:T(8,128)} %taps_ref.3), custom_call_target="tpu_custom_call" | custom-call | flops 17301504 | bytes 11796480 | tf_op jit(solution)/shard_map/pallas_call | solution.py:133
  24.1 4.8 %all-to-all-done.1.x_ref = bf16[32,128,128]{2,1,0:T(8,128)(2,1)S(1)} async-done(((bf16[32,128,128]{2,1,0:T(8,128)(2,1)}), bf16[32,128,128]{2,1,0:T(8,128)(2,1)S(1)}, u32[]{:S(2)}, u32[]{:S(2)}) %all-to-all-start.1) | async-done | bytes 1048608 | tf_op jit(solution)/shard_map/all_to_all | solution.py:366
  28.9 4.0 %all-to-all-start = ((bf16[32,128,128]{2,1,0:T(8,128)(2,1)}), bf16[32,128,128]{2,1,0:T(8,128)(2,1)S(1)}, u32[]{:S(2)}, u32[]{:S(2)}) async-start(bf16[32,128,128]{2,1,0:T(8,128)(2,1)} %get-tuple-element.18), calls=%async_computation | async-start | bytes 2097152 | tf_op jit(solution)/shard_map/all_to_all | solution.py:366
  32.9 0.0 copy-done.4
  32.9 11.2 %shard_map.103 = bf16[32,128,128]{2,1,0:T(8,128)(2,1)} custom-call(s32[32]{0:T(128)} %order_ref.5, bf16[32,128,128]{2,1,0:T(8,128)(2,1)} %copy-done.4, bf16[8,128,4224]{2,1,0:T(8,128)(2,1)} %get-tuple-element.19.strip_ref), custom_call_target="tpu_custom_call" | custom-call | flops 1000 | bytes 1000 | tf_op jit(solution)/shard_map/pallas_call | solution.py:213
  44.0 6.1 %all-to-all-done.w_ref.x_ref = bf16[32,128,128]{2,1,0:T(8,128)(2,1)S(1)} async-done(((bf16[32,128,128]{2,1,0:T(8,128)(2,1)}), bf16[32,128,128]{2,1,0:T(8,128)(2,1)S(1)}, u32[]{:S(2)}, u32[]{:S(2)}) %all-to-all-start) | async-done | bytes 1048608 | tf_op jit(solution)/shard_map/all_to_all | solution.py:366
  50.1 4.6 %all-to-all-start.2 = ((bf16[32,128,128]{2,1,0:T(8,128)(2,1)}), bf16[32,128,128]{2,1,0:T(8,128)(2,1)}, u32[]{:S(2)}, u32[]{:S(2)}) async-start(bf16[32,128,128]{2,1,0:T(8,128)(2,1)} %shard_map.103), calls=%async_computation.2 | async-start | bytes 2097152 | tf_op jit(solution)/shard_map/all_to_all | solution.py:366
  54.8 0.0 copy-done.5
  54.8 11.9 %shard_map.104 = f32[8,4096]{1,0:T(8,128)} custom-call(s32[32]{0:T(128)} %order_ref.5, bf16[32,128,128]{2,1,0:T(8,128)(2,1)} %copy-done.4, bf16[32,128,128]{2,1,0:T(8,128)(2,1)} %copy-done.5), custom_call_target="tpu_custom_call" | custom-call | flops 1000 | bytes 1000 | tf_op jit(solution)/shard_map/pallas_call | solution.py:276
  66.7 4.4 %collective-permute-start.2 = (f32[8,4096]{1,0:T(8,128)}, f32[8,4096]{1,0:T(8,128)S(1)}, u32[]{:S(2)}, u32[]{:S(2)}) collective-permute-start(f32[8,4096]{1,0:T(8,128)} %shard_map.104), channel_id=1, source_target_pairs={{0,96},{32,64},{64,32},{96,0},{128,224},{160,192},{192,160},{224,1... | collective-permute-start | bytes 393224 | tf_op jit(solution)/shard_map/ppermute | solution.py:370
  71.2 0.0 collective-permute-start.1
  71.2 0.4 collective-permute-start
  71.6 11.7 %shard_map.105 = bf16[32,128,128]{2,1,0:T(8,128)(2,1)} custom-call(s32[32]{0:T(128)} %order_ref.5, bf16[32,128,128]{2,1,0:T(8,128)(2,1)} %copy-done.5, bf16[8,128,4224]{2,1,0:T(8,128)(2,1)} %get-tuple-element.19.strip_ref), custom_call_target="tpu_custom_call" | custom-call | flops 10000000000 | bytes 1000 | tf_op jit(solution)/shard_map/pallas_call | solution.py:213
  83.3 0.0 collective-permute-done.2
  83.3 0.0 collective-permute-done.1
  83.3 0.0 collective-permute-done
  83.3 0.0 copy-done.6
  83.4 0.0 copy-start.7
  83.4 0.0 all-to-all-done.2.r_hbm
  83.4 8.1 %all-to-all-start.3 = ((bf16[32,128,128]{2,1,0:T(8,128)(2,1)}), bf16[32,128,128]{2,1,0:T(8,128)(2,1)}, u32[]{:S(2)}, u32[]{:S(2)}) async-start(bf16[32,128,128]{2,1,0:T(8,128)(2,1)} %shard_map.105), calls=%async_computation.3 | async-start | bytes 2097152 | tf_op jit(solution)/shard_map/all_to_all | solution.py:366
  91.5 6.1 %collective-permute-start.3 = (f32[8,4096]{1,0:T(8,128)S(1)}, f32[8,4096]{1,0:T(8,128)S(1)}, u32[]{:S(2)}, u32[]{:S(2)}) collective-permute-start(f32[8,4096]{1,0:T(8,128)S(1)} %add_add_fusion.mine_ref), channel_id=1, source_target_pairs={{0,128},{32,160},{64,192},{96,224},{128,0},{160,32},{192,64},{224,... | collective-permute-start | bytes 393224 | tf_op jit(solution)/shard_map/ppermute | solution.py:370
  97.6 0.0 copy-done.2
  97.6 1.2 %copy-done.3 = bf16[1,128,4096]{2,1,0:T(8,128)(2,1)S(1)} copy-done((bf16[1,128,4096]{2,1,0:T(8,128)(2,1)S(1)}, bf16[1,128,4096]{2,1,0:T(8,128)(2,1)}, u32[]{:S(2)}) %copy-start.3) | copy-done | bytes 1048600
  98.8 2.6 %shard_map.106 = (bf16[1,128,4096]{2,1,0:T(8,128)(2,1)}, bf16[1,128,4096]{2,1,0:T(8,128)(2,1)}) custom-call(bf16[32,128,128]{2,1,0:T(8,128)(2,1)} %all-to-all-done.2.r_hbm, bf16[1,128,4096]{2,1,0:T(8,128)(2,1)S(1)} %copy-done.3, bf16[1,128,4096]{2,1,0:T(8,128)(2,1)S(1)} %copy-done.2), custom_call_target="tpu_custom_call" | custom-call | flops 1048576 | bytes 5242880 | tf_op jit(solution)/shard_map/pallas_call | solution.py:332
  101.5 0.0 collective-permute-done.3.others_ref
  101.5 0.0 copy-done.7
  101.5 0.6 copy-done.8
  102.1 1.8 %shard_map.108 = f32[8,4096]{1,0:T(8,128)} custom-call(f32[8,4096]{1,0:T(8,128)} %taps_ref.3, f32[8,4096]{1,0:T(8,128)} %copy-done.7, f32[8,4096]{1,0:T(8,128)} %copy-done.8), custom_call_target="tpu_custom_call" | custom-call | tf_op jit(solution)/shard_map/pallas_call | solution.py:358
  104.0 4.8 %all-to-all-done.3.r_hbm = bf16[32,128,128]{2,1,0:T(8,128)(2,1)} async-done(((bf16[32,128,128]{2,1,0:T(8,128)(2,1)}), bf16[32,128,128]{2,1,0:T(8,128)(2,1)}, u32[]{:S(2)}, u32[]{:S(2)}) %all-to-all-start.3) | async-done | bytes 1048608 | tf_op jit(solution)/shard_map/all_to_all | solution.py:366
  108.7 2.6 %shard_map.107 = (bf16[1,128,4096]{2,1,0:T(8,128)(2,1)}, bf16[1,128,4096]{2,1,0:T(8,128)(2,1)}) custom-call(bf16[32,128,128]{2,1,0:T(8,128)(2,1)} %all-to-all-done.3.r_hbm, bf16[1,128,4096]{2,1,0:T(8,128)(2,1)S(1)} %copy-done.1, bf16[1,128,4096]{2,1,0:T(8,128)(2,1)S(1)} %copy-done), custom_call_target="tpu_custom_call" | custom-call | flops 1048576 | bytes 5242880 | tf_op jit(solution)/shard_map/pallas_call | solution.py:332
  (11 shorter events, 0.0 us)
Async XLA Ops:
  3.1 25.8 %all-to-all-start.1 = ((bf16[32,128,128]{2,1,0:T(8,128)(2,1)}), bf16[32,128,128]{2,1,0:T(8,128)(2,1)S(1)}, u32[]{:S(2)}, u32[]{:S(2)}) async-start(bf16[32,128,128]{2,1,0:T(8,128)(2,1)} %shard_map.102), calls=%async_computation.1 | async-start | bytes 2097152 | tf_op jit(solution)/shard_map/all_to_all | solution.py:366
  28.9 4.0 %copy-start.4 = (bf16[32,128,128]{2,1,0:T(8,128)(2,1)}, bf16[32,128,128]{2,1,0:T(8,128)(2,1)S(1)}, u32[]{:S(2)}) copy-start(bf16[32,128,128]{2,1,0:T(8,128)(2,1)S(1)} %all-to-all-done.1.x_ref) | copy-start | bytes 3145732
  28.9 21.3 %all-to-all-start = ((bf16[32,128,128]{2,1,0:T(8,128)(2,1)}), bf16[32,128,128]{2,1,0:T(8,128)(2,1)S(1)}, u32[]{:S(2)}, u32[]{:S(2)}) async-start(bf16[32,128,128]{2,1,0:T(8,128)(2,1)} %get-tuple-element.18), calls=%async_computation | async-start | bytes 2097152 | tf_op jit(solution)/shard_map/all_to_all | solution.py:366
  50.1 4.6 %copy-start.5 = (bf16[32,128,128]{2,1,0:T(8,128)(2,1)}, bf16[32,128,128]{2,1,0:T(8,128)(2,1)S(1)}, u32[]{:S(2)}) copy-start(bf16[32,128,128]{2,1,0:T(8,128)(2,1)S(1)} %all-to-all-done.w_ref.x_ref) | copy-start | bytes 3145732
  50.1 33.2 %all-to-all-start.2 = ((bf16[32,128,128]{2,1,0:T(8,128)(2,1)}), bf16[32,128,128]{2,1,0:T(8,128)(2,1)}, u32[]{:S(2)}, u32[]{:S(2)}) async-start(bf16[32,128,128]{2,1,0:T(8,128)(2,1)} %shard_map.103), calls=%async_computation.2 | async-start | bytes 2097152 | tf_op jit(solution)/shard_map/all_to_all | solution.py:366
  66.7 16.6 %copy-start.6 = (f32[8,4096]{1,0:T(8,128)S(1)}, f32[8,4096]{1,0:T(8,128)}, u32[]{:S(2)}) copy-start(f32[8,4096]{1,0:T(8,128)} %shard_map.104) | copy-start | bytes 393220
  66.7 30.9 %copy-start.2 = (bf16[1,128,4096]{2,1,0:T(8,128)(2,1)S(1)}, bf16[1,128,4096]{2,1,0:T(8,128)(2,1)}, u32[]{:S(2)}) copy-start(bf16[1,128,4096]{2,1,0:T(8,128)(2,1)} %b_hbm.4) | copy-start | bytes 3145732
  66.7 42.0 %copy-start = (bf16[1,128,4096]{2,1,0:T(8,128)(2,1)S(1)}, bf16[1,128,4096]{2,1,0:T(8,128)(2,1)}, u32[]{:S(2)}) copy-start(bf16[1,128,4096]{2,1,0:T(8,128)(2,1)} %b_hbm.5) | copy-start | bytes 3145732
  66.7 42.0 %copy-start.1 = (bf16[1,128,4096]{2,1,0:T(8,128)(2,1)S(1)}, bf16[1,128,4096]{2,1,0:T(8,128)(2,1)}, u32[]{:S(2)}) copy-start(bf16[1,128,4096]{2,1,0:T(8,128)(2,1)} %a_hbm.5) | copy-start | bytes 3145732
  66.7 16.6 %collective-permute-start.2 = (f32[8,4096]{1,0:T(8,128)}, f32[8,4096]{1,0:T(8,128)S(1)}, u32[]{:S(2)}, u32[]{:S(2)}) collective-permute-start(f32[8,4096]{1,0:T(8,128)} %shard_map.104), channel_id=1, source_target_pairs={{0,96},{32,64},{64,32},{96,0},{128,224},{160,192},{192,160},{224,1... | collective-permute-start | bytes 393224 | tf_op jit(solution)/shard_map/ppermute | solution.py:370
  71.2 12.1 %collective-permute-start.1 = (f32[8,4096]{1,0:T(8,128)}, f32[8,4096]{1,0:T(8,128)S(1)}, u32[]{:S(2)}, u32[]{:S(2)}) collective-permute-start(f32[8,4096]{1,0:T(8,128)} %shard_map.104), channel_id=1, source_target_pairs={{0,64},{32,96},{64,0},{96,32},{128,192},{160,224},{192,128},{224,1... | collective-permute-start | bytes 393224 | tf_op jit(solution)/shard_map/ppermute | solution.py:370
  71.2 12.1 %collective-permute-start = (f32[8,4096]{1,0:T(8,128)}, f32[8,4096]{1,0:T(8,128)S(1)}, u32[]{:S(2)}, u32[]{:S(2)}) collective-permute-start(f32[8,4096]{1,0:T(8,128)} %shard_map.104), channel_id=1, source_target_pairs={{0,32},{32,0},{64,96},{96,64},{128,160},{160,128},{192,224},{224,1... | collective-permute-start | bytes 393224 | tf_op jit(solution)/shard_map/ppermute | solution.py:370
  83.4 18.1 %copy-start.7 = (f32[8,4096]{1,0:T(8,128)}, f32[8,4096]{1,0:T(8,128)S(1)}, u32[]{:S(2)}) copy-start(f32[8,4096]{1,0:T(8,128)S(1)} %add_add_fusion.mine_ref) | copy-start | bytes 393220
  83.4 25.4 %all-to-all-start.3 = ((bf16[32,128,128]{2,1,0:T(8,128)(2,1)}), bf16[32,128,128]{2,1,0:T(8,128)(2,1)}, u32[]{:S(2)}, u32[]{:S(2)}) async-start(bf16[32,128,128]{2,1,0:T(8,128)(2,1)} %shard_map.105), calls=%async_computation.3 | async-start | bytes 2097152 | tf_op jit(solution)/shard_map/all_to_all | solution.py:366
  91.5 10.0 %collective-permute-start.3 = (f32[8,4096]{1,0:T(8,128)S(1)}, f32[8,4096]{1,0:T(8,128)S(1)}, u32[]{:S(2)}, u32[]{:S(2)}) collective-permute-start(f32[8,4096]{1,0:T(8,128)S(1)} %add_add_fusion.mine_ref), channel_id=1, source_target_pairs={{0,128},{32,160},{64,192},{96,224},{128,0},{160,32},{192,64},{224,... | collective-permute-start | bytes 393224 | tf_op jit(solution)/shard_map/ppermute | solution.py:370
  97.6 1.2 %copy-start.3 = (bf16[1,128,4096]{2,1,0:T(8,128)(2,1)S(1)}, bf16[1,128,4096]{2,1,0:T(8,128)(2,1)}, u32[]{:S(2)}) copy-start(bf16[1,128,4096]{2,1,0:T(8,128)(2,1)} %a_hbm.4) | copy-start | bytes 3145732
  101.5 0.7 copy-start.8

commit v5 on v4

--- a/solution.py
+++ b/solution.py
@@ -13,6 +13,7 @@
 GROUP = 16
 MIB = 1024 * 1024
 SPAN = 4
+AT_ONCE = 4
 CHUNKS = 4
 
 SHORT = pl.CostEstimate(flops=1000, bytes_accessed=1000, transcendentals=0)
@@ -151,146 +152,252 @@
     )(a, b, taps)
 
 
-def rows_of(block):
-    return pl.ds(pl.multiple_of(GROUP * block, GROUP), GROUP)
-
-
-def conv_kernel(backward, order_ref, x_ref, strip_ref, out_ref, xs, acc):
-    pieces = x_ref.shape[0]
-    rows = acc.shape[1]
-    spare = GROUP * (SPAN - 1)
-    first = 0 if backward else SPAN - 1
-    if backward:
-        xs[:, rows : rows + spare, :] = jnp.zeros((2, spare, BLOCK), jnp.bfloat16)
-    else:
-        xs[:, :spare, :] = jnp.zeros((2, spare, BLOCK), jnp.bfloat16)
-    for d in range(pieces):
-        b = order_ref[d]
-        xs[b % 2, rows_of(b // 2 + first), :] = x_ref[d, rows_of(pl.program_id(0)), :]
+def in_order(order_ref, source, target, sems):
+    return [
+        pltpu.make_async_copy(source.at[d], target.at[order_ref[d]], sems.at[d])
+        for d in range(source.shape[0])
+    ]
+
+
+def start(made):
+    for copy in made:
+        copy.start()
+
+
+def wait(made):
+    for copy in made:
+        copy.wait()
+
+
+def rows_of(group):
+    first = GROUP * group
+    return pl.ds(first if isinstance(first, int) else pl.multiple_of(first, GROUP), GROUP)
+
+
+def forward_kernel(
+    order_ref, x_hbm, strip_hbm, out_hbm, x, strip, out, acc, x_sem, s_sem, out_sem
+):
+    groups = strip.shape[0]
+    arrive = in_order(order_ref, x_hbm, x, x_sem)
+    start(arrive)
+    strips = [
+        pltpu.make_async_copy(strip_hbm.at[g], strip.at[g], s_sem.at[g]) for g in range(groups)
+    ]
+    start(strips)
+    wait(arrive)
+
+    def ready(g):
+        pltpu.make_async_copy(strip_hbm.at[g], strip.at[g], s_sem.at[g]).wait()
+
+    filter_groups(False, x, strip, out, acc, ready)
+    send(order_ref, out, out_hbm, out_sem)
+
+
+def back_kernel(order_ref, x, strip, out_hbm, out, acc, out_sem):
+    filter_groups(True, x, strip, out, acc, lambda g: None)
+    send(order_ref, out, out_hbm, out_sem)
+
+
+def send(order_ref, out, out_hbm, out_sem):
+    leave = [
+        pltpu.make_async_copy(out.at[order_ref[d]], out_hbm.at[d], out_sem.at[d])
+        for d in range(out.shape[0])
+    ]
+    start(leave)
+    wait(leave)
+
+
+def filter_groups(backward, x, strip, out, acc, ready):
+    pieces = x.shape[0]
+    groups = strip.shape[0]
+    pairs = pieces // 2
     wide = 2 * BLOCK
-    for lag in range(0, rows // GROUP, SPAN):
-        depth = rows - GROUP * lag
-        at = BLOCK + wide * lag
-        lefts, weights = [], []
-        for k in range(SPAN):
-            start = GROUP * (lag + k) if backward else GROUP * (SPAN - 1 - k)
-            lefts += [xs[0, start : start + depth, :], xs[1, start : start + depth, :]]
-            weights += [
-                strip_ref[0, :, at + wide * k : at + wide * (k + 1)],
-                strip_ref[0, :, at + wide * k - BLOCK : at + wide * k + BLOCK],
-            ]
-        left = jnp.concatenate(lefts, axis=1)
-        if backward:
-            weights = [
-                strip_ref[0, :, at : at + wide * SPAN],
-                strip_ref[0, :, at - BLOCK : at - BLOCK + wide * SPAN],
-            ]
-        part = dot(left, jnp.concatenate(weights, axis=0), NT if backward else NN)
-        if lag == 0:
-            acc[0] = part[:, :BLOCK]
-            acc[1] = part[:, BLOCK:]
-        else:
-            target = slice(0, depth) if backward else slice(rows - depth, rows)
-            acc[0, target, :] += part[:, :BLOCK]
-            acc[1, target, :] += part[:, BLOCK:]
-    for d in range(pieces):
-        b = order_ref[d]
-        out_ref[d] = acc[b % 2, rows_of(b // 2), :].astype(jnp.bfloat16)
-
-
-def conv_scratch(rows):
-    return [
-        pltpu.VMEM((2, rows + GROUP * (SPAN - 1), BLOCK), jnp.bfloat16),
-        pltpu.VMEM((2, rows, BLOCK), jnp.float32),
-    ]
-
-
-def conv(order, x, strip, backward):
+    nothing = jnp.zeros((GROUP, wide), jnp.bfloat16)
+    @pl.loop(0, groups)
+    def _(g):
+        ready(g)
+        blocks = [
+            jnp.concatenate([x[2 * i, rows_of(g), :], x[2 * i + 1, rows_of(g), :]], axis=1)
+            for i in range(pairs)
+        ]
+        for lag in range(0, pairs, SPAN):
+            at = BLOCK + wide * lag
+            lefts, weights = [], []
+            for k in range(min(SPAN, pairs - lag)):
+                if backward:
+                    froms = range(lag + k, pairs + k)
+                else:
+                    froms = range(-k, pairs - lag - k)
+                lefts.append(
+                    jnp.concatenate(
+                        [blocks[i] if 0 <= i < pairs else nothing for i in froms], axis=0
+                    )
+                )
+                weights += [
+                    strip[g, :, at + wide * k : at + wide * (k + 1)],
+                    strip[g, :, at + wide * k - BLOCK : at + wide * k + BLOCK],
+                ]
+            if backward:
+                ends = at + wide * min(SPAN, pairs - lag)
+                weights = [strip[g, :, at:ends], strip[g, :, at - BLOCK : ends - BLOCK]]
+            part = dot(
+                jnp.concatenate(lefts, axis=1),
+                jnp.concatenate(weights, axis=0),
+                NT if backward else NN,
+            )
+            depth = GROUP * (pairs - lag)
+            if lag == 0:
+                acc[0] = part
+            elif backward:
+                acc[0, :depth, :] += part
+            else:
+                acc[0, GROUP * lag :, :] += part
+        for i in range(pairs):
+            both = acc[0, rows_of(i), :].astype(jnp.bfloat16)
+            out[2 * i, rows_of(g), :] = both[:, :BLOCK]
+            out[2 * i + 1, rows_of(g), :] = both[:, BLOCK:]
+
+
+def forward(order, x, strip):
     pieces = x.shape[0]
-    groups, _, width = strip.shape
+    groups = strip.shape[0]
     rows = GROUP * pieces // 2
-    spec = pl.BlockSpec((pieces, GROUP, BLOCK), lambda g, order: (0, g, 0))
-    return pl.pallas_call(
-        functools.partial(conv_kernel, backward),
-        grid_spec=pltpu.PrefetchScalarGridSpec(
-            num_scalar_prefetch=1,
-            grid=(groups,),
-            in_specs=[
-                pl.BlockSpec(x.shape, lambda g, order: (0, 0, 0)),
-                pl.BlockSpec((1, BLOCK, width), lambda g, order: (g, 0, 0)),
-            ],
-            out_specs=spec,
-            scratch_shapes=conv_scratch(rows),
-        ),
+    anywhere = pl.BlockSpec(memory_space=pl.ANY)
+    return pl.pallas_call(
+        forward_kernel,
+        in_specs=[pl.BlockSpec(memory_space=pltpu.SMEM), anywhere, anywhere],
+        out_specs=anywhere,
+        scratch_shapes=[
+            pltpu.VMEM(x.shape, x.dtype),
+            pltpu.VMEM(strip.shape, strip.dtype),
+            pltpu.VMEM(x.shape, x.dtype),
+            pltpu.VMEM((2, rows, 2 * BLOCK), jnp.float32),
+            pltpu.SemaphoreType.DMA((pieces,)),
+            pltpu.SemaphoreType.DMA((groups,)),
+            pltpu.SemaphoreType.DMA((pieces,)),
+        ],
         out_shape=jax.ShapeDtypeStruct(x.shape, jnp.bfloat16),
         compiler_params=params(),
-        cost_estimate=LONG if backward else SHORT,
+        cost_estimate=SHORT,
     )(order, x, strip)
 
 
-def lag_kernel(order_ref, x_ref, w_ref, out_ref, xs, ws, squares, sums):
-    pieces = x_ref.shape[0]
+def back(order, x, strip):
+    pieces = x.shape[0]
+    vmem = pl.BlockSpec(memory_space=pltpu.VMEM)
+    return pl.pallas_call(
+        back_kernel,
+        in_specs=[pl.BlockSpec(memory_space=pltpu.SMEM), vmem, vmem],
+        out_specs=pl.BlockSpec(memory_space=pl.ANY),
+        scratch_shapes=[
+            pltpu.VMEM(x.shape, x.dtype),
+            pltpu.VMEM((2, GROUP * pieces // 2, 2 * BLOCK), jnp.float32),
+            pltpu.SemaphoreType.DMA((pieces,)),
+        ],
+        out_shape=pltpu.HBM(x.shape, jnp.bfloat16),
+        compiler_params=params(50),
+        cost_estimate=LONG,
+    )(
+        order,
+        pltpu.with_memory_space_constraint(x, pltpu.VMEM),
+        pltpu.with_memory_space_constraint(strip, pltpu.VMEM),
+    )
+
+
+def lag_kernel(
+    order_ref, x_hbm, w_hbm, strip_hbm, out_ref, w, strip, x, squares, sums, x_sem, w_sem, s_sem
+):
+    pieces = x.shape[0]
+    groups = out_ref.shape[0]
     total = GROUP * pieces
     last = BLOCK - 1
-    g = pl.program_id(0)
-    for d in range(pieces):
-        rows = rows_of(order_ref[d])
-        xs[rows, :] = x_ref[d, rows_of(g), :]
-        ws[rows, :] = w_ref[d, rows_of(g), :]
-    ws[total:, :] = jnp.zeros((BLOCK, BLOCK), jnp.bfloat16)
+    arrive = in_order(order_ref, x_hbm, x, x_sem) + in_order(order_ref, w_hbm, w, w_sem)
+    start(arrive)
+    kept = pltpu.make_async_copy(strip_hbm, strip, s_sem)
+    kept.start()
     row = lax.broadcasted_iota(jnp.int32, (BLOCK, BLOCK), 0)
     col = lax.broadcasted_iota(jnp.int32, (BLOCK, BLOCK), 1)
     mirror = jnp.where(row + col == last, 1.0, 0.0).astype(jnp.bfloat16)
-    x_turned = dot(mirror, xs[...], NT).astype(jnp.bfloat16)
-    for lag in range(0, pieces, 2):
-        depth = total - GROUP * lag // BLOCK * BLOCK
-        start = GROUP * lag
-        right = jnp.concatenate(
-            [ws[start : start + depth, :], ws[start + GROUP : start + GROUP + depth, :]],
-            axis=1,
-        )
-        squares[:, lag * BLOCK : (lag + 2) * BLOCK] = dot(x_turned[:, :depth], right, NN)
-    squares[:, pieces * BLOCK :] = jnp.zeros((BLOCK, BLOCK), jnp.float32)
-    step = 8
-    for t in range(0, pieces, step):
-        cols = slice(t * BLOCK, (t + step + 1) * BLOCK)
-        added = None
-        for q in range(BLOCK // 8):
-            moved = pltpu.roll(squares[8 * q : 8 * q + 8, cols], 8 * q, 1, stride=1, stride_axis=0)
-            added = moved if added is None else added + moved
-        added = jnp.sum(added, axis=0, keepdims=True)
-        skip = BLOCK if t else 0
-        sums[pl.ds(g, 1), t * BLOCK + skip : (t + step + 1) * BLOCK] = added[:, skip:]
-
-    @pl.when(g == pl.num_programs(0) - 1)
-    def _():
-        width = sums.shape[1]
-        out_ref[...] = pltpu.roll(sums[...], width - last, 1)[:, : pieces * BLOCK]
-
-
-def lag_sums_of(order, x, w, groups):
+    nothing = jnp.zeros((GROUP, BLOCK), jnp.bfloat16)
+    for i in range(2):
+        squares[i, :, pieces * BLOCK :] = jnp.zeros((BLOCK, BLOCK), jnp.float32)
+    wait(arrive)
+    def one(g, here):
+        xs = jnp.concatenate([x[j, rows_of(g), :] for j in range(pieces)], axis=0)
+        x_turned = dot(mirror, xs, NT).astype(jnp.bfloat16)
+        blocks = [w[j, rows_of(g), :] for j in range(pieces)]
+        for lag in range(0, pieces, 2):
+            depth = total - GROUP * lag // BLOCK * BLOCK
+            right = jnp.concatenate(
+                [
+                    jnp.concatenate(
+                        [
+                            blocks[j] if j < pieces else nothing
+                            for j in range(first, first + depth // GROUP)
+                        ],
+                        axis=0,
+                    )
+                    for first in (lag, lag + 1)
+                ],
+                axis=1,
+            )
+            squares[here, :, lag * BLOCK : (lag + 2) * BLOCK] = dot(
+                x_turned[:, :depth], right, NN
+            )
+        step = 8
+        for t in range(0, pieces, step):
+            cols = slice(t * BLOCK, (t + step + 1) * BLOCK)
+            added = None
+            for q in range(BLOCK // 8):
+                moved = pltpu.roll(
+                    squares[here, 8 * q : 8 * q + 8, cols], 8 * q, 1, stride=1, stride_axis=0
+                )
+                added = moved if added is None else added + moved
+            added = jnp.sum(added, axis=0, keepdims=True)
+            skip = BLOCK if t else 0
+            sums[pl.ds(g, 1), t * BLOCK + skip : (t + step + 1) * BLOCK] = added[:, skip:]
+
+    @pl.loop(0, groups // AT_ONCE)
+    def _(i):
+        for k in range(AT_ONCE):
+            one(i * AT_ONCE + k, k % 2)
+
+    width = sums.shape[1]
+    out_ref[...] = pltpu.roll(sums[...], width - last, 1)[:, : pieces * BLOCK]
+    kept.wait()
+
+
+def lag_sums_of(order, x, w, strip):
     pieces = x.shape[0]
+    groups = strip.shape[0]
     length = pieces * BLOCK
-    rows = GROUP * pieces
-    whole = pl.BlockSpec(x.shape, lambda g, order: (0, 0, 0))
+    anywhere = pl.BlockSpec(memory_space=pl.ANY)
+    vmem = pl.BlockSpec(memory_space=pltpu.VMEM)
     return pl.pallas_call(
         lag_kernel,
-        grid_spec=pltpu.PrefetchScalarGridSpec(
-            num_scalar_prefetch=1,
-            grid=(groups,),
-            in_specs=[whole, whole],
-            out_specs=pl.BlockSpec((groups, length), lambda g, order: (0, 0)),
-            scratch_shapes=[
-                pltpu.VMEM((rows, BLOCK), jnp.bfloat16),
-                pltpu.VMEM((rows + BLOCK, BLOCK), jnp.bfloat16),
-                pltpu.VMEM((BLOCK, length + BLOCK), jnp.float32),
-                pltpu.VMEM((groups, length + BLOCK), jnp.float32),
-            ],
-        ),
-        out_shape=jax.ShapeDtypeStruct((groups, length), jnp.float32),
-        compiler_params=params(),
+        in_specs=[pl.BlockSpec(memory_space=pltpu.SMEM), anywhere, anywhere, anywhere],
+        out_specs=[vmem, vmem, vmem],
+        scratch_shapes=[
+            pltpu.VMEM(x.shape, x.dtype),
+            pltpu.VMEM((2, BLOCK, length + BLOCK), jnp.float32),
+            pltpu.VMEM((groups, length + BLOCK), jnp.float32),
+            pltpu.SemaphoreType.DMA((pieces,)),
+            pltpu.SemaphoreType.DMA((pieces,)),
+            pltpu.SemaphoreType.DMA,
+        ],
+        out_shape=[
+            jax.ShapeDtypeStruct((groups, length), jnp.float32),
+            pltpu.VMEM(w.shape, w.dtype),
+            pltpu.VMEM(strip.shape, strip.dtype),
+        ],
+        compiler_params=params(50),
         cost_estimate=SHORT,
-    )(order, x, w)
+    )(
+        order,
+        pltpu.with_memory_space_constraint(x, pltpu.HBM),
+        w,
+        pltpu.with_memory_space_constraint(strip, pltpu.HBM),
+    )
 
 
 def post_kernel(
@@ -371,19 +478,17 @@
 
 
 def shards(output_gate_input, key_input, value_input, upstream, filter_taps, order):
-    groups = filter_taps.shape[0]
     sequences = lax.axis_size("dp")
     product_tiles = pre(key_input, value_input)
     product = exchange(product_tiles)
     weighted_tiles, strip = pre_and_strips(upstream, output_gate_input, filter_taps)
     weighted = exchange(weighted_tiles)
-    mixing_tiles = conv(order, product, strip, False)
+    mixing_tiles = forward(order, product, strip)
     mixing = exchange(mixing_tiles)
     product, _ = lax.optimization_barrier((product, mixing_tiles))
-    lag_sums = lag_sums_of(order, product, weighted, groups)
-    later, lag_sums = lax.optimization_barrier((weighted, lag_sums))
+    lag_sums, weighted_kept, strip_kept = lag_sums_of(order, product, weighted, strip)
     near = [from_partner(lag_sums, step) for step in range(1, sequences // 2)]
-    returned_tiles = conv(order, later, strip, True)
+    returned_tiles = back(order, weighted_kept, strip_kept)
     half = sum(near, lag_sums)
     returned_tiles, half = lax.optimization_barrier((returned_tiles, half))
     returned = exchange(returned_tiles)

time: 113 us -> 111 us (0.982)
  Pallas kernels: 56.8 us -> 51.9 us
  waiting for transfers between devices: 15.7 us -> 19.3 us
    pallas_call x3, Pallas kernels: 34.8 us -> 30 us  [the longest x1 12 us: lag_sums_of(): pl.pallas_call(lag_kernel, in_specs=[pl.BlockSpec(memory_space=pltpu.SMEM...]
    ppermute x4, waiting for transfers between devices: 0.01 us -> 2.5 us  [from_partner(): lax.ppermute(x, 'dp', [(i, i ^ step) for i in range(lax.axis_size('dp'))])]
    all_to_all x4, waiting for transfers between devices: 15.6 us -> 16.8 us  [exchange(): return lax.all_to_all(tiles, 'ctx', split_axis=0, concat_axis=0, tiled=True)]
  transfers between devices with their start and end apart: 8 -> 8, of which waited for: 3 -> 4; matrix products, arithmetic and copies ran while one was open for 0% -> 0% of each run, Pallas kernels for 46% -> 42%
where the time goes in v5:
time: 111 us; the launch traced here: 110 us
  Pallas kernels  51.9 us (47%)
  starting transfers between devices  36.2 us (33%)
  waiting for transfers between devices  19.3 us (17%)
  local copies, waits for them, and re-layouts  1.91 us (2%)
    all_to_all x4, starting transfers between devices, exchange(): return lax.all_to_all(tiles, 'ctx', split_axis=0, concat_axis=0, tiled=True)  25.5 us
    all_to_all x4, waiting for transfers between devices, exchange(): return lax.all_to_all(tiles, 'ctx', split_axis=0, concat_axis=0, tiled=True)  16.8 us
    pallas_call x1, Pallas kernels, pre_and_strips(): pl.pallas_call(functools.partial(pre_strip_kernel, tiles), grid=(groups,)...  12.4 us
    pallas_call x1, Pallas kernels, lag_sums_of(): pl.pallas_call(lag_kernel, in_specs=[pl.BlockSpec(memory_space=pltpu.SMEM...  12 us
    ppermute x4, starting transfers between devices, from_partner(): lax.ppermute(x, 'dp', [(i, i ^ step) for i in range(lax.axis_size('dp'))])  10.7 us
    pallas_call x1, Pallas kernels, forward(): pl.pallas_call(forward_kernel, in_specs=[pl.BlockSpec(memory_space=pltpu....  10.2 us
    pallas_call x1, Pallas kernels, back(): pl.pallas_call(back_kernel, in_specs=[pl.BlockSpec(memory_space=pltpu.SME...  7.79 us
    pallas_call x2, Pallas kernels, post(): pl.pallas_call(post_kernel, in_specs=[anywhere] * 3, out_specs=[anywhere]...  5.25 us
  transfers between devices with their start and end apart: 8, of which 4 were waited for; matrix products, arithmetic and copies ran while one was open for 0% of the time, Pallas kernels for 42%

profile of v5, /device:TPU:1, one launch (start us, length us, event | category | flops | bytes accessed | tf_op | source)
XLA Modules:
  0.0 110.1 jit_solution(1103666884673705605)
XLA Ops:
  0.6 2.4 %shard_map.101 = bf16[32,128,128]{2,1,0:T(8,128)(2,1)} custom-call(bf16[1,128,4096]{2,1,0:T(8,128)(2,1)} %b_hbm.5, bf16[1,128,4096]{2,1,0:T(8,128)(2,1)} %a_hbm.5), custom_call_target="tpu_custom_call" | custom-call | flops 524288 | bytes 3145728 | tf_op jit(solution)/shard_map/pallas_call | solution.py:83
  3.1 8.6 %all-to-all-start = ((bf16[32,128,128]{2,1,0:T(8,128)(2,1)}), bf16[32,128,128]{2,1,0:T(8,128)(2,1)S(1)}, u32[]{:S(2)}, u32[]{:S(2)}) async-start(bf16[32,128,128]{2,1,0:T(8,128)(2,1)} %shard_map.101), calls=%async_computation | async-start | bytes 2097152 | tf_op jit(solution)/shard_map/all_to_all | solution.py:473
  11.7 12.4 %shard_map.102 = (bf16[32,128,128]{2,1,0:T(8,128)(2,1)}, bf16[8,128,4224]{2,1,0:T(8,128)(2,1)}) custom-call(bf16[1,128,4096]{2,1,0:T(8,128)(2,1)} %b_hbm.4, bf16[1,128,4096]{2,1,0:T(8,128)(2,1)} %a_hbm.4, f32[8,4096]{1,0:T(8,128)} %taps_ref.3), custom_call_target="tpu_custom_call" | custom-call | flops 17301504 | bytes 11796480 | tf_op jit(solution)/shard_map/pallas_call | solution.py:134
  24.1 4.8 %all-to-all-done.x_hbm = bf16[32,128,128]{2,1,0:T(8,128)(2,1)S(1)} async-done(((bf16[32,128,128]{2,1,0:T(8,128)(2,1)}), bf16[32,128,128]{2,1,0:T(8,128)(2,1)S(1)}, u32[]{:S(2)}, u32[]{:S(2)}) %all-to-all-start) | async-done | bytes 1048608 | tf_op jit(solution)/shard_map/all_to_all | solution.py:473
  28.9 4.0 %all-to-all-start.1 = ((bf16[32,128,128]{2,1,0:T(8,128)(2,1)}), bf16[32,128,128]{2,1,0:T(8,128)(2,1)S(1)}, u32[]{:S(2)}, u32[]{:S(2)}) async-start(bf16[32,128,128]{2,1,0:T(8,128)(2,1)} %get-tuple-element.21), calls=%async_computation.1 | async-start | bytes 2097152 | tf_op jit(solution)/shard_map/all_to_all | solution.py:473
  32.9 0.0 copy-done.4
  32.9 10.2 %shard_map.103 = bf16[32,128,128]{2,1,0:T(8,128)(2,1)} custom-call(s32[32]{0:T(128)} %order_ref.5, bf16[32,128,128]{2,1,0:T(8,128)(2,1)} %copy-done.4, bf16[8,128,4224]{2,1,0:T(8,128)(2,1)} %get-tuple-element.19.strip_hbm), custom_call_target="tpu_custom_call" | custom-call | flops 1000 | bytes 1000 | tf_op jit(solution)/shard_map/pallas_call | solution.py:266
  43.0 7.1 %all-to-all-done.1.w_hbm = bf16[32,128,128]{2,1,0:T(8,128)(2,1)S(1)} async-done(((bf16[32,128,128]{2,1,0:T(8,128)(2,1)}), bf16[32,128,128]{2,1,0:T(8,128)(2,1)S(1)}, u32[]{:S(2)}, u32[]{:S(2)}) %all-to-all-start.1) | async-done | bytes 1048608 | tf_op jit(solution)/shard_map/all_to_all | solution.py:473
  50.1 4.6 %all-to-all-start.2 = ((bf16[32,128,128]{2,1,0:T(8,128)(2,1)}), bf16[32,128,128]{2,1,0:T(8,128)(2,1)}, u32[]{:S(2)}, u32[]{:S(2)}) async-start(bf16[32,128,128]{2,1,0:T(8,128)(2,1)} %shard_map.103), calls=%async_computation.2 | async-start | bytes 2097152 | tf_op jit(solution)/shard_map/all_to_all | solution.py:473
  54.8 0.0 copy-done.5
  54.8 12.0 %shard_map.104 = (f32[8,4096]{1,0:T(8,128)}, bf16[32,128,128]{2,1,0:T(8,128)(2,1)S(1)}, bf16[8,128,4224]{2,1,0:T(8,128)(2,1)S(1)}) custom-call(s32[32]{0:T(128)} %order_ref.5, bf16[32,128,128]{2,1,0:T(8,128)(2,1)} %copy-done.4, bf16[32,128,128]{2,1,0:T(8,128)(2,1)} %copy-done.5, bf16[8,128,4224]{2,1,0:T(8,128)(2,1)} %get-tuple-element.19.strip_hbm), custom_call_target="tpu_custom_call" | custom-call | flops 1000 | bytes 1000 | tf_op jit(solution)/shard_map/pallas_call | solution.py:376
  66.8 4.4 %collective-permute-start.2 = (f32[8,4096]{1,0:T(8,128)}, f32[8,4096]{1,0:T(8,128)S(1)}, u32[]{:S(2)}, u32[]{:S(2)}) collective-permute-start(f32[8,4096]{1,0:T(8,128)} %get-tuple-element.24), channel_id=1, source_target_pairs={{0,96},{32,64},{64,32},{96,0},{128,224},{160,192},{192,160},{224,1... | collective-permute-start | bytes 393224 | tf_op jit(solution)/shard_map/ppermute | solution.py:477
  71.3 0.0 collective-permute-start.1
  71.3 0.4 collective-permute-start
  71.7 7.8 %shard_map.105 = bf16[32,128,128]{2,1,0:T(8,128)(2,1)} custom-call(s32[32]{0:T(128)} %order_ref.5, bf16[32,128,128]{2,1,0:T(8,128)(2,1)S(1)} %get-tuple-element.22.x, bf16[8,128,4224]{2,1,0:T(8,128)(2,1)S(1)} %get-tuple-element.23.strip), custom_call_target="tpu_custom_call" | custom-call | flops 10000000000 | bytes 1000 | tf_op jit(solution)/shard_map/pallas_call | solution.py:288
  79.5 0.0 collective-permute-done.2
  79.5 2.5 %collective-permute-done.1 = f32[8,4096]{1,0:T(8,128)S(1)} collective-permute-done((f32[8,4096]{1,0:T(8,128)}, f32[8,4096]{1,0:T(8,128)S(1)}, u32[]{:S(2)}, u32[]{:S(2)}) %collective-permute-start.1) | collective-permute-done | bytes 131104 | tf_op jit(solution)/shard_map/ppermute | solution.py:477
  82.0 0.0 collective-permute-done
  82.0 0.0 copy-done.7
  82.0 0.0 copy-start.6
  82.0 0.0 all-to-all-done.2.r_hbm
  82.0 8.2 %all-to-all-start.3 = ((bf16[32,128,128]{2,1,0:T(8,128)(2,1)}), bf16[32,128,128]{2,1,0:T(8,128)(2,1)}, u32[]{:S(2)}, u32[]{:S(2)}) async-start(bf16[32,128,128]{2,1,0:T(8,128)(2,1)} %shard_map.105), calls=%async_computation.3 | async-start | bytes 2097152 | tf_op jit(solution)/shard_map/all_to_all | solution.py:473
  90.3 5.9 %collective-permute-start.3 = (f32[8,4096]{1,0:T(8,128)S(1)}, f32[8,4096]{1,0:T(8,128)S(1)}, u32[]{:S(2)}, u32[]{:S(2)}) collective-permute-start(f32[8,4096]{1,0:T(8,128)S(1)} %add_add_fusion.mine_ref), channel_id=1, source_target_pairs={{0,128},{32,160},{64,192},{96,224},{128,0},{160,32},{192,64},{224,... | collective-permute-start | bytes 393224 | tf_op jit(solution)/shard_map/ppermute | solution.py:477
  96.2 0.0 copy-done.2
  96.2 1.2 %copy-done.3 = bf16[1,128,4096]{2,1,0:T(8,128)(2,1)S(1)} copy-done((bf16[1,128,4096]{2,1,0:T(8,128)(2,1)S(1)}, bf16[1,128,4096]{2,1,0:T(8,128)(2,1)}, u32[]{:S(2)}) %copy-start.3) | copy-done | bytes 1048600
  97.4 2.6 %shard_map.106 = (bf16[1,128,4096]{2,1,0:T(8,128)(2,1)}, bf16[1,128,4096]{2,1,0:T(8,128)(2,1)}) custom-call(bf16[32,128,128]{2,1,0:T(8,128)(2,1)} %all-to-all-done.2.r_hbm, bf16[1,128,4096]{2,1,0:T(8,128)(2,1)S(1)} %copy-done.3, bf16[1,128,4096]{2,1,0:T(8,128)(2,1)S(1)} %copy-done.2), custom_call_target="tpu_custom_call" | custom-call | flops 1048576 | bytes 5242880 | tf_op jit(solution)/shard_map/pallas_call | solution.py:439
  100.0 0.0 collective-permute-done.3.others_ref
  100.1 0.0 copy-done.6
  100.1 0.7 copy-done.8
  100.7 1.8 %shard_map.108 = f32[8,4096]{1,0:T(8,128)} custom-call(f32[8,4096]{1,0:T(8,128)} %taps_ref.3, f32[8,4096]{1,0:T(8,128)} %copy-done.6, f32[8,4096]{1,0:T(8,128)} %copy-done.8), custom_call_target="tpu_custom_call" | custom-call | tf_op jit(solution)/shard_map/pallas_call | solution.py:465
  102.6 4.9 %all-to-all-done.3.r_hbm = bf16[32,128,128]{2,1,0:T(8,128)(2,1)} async-done(((bf16[32,128,128]{2,1,0:T(8,128)(2,1)}), bf16[32,128,128]{2,1,0:T(8,128)(2,1)}, u32[]{:S(2)}, u32[]{:S(2)}) %all-to-all-start.3) | async-done | bytes 1048608 | tf_op jit(solution)/shard_map/all_to_all | solution.py:473
  107.5 2.6 %shard_map.107 = (bf16[1,128,4096]{2,1,0:T(8,128)(2,1)}, bf16[1,128,4096]{2,1,0:T(8,128)(2,1)}) custom-call(bf16[32,128,128]{2,1,0:T(8,128)(2,1)} %all-to-all-done.3.r_hbm, bf16[1,128,4096]{2,1,0:T(8,128)(2,1)S(1)} %copy-done.1, bf16[1,128,4096]{2,1,0:T(8,128)(2,1)S(1)} %copy-done), custom_call_target="tpu_custom_call" | custom-call | flops 1048576 | bytes 5242880 | tf_op jit(solution)/shard_map/pallas_call | solution.py:439
  (11 shorter events, 0.0 us)
Async XLA Ops:
  3.1 25.8 %all-to-all-start = ((bf16[32,128,128]{2,1,0:T(8,128)(2,1)}), bf16[32,128,128]{2,1,0:T(8,128)(2,1)S(1)}, u32[]{:S(2)}, u32[]{:S(2)}) async-start(bf16[32,128,128]{2,1,0:T(8,128)(2,1)} %shard_map.101), calls=%async_computation | async-start | bytes 2097152 | tf_op jit(solution)/shard_map/all_to_all | solution.py:473
  28.9 4.0 %copy-start.4 = (bf16[32,128,128]{2,1,0:T(8,128)(2,1)}, bf16[32,128,128]{2,1,0:T(8,128)(2,1)S(1)}, u32[]{:S(2)}) copy-start(bf16[32,128,128]{2,1,0:T(8,128)(2,1)S(1)} %all-to-all-done.x_hbm) | copy-start | bytes 3145732
  28.9 21.3 %all-to-all-start.1 = ((bf16[32,128,128]{2,1,0:T(8,128)(2,1)}), bf16[32,128,128]{2,1,0:T(8,128)(2,1)S(1)}, u32[]{:S(2)}, u32[]{:S(2)}) async-start(bf16[32,128,128]{2,1,0:T(8,128)(2,1)} %get-tuple-element.21), calls=%async_computation.1 | async-start | bytes 2097152 | tf_op jit(solution)/shard_map/all_to_all | solution.py:473
  50.1 4.7 %copy-start.5 = (bf16[32,128,128]{2,1,0:T(8,128)(2,1)}, bf16[32,128,128]{2,1,0:T(8,128)(2,1)S(1)}, u32[]{:S(2)}) copy-start(bf16[32,128,128]{2,1,0:T(8,128)(2,1)S(1)} %all-to-all-done.1.w_hbm) | copy-start | bytes 3145732
  50.1 31.9 %all-to-all-start.2 = ((bf16[32,128,128]{2,1,0:T(8,128)(2,1)}), bf16[32,128,128]{2,1,0:T(8,128)(2,1)}, u32[]{:S(2)}, u32[]{:S(2)}) async-start(bf16[32,128,128]{2,1,0:T(8,128)(2,1)} %shard_map.103), calls=%async_computation.2 | async-start | bytes 2097152 | tf_op jit(solution)/shard_map/all_to_all | solution.py:473
  66.8 12.6 %collective-permute-start.2 = (f32[8,4096]{1,0:T(8,128)}, f32[8,4096]{1,0:T(8,128)S(1)}, u32[]{:S(2)}, u32[]{:S(2)}) collective-permute-start(f32[8,4096]{1,0:T(8,128)} %get-tuple-element.24), channel_id=1, source_target_pairs={{0,96},{32,64},{64,32},{96,0},{128,224},{160,192},{192,160},{224,1... | collective-permute-start | bytes 393224 | tf_op jit(solution)/shard_map/ppermute | solution.py:477
  71.3 10.7 %collective-permute-start.1 = (f32[8,4096]{1,0:T(8,128)}, f32[8,4096]{1,0:T(8,128)S(1)}, u32[]{:S(2)}, u32[]{:S(2)}) collective-permute-start(f32[8,4096]{1,0:T(8,128)} %get-tuple-element.24), channel_id=1, source_target_pairs={{0,64},{32,96},{64,0},{96,32},{128,192},{160,224},{192,128},{224,1... | collective-permute-start | bytes 393224 | tf_op jit(solution)/shard_map/ppermute | solution.py:477
  71.3 10.7 %collective-permute-start = (f32[8,4096]{1,0:T(8,128)}, f32[8,4096]{1,0:T(8,128)S(1)}, u32[]{:S(2)}, u32[]{:S(2)}) collective-permute-start(f32[8,4096]{1,0:T(8,128)} %get-tuple-element.24), channel_id=1, source_target_pairs={{0,32},{32,0},{64,96},{96,64},{128,160},{160,128},{192,224},{224,1... | collective-permute-start | bytes 393224 | tf_op jit(solution)/shard_map/ppermute | solution.py:477
  71.6 10.3 %copy-start.7 = (f32[8,4096]{1,0:T(8,128)S(1)}, f32[8,4096]{1,0:T(8,128)}, u32[]{:S(2)}) copy-start(f32[8,4096]{1,0:T(8,128)} %get-tuple-element.24) | copy-start | bytes 393220
  71.6 24.5 %copy-start.2 = (bf16[1,128,4096]{2,1,0:T(8,128)(2,1)S(1)}, bf16[1,128,4096]{2,1,0:T(8,128)(2,1)}, u32[]{:S(2)}) copy-start(bf16[1,128,4096]{2,1,0:T(8,128)(2,1)} %b_hbm.4) | copy-start | bytes 3145732
  71.6 35.8 %copy-start = (bf16[1,128,4096]{2,1,0:T(8,128)(2,1)S(1)}, bf16[1,128,4096]{2,1,0:T(8,128)(2,1)}, u32[]{:S(2)}) copy-start(bf16[1,128,4096]{2,1,0:T(8,128)(2,1)} %b_hbm.5) | copy-start | bytes 3145732
  71.7 35.8 %copy-start.1 = (bf16[1,128,4096]{2,1,0:T(8,128)(2,1)S(1)}, bf16[1,128,4096]{2,1,0:T(8,128)(2,1)}, u32[]{:S(2)}) copy-start(bf16[1,128,4096]{2,1,0:T(8,128)(2,1)} %a_hbm.5) | copy-start | bytes 3145732
  82.0 18.1 %copy-start.6 = (f32[8,4096]{1,0:T(8,128)}, f32[8,4096]{1,0:T(8,128)S(1)}, u32[]{:S(2)}) copy-start(f32[8,4096]{1,0:T(8,128)S(1)} %add_add_fusion.mine_ref) | copy-start | bytes 393220
  82.0 25.5 %all-to-all-start.3 = ((bf16[32,128,128]{2,1,0:T(8,128)(2,1)}), bf16[32,128,128]{2,1,0:T(8,128)(2,1)}, u32[]{:S(2)}, u32[]{:S(2)}) async-start(bf16[32,128,128]{2,1,0:T(8,128)(2,1)} %shard_map.105), calls=%async_computation.3 | async-start | bytes 2097152 | tf_op jit(solution)/shard_map/all_to_all | solution.py:473
  90.3 9.8 %collective-permute-start.3 = (f32[8,4096]{1,0:T(8,128)S(1)}, f32[8,4096]{1,0:T(8,128)S(1)}, u32[]{:S(2)}, u32[]{:S(2)}) collective-permute-start(f32[8,4096]{1,0:T(8,128)S(1)} %add_add_fusion.mine_ref), channel_id=1, source_target_pairs={{0,128},{32,160},{64,192},{96,224},{128,0},{160,32},{192,64},{224,... | collective-permute-start | bytes 393224 | tf_op jit(solution)/shard_map/ppermute | solution.py:477
  96.2 1.2 %copy-start.3 = (bf16[1,128,4096]{2,1,0:T(8,128)(2,1)S(1)}, bf16[1,128,4096]{2,1,0:T(8,128)(2,1)}, u32[]{:S(2)}) copy-start(bf16[1,128,4096]{2,1,0:T(8,128)(2,1)} %a_hbm.4) | copy-start | bytes 3145732
  100.1 0.7 copy-start.8

commit v6 on v5

v6 whole, which is shorter than its diff:
```python
import functools
import math

import jax
import jax.numpy as jnp
from jax import lax
from jax.experimental import pallas as pl
from jax.experimental.pallas import tpu as pltpu
from jax.sharding import PartitionSpec as P

EPSILON = 1e-06
BLOCK = 128
GROUP = 16
MIB = 1024 * 1024
SPAN = 1
AT_ONCE = 8
CHUNKS = 4

SHORT = pl.CostEstimate(flops=1000, bytes_accessed=1000, transcendentals=0)
LONG = pl.CostEstimate(flops=10**10, bytes_accessed=1000, transcendentals=0)

NN = (((1,), (0,)), ((), ()))
NT = (((1,), (1,)), ((), ()))
TN = (((0,), (0,)), ((), ()))


def dot(a, b, dims):
    return lax.dot_general(a, b, dims, preferred_element_type=jnp.float32)


def params(mib=60):
    return pltpu.CompilerParams(vmem_limit_bytes=mib * MIB)


def product_of(a, b):
    return a * b


def copies(source, target, sems, chunks):
    step = source.shape[-1] // chunks
    made = []
    for i in range(chunks):
        cols = pl.ds(i * step, step)
        made.append(
            pltpu.make_async_copy(source.at[0, :, cols], target.at[0, :, cols], sems.at[i])
        )
    return made


def tile_copies(source, target, sems, chunks):
    step = source.shape[0] // chunks
    made = []
    for i in range(chunks):
        part = pl.ds(i * step, step)
        made.append(pltpu.make_async_copy(source.at[part], target.at[part], sems.at[i]))
    return made


def pre_kernel(a_hbm, b_hbm, c_hbm, d_hbm, out_hbm, a, b, c, d, out, in_sem, out_sem):
    into = list(
        zip(
            *[
                copies(source, target, in_sem.at[k], CHUNKS)
                for k, (source, target) in enumerate(
                    ((a_hbm, a), (b_hbm, b), (c_hbm, c), (d_hbm, d))
                )
            ],
            strict=True,
        )
    )
    leave = tile_copies(out, out_hbm, out_sem, CHUNKS)
    for group in into:
        start(group)
    tiles = out.shape[0] // CHUNKS
    for i in range(CHUNKS):
        wait(into[i])
        for t in range(i * tiles, (i + 1) * tiles):
            cols = slice(t * BLOCK, (t + 1) * BLOCK)
            out[t, :BLOCK, :] = product_of(a[0, :, cols], b[0, :, cols]).T
            out[t, BLOCK:, :] = product_of(c[0, :, cols], d[0, :, cols]).T
        leave[i].start()
    wait(leave)


def pre(a, b, c, d):
    _, rows, channels = a.shape
    tiles = (channels // BLOCK, 2 * BLOCK, rows)
    anywhere = pl.BlockSpec(memory_space=pl.ANY)
    return pl.pallas_call(
        pre_kernel,
        in_specs=[anywhere] * 4,
        out_specs=anywhere,
        out_shape=jax.ShapeDtypeStruct(tiles, jnp.bfloat16),
        scratch_shapes=[pltpu.VMEM(a.shape, jnp.bfloat16)] * 4
        + [
            pltpu.VMEM(tiles, jnp.bfloat16),
            pltpu.SemaphoreType.DMA((4, CHUNKS)),
            pltpu.SemaphoreType.DMA((CHUNKS,)),
        ],
        compiler_params=params(),
        cost_estimate=pl.CostEstimate(
            flops=2 * a.size, bytes_accessed=12 * a.size, transcendentals=0
        ),
    )(a, b, c, d)


def strip_kernel(taps_ref, out_ref):
    g = pl.program_id(0)
    taps = taps_ref[pl.ds(g, 1), :]
    length = taps.shape[1]
    root = jnp.sqrt(jnp.mean(taps * taps, axis=1, keepdims=True) + EPSILON)
    row = taps * (1.0 / (math.sqrt(length) * root))
    width = length + BLOCK
    cur = jnp.concatenate([jnp.zeros((1, BLOCK), jnp.float32), row], axis=1)
    cur = jnp.broadcast_to(cur, (16, width))
    line = lax.broadcasted_iota(jnp.int32, (16, width), 0)
    for step in (1, 2, 4, 8):
        cur = jnp.where((line & step) != 0, pltpu.roll(cur, step, 1), cur)
    for q in range(BLOCK // 16):
        if q:
            cur = pltpu.roll(cur, 16, 1)
        out_ref[0, 16 * q : 16 * (q + 1), :] = cur.astype(jnp.bfloat16)
    out_ref[0, :, :BLOCK] = jnp.zeros((BLOCK, BLOCK), jnp.bfloat16)


def strips(taps):
    groups, length = taps.shape
    width = length + BLOCK
    return pl.pallas_call(
        strip_kernel,
        grid=(groups,),
        in_specs=[pl.BlockSpec((groups, length), lambda g: (0, 0))],
        out_specs=pl.BlockSpec((1, BLOCK, width), lambda g: (g, 0, 0)),
        out_shape=jax.ShapeDtypeStruct((groups, BLOCK, width), jnp.bfloat16),
        compiler_params=params(),
        cost_estimate=LONG,
    )(taps)


def in_order(order_ref, source, target, sems):
    return [
        pltpu.make_async_copy(source.at[d], target.at[order_ref[d]], sems.at[d])
        for d in range(source.shape[0])
    ]


def start(made):
    for copy in made:
        copy.start()


def wait(made):
    for copy in made:
        copy.wait()


def rows_of(group):
    first = GROUP * group
    return pl.ds(first if isinstance(first, int) else pl.multiple_of(first, GROUP), GROUP)


def filters_kernel(order_ref, x_hbm, strip_hbm, out_hbm, x, strip, out, acc, x_sem, s_sem, out_sem):
    groups = strip.shape[0]
    arrive = in_order(order_ref, x_hbm, x, x_sem)
    start(arrive)
    for g in range(groups):
        pltpu.make_async_copy(strip_hbm.at[g], strip.at[g], s_sem.at[g]).start()
    wait(arrive)

    @pl.loop(0, groups)
    def _(g):
        pltpu.make_async_copy(strip_hbm.at[g], strip.at[g], s_sem.at[g]).wait()
        filter_group(False, g, 0, x, strip, out, acc.at[0])
        filter_group(True, g, groups, x, strip, out, acc.at[1])

    leave = [
        pltpu.make_async_copy(out.at[order_ref[d]], out_hbm.at[d], out_sem.at[d])
        for d in range(out.shape[0])
    ]
    start(leave)
    wait(leave)


def filter_group(backward, g, shift, x, strip, out, acc):
    pieces = x.shape[0]
    pairs = pieces // 2
    wide = 2 * BLOCK
    nothing = jnp.zeros((GROUP, wide), jnp.bfloat16)
    rows = rows_of(g + shift)
    blocks = [
        jnp.concatenate([x[2 * i, rows, :], x[2 * i + 1, rows, :]], axis=1)
        for i in range(pairs)
    ]
    for lag in range(0, pairs, SPAN):
        at = BLOCK + wide * lag
        lefts, weights = [], []
        for k in range(min(SPAN, pairs - lag)):
            if backward:
                froms = range(lag + k, pairs + k)
            else:
                froms = range(-k, pairs - lag - k)
            lefts.append(
                jnp.concatenate(
                    [blocks[i] if 0 <= i < pairs else nothing for i in froms], axis=0
                )
            )
            weights += [
                strip[g, :, at + wide * k : at + wide * (k + 1)],
                strip[g, :, at + wide * k - BLOCK : at + wide * k + BLOCK],
            ]
        if backward:
            ends = at + wide * min(SPAN, pairs - lag)
            weights = [strip[g, :, at:ends], strip[g, :, at - BLOCK : ends - BLOCK]]
        part = dot(
            jnp.concatenate(lefts, axis=1),
            jnp.concatenate(weights, axis=0),
            NT if backward else NN,
        )
        depth = GROUP * (pairs - lag)
        if lag == 0:
            acc[...] = part
        elif backward:
            acc[:depth, :] += part
        else:
            acc[GROUP * lag :, :] += part
    for i in range(pairs):
        both = acc[rows_of(i), :].astype(jnp.bfloat16)
        out[2 * i, rows, :] = both[:, :BLOCK]
        out[2 * i + 1, rows, :] = both[:, BLOCK:]


def filters(order, x, strip):
    pieces = x.shape[0]
    groups = strip.shape[0]
    rows = GROUP * pieces // 2
    anywhere = pl.BlockSpec(memory_space=pl.ANY)
    return pl.pallas_call(
        filters_kernel,
        in_specs=[pl.BlockSpec(memory_space=pltpu.SMEM), anywhere, anywhere],
        out_specs=anywhere,
        scratch_shapes=[
            pltpu.VMEM(x.shape, x.dtype),
            pltpu.VMEM(strip.shape, strip.dtype),
            pltpu.VMEM(x.shape, x.dtype),
            pltpu.VMEM((2, rows, 2 * BLOCK), jnp.float32),
            pltpu.SemaphoreType.DMA((pieces,)),
            pltpu.SemaphoreType.DMA((groups,)),
            pltpu.SemaphoreType.DMA((pieces,)),
        ],
        out_shape=pltpu.HBM(x.shape, x.dtype),
        compiler_params=params(40),
        cost_estimate=LONG,
    )(order, x, pltpu.with_memory_space_constraint(strip, pltpu.HBM))


def lag_kernel(order_ref, x_hbm, out_ref, x, squares, sums, x_sem):
    pieces = x.shape[0]
    groups = out_ref.shape[0]
    total = GROUP * pieces
    last = BLOCK - 1
    arrive = in_order(order_ref, x_hbm, x, x_sem)
    start(arrive)
    row = lax.broadcasted_iota(jnp.int32, (BLOCK, BLOCK), 0)
    col = lax.broadcasted_iota(jnp.int32, (BLOCK, BLOCK), 1)
    mirror = jnp.where(row + col == last, 1.0, 0.0).astype(jnp.bfloat16)
    nothing = jnp.zeros((GROUP, BLOCK), jnp.bfloat16)
    for i in range(2):
        squares[i, :, pieces * BLOCK :] = jnp.zeros((BLOCK, BLOCK), jnp.float32)
    wait(arrive)
    def one(g, here):
        xs = jnp.concatenate([x[j, rows_of(g), :] for j in range(pieces)], axis=0)
        x_turned = dot(mirror, xs, NT).astype(jnp.bfloat16)
        blocks = [x[j, rows_of(g + groups), :] for j in range(pieces)]
        for lag in range(0, pieces, 2):
            depth = total - GROUP * lag // BLOCK * BLOCK
            right = jnp.concatenate(
                [
                    jnp.concatenate(
                        [
                            blocks[j] if j < pieces else nothing
                            for j in range(first, first + depth // GROUP)
                        ],
                        axis=0,
                    )
                    for first in (lag, lag + 1)
                ],
                axis=1,
            )
            squares[here, :, lag * BLOCK : (lag + 2) * BLOCK] = dot(
                x_turned[:, :depth], right, NN
            )
        step = 8
        for t in range(0, pieces, step):
            cols = slice(t * BLOCK, (t + step + 1) * BLOCK)
            added = None
            for q in range(BLOCK // 8):
                moved = pltpu.roll(
                    squares[here, 8 * q : 8 * q + 8, cols], 8 * q, 1, stride=1, stride_axis=0
                )
                added = moved if added is None else added + moved
            added = jnp.sum(added, axis=0, keepdims=True)
            skip = BLOCK if t else 0
            sums[pl.ds(g, 1), t * BLOCK + skip : (t + step + 1) * BLOCK] = added[:, skip:]

    @pl.loop(0, groups // AT_ONCE)
    def _(i):
        for k in range(AT_ONCE):
            one(i * AT_ONCE + k, k % 2)

    width = sums.shape[1]
    out_ref[...] = pltpu.roll(sums[...], width - last, 1)[:, : pieces * BLOCK]


def lag_sums_of(order, x, groups):
    pieces = x.shape[0]
    length = pieces * BLOCK
    return pl.pallas_call(
        lag_kernel,
        in_specs=[
            pl.BlockSpec(memory_space=pltpu.SMEM),
            pl.BlockSpec(memory_space=pl.ANY),
        ],
        out_specs=pl.BlockSpec(memory_space=pltpu.VMEM),
        scratch_shapes=[
            pltpu.VMEM(x.shape, x.dtype),
            pltpu.VMEM((2, BLOCK, length + BLOCK), jnp.float32),
            pltpu.VMEM((groups, length + BLOCK), jnp.float32),
            pltpu.SemaphoreType.DMA((pieces,)),
        ],
        out_shape=jax.ShapeDtypeStruct((groups, length), jnp.float32),
        compiler_params=params(),
        cost_estimate=SHORT,
    )(order, pltpu.with_memory_space_constraint(x, pltpu.HBM))


def post_kernel(r_hbm, *refs):
    ins, outs = refs[:4], refs[4:8]
    r, here, made, r_sem, in_sem, out_sem = refs[8], refs[9:13], refs[13:17], *refs[17:]
    into = list(
        zip(
            tile_copies(r_hbm, r, r_sem, CHUNKS),
            *[copies(ins[k], here[k], in_sem.at[k], CHUNKS) for k in range(4)],
            strict=True,
        )
    )
    leave = list(
        zip(*[copies(made[k], outs[k], out_sem.at[k], CHUNKS) for k in range(4)], strict=True)
    )
    for group in into:
        start(group)
    tiles = r.shape[0] // CHUNKS
    for i in range(CHUNKS):
        wait(into[i])
        for t in range(i * tiles, (i + 1) * tiles):
            cols = slice(t * BLOCK, (t + 1) * BLOCK)
            for half in range(2):
                turned = r[t, half * BLOCK : (half + 1) * BLOCK, :].T
                for k in (2 * half, 2 * half + 1):
                    made[k][0, :, cols] = product_of(here[k][0, :, cols], turned)
        start(leave[i])
    for group in leave:
        wait(group)


def post(r, *factors):
    anywhere = pl.BlockSpec(memory_space=pl.ANY)
    a = factors[0]
    return pl.pallas_call(
        post_kernel,
        in_specs=[anywhere] * 5,
        out_specs=[anywhere] * 4,
        out_shape=[jax.ShapeDtypeStruct(a.shape, a.dtype)] * 4,
        scratch_shapes=[pltpu.VMEM(r.shape, r.dtype)]
        + [pltpu.VMEM(a.shape, a.dtype)] * 8
        + [
            pltpu.SemaphoreType.DMA((CHUNKS,)),
            pltpu.SemaphoreType.DMA((4, CHUNKS)),
            pltpu.SemaphoreType.DMA((4, CHUNKS)),
        ],
        compiler_params=params(40),
        cost_estimate=pl.CostEstimate(
            flops=4 * a.size, bytes_accessed=20 * a.size, transcendentals=0
        ),
    )(r, *[pltpu.with_memory_space_constraint(a, pltpu.HBM) for a in factors])


def taps_kernel(sequences, taps_ref, mine_ref, others_ref, out_ref):
    taps = taps_ref[...]
    length = taps.shape[1]
    root = jnp.sqrt(jnp.mean(taps * taps, axis=1, keepdims=True) + EPSILON)
    scale = 1.0 / (math.sqrt(length) * root)
    mean = (mine_ref[...] + others_ref[...]) / sequences
    projection = jnp.sum(mean * taps, axis=1, keepdims=True)
    out_ref[...] = scale * mean - taps * (scale * scale * scale) * projection


def taps_grad_of(taps, mine, others, sequences):
    return pl.pallas_call(
        functools.partial(taps_kernel, sequences),
        out_shape=jax.ShapeDtypeStruct(taps.shape, jnp.float32),
        compiler_params=params(),
    )(taps, mine, others)


def exchange(tiles):
    return lax.all_to_all(tiles, "ctx", split_axis=0, concat_axis=0, tiled=True)


def from_partner(x, step):
    return lax.ppermute(x, "dp", [(i, i ^ step) for i in range(lax.axis_size("dp"))])


def shards(output_gate_input, key_input, value_input, upstream, filter_taps, order):
    sequences = lax.axis_size("dp")
    arrived = exchange(pre(key_input, value_input, upstream, output_gate_input))
    strip = strips(filter_taps)
    filtered = filters(order, arrived, strip)
    returned = exchange(filtered)
    arrived, _ = lax.optimization_barrier((arrived, filtered))
    lag_sums = lag_sums_of(order, arrived, filter_taps.shape[0])
    near = [from_partner(lag_sums, step) for step in range(1, sequences // 2)]
    half = sum(near, lag_sums)
    far = from_partner(half, sequences // 2)
    mixed_out, gate_grad, key_grad, value_grad = post(
        returned, output_gate_input, upstream, value_input, key_input
    )
    half, mixed_out = lax.optimization_barrier((half, mixed_out))
    taps_grad = taps_grad_of(filter_taps, half, far, sequences)
    return mixed_out, gate_grad, key_grad, value_grad, taps_grad


def solution(mesh):
    rows = P("dp", "ctx", None)
    return jax.shard_map(
        shards,
        mesh=mesh,
        in_specs=(rows, rows, rows, rows, P("ctx", None), P()),
        out_specs=(rows, rows, rows, rows, P("ctx", None)),
        check_vma=False,
    )
```

time: 111 us -> 101 us (0.910)
  the two profiles are of different devices: /device:TPU:1 before, /device:TPU:2 now
where the time goes in v6:
time: 101 us; the launch traced here: 100 us
  Pallas kernels  45.3 us (45%)
  waiting for transfers between devices  27.6 us (27%)
  starting transfers between devices  25.3 us (25%)
    all_to_all x2, waiting for transfers between devices, exchange(): return lax.all_to_all(tiles, 'ctx', split_axis=0, concat_axis=0, tiled=True)  15.8 us
    pallas_call x1, Pallas kernels, filters(): pl.pallas_call(filters_kernel, in_specs=[pl.BlockSpec(memory_space=pltpu....  15 us
    all_to_all x2, starting transfers between devices, exchange(): return lax.all_to_all(tiles, 'ctx', split_axis=0, concat_axis=0, tiled=True)  13.7 us
    pallas_call x1, Pallas kernels, strips(): pl.pallas_call(strip_kernel, grid=(groups,), in_specs=[pl.BlockSpec((grou...  12 us
    ppermute x4, waiting for transfers between devices, from_partner(): lax.ppermute(x, 'dp', [(i, i ^ step) for i in range(lax.axis_size('dp'))])  11.8 us
    ppermute x4, starting transfers between devices, from_partner(): lax.ppermute(x, 'dp', [(i, i ^ step) for i in range(lax.axis_size('dp'))])  11.6 us
    pallas_call x1, Pallas kernels, lag_sums_of(): pl.pallas_call(lag_kernel, in_specs=[pl.BlockSpec(memory_space=pltpu.SMEM...  8.78 us
    pallas_call x1, Pallas kernels, post(): pl.pallas_call(post_kernel, in_specs=[anywhere] * 5, out_specs=[anywhere]...  4.19 us
  transfers between devices with their start and end apart: 6, of which 4 were waited for; matrix products, arithmetic and copies ran while one was open for 1% of the time, Pallas kernels for 25%

profile of v6, /device:TPU:2, one launch (start us, length us, event | category | flops | bytes accessed | tf_op | source)
XLA Modules:
  0.0 100.5 jit_solution(4790302585995703247)
XLA Ops:
  0.6 3.4 %shard_map.101 = bf16[32,256,128]{2,1,0:T(8,128)(2,1)} custom-call(bf16[1,128,4096]{2,1,0:T(8,128)(2,1)} %refs_3_.1, bf16[1,128,4096]{2,1,0:T(8,128)(2,1)} %refs_2_.1, bf16[1,128,4096]{2,1,0:T(8,128)(2,1)} %refs_1_.1, bf16[1,128,4096]{2,1,0:T(8,128)(2,1)} %refs_0_.1), custom_call_target="tpu_custom_call" | custom-call | flops 1048576 | bytes 6291456 | tf_op jit(solution)/shard_map/pallas_call | solution.py:89
  4.0 7.6 %all-to-all-start = ((bf16[32,256,128]{2,1,0:T(8,128)(2,1)}), bf16[32,256,128]{2,1,0:T(8,128)(2,1)S(1)}, u32[]{:S(2)}, u32[]{:S(2)}) async-start(bf16[32,256,128]{2,1,0:T(8,128)(2,1)} %shard_map.101), calls=%async_computation | async-start | bytes 4194304 | tf_op jit(solution)/shard_map/all_to_all | solution.py:406
  11.6 0.0 copy-start.1
  11.7 12.0 %shard_map.102.strip_hbm = bf16[8,128,4224]{2,1,0:T(8,128)(2,1)} custom-call(f32[8,4096]{1,0:T(8,128)} %taps_ref.3), custom_call_target="tpu_custom_call" | custom-call | flops 10000000000 | bytes 1000 | tf_op jit(solution)/shard_map/pallas_call | solution.py:129
  23.7 15.8 %all-to-all-done.x_hbm = bf16[32,256,128]{2,1,0:T(8,128)(2,1)S(1)} async-done(((bf16[32,256,128]{2,1,0:T(8,128)(2,1)}), bf16[32,256,128]{2,1,0:T(8,128)(2,1)S(1)}, u32[]{:S(2)}, u32[]{:S(2)}) %all-to-all-start) | async-done | bytes 2097184 | tf_op jit(solution)/shard_map/all_to_all | solution.py:406
  39.5 0.0 copy-done.1
  39.5 0.0 copy-start
  39.5 15.0 %shard_map.103 = bf16[32,256,128]{2,1,0:T(8,128)(2,1)} custom-call(s32[32]{0:T(128)S(1)} %copy-done.1, bf16[32,256,128]{2,1,0:T(8,128)(2,1)S(1)} %all-to-all-done.x_hbm, bf16[8,128,4224]{2,1,0:T(8,128)(2,1)} %shard_map.102.strip_hbm), custom_call_target="tpu_custom_call" | custom-call | flops 10000000000 | bytes 1000 | tf_op jit(solution)/shard_map/pallas_call | solution.py:237
  54.6 0.0 copy-done
  54.6 6.0 %all-to-all-start.1 = ((bf16[32,256,128]{2,1,0:T(8,128)(2,1)}), bf16[32,256,128]{2,1,0:T(8,128)(2,1)S(1)}, u32[]{:S(2)}, u32[]{:S(2)}) async-start(bf16[32,256,128]{2,1,0:T(8,128)(2,1)} %shard_map.103), calls=%async_computation.1 | async-start | bytes 4194304 | tf_op jit(solution)/shard_map/all_to_all | solution.py:406
  60.6 8.8 %shard_map.104 = f32[8,4096]{1,0:T(8,128)} custom-call(s32[32]{0:T(128)} %order_ref.3, bf16[32,256,128]{2,1,0:T(8,128)(2,1)} %copy-done), custom_call_target="tpu_custom_call" | custom-call | flops 1000 | bytes 1000 | tf_op jit(solution)/shard_map/pallas_call | solution.py:317
  69.4 4.7 %collective-permute-start.2 = (f32[8,4096]{1,0:T(8,128)}, f32[8,4096]{1,0:T(8,128)S(1)}, u32[]{:S(2)}, u32[]{:S(2)}) collective-permute-start(f32[8,4096]{1,0:T(8,128)} %shard_map.104), channel_id=1, source_target_pairs={{0,96},{32,64},{64,32},{96,0},{128,224},{160,192},{192,160},{224,1... | collective-permute-start | bytes 393224 | tf_op jit(solution)/shard_map/ppermute | solution.py:410
  74.1 0.0 collective-permute-start.1
  74.1 0.7 collective-permute-start
  74.8 3.9 %collective-permute-done.2 = f32[8,4096]{1,0:T(8,128)S(1)} collective-permute-done((f32[8,4096]{1,0:T(8,128)}, f32[8,4096]{1,0:T(8,128)S(1)}, u32[]{:S(2)}, u32[]{:S(2)}) %collective-permute-start.2) | collective-permute-done | bytes 131104 | tf_op jit(solution)/shard_map/ppermute | solution.py:410
  78.7 6.5 %collective-permute-done.1 = f32[8,4096]{1,0:T(8,128)S(1)} collective-permute-done((f32[8,4096]{1,0:T(8,128)}, f32[8,4096]{1,0:T(8,128)S(1)}, u32[]{:S(2)}, u32[]{:S(2)}) %collective-permute-start.1) | collective-permute-done | bytes 131104 | tf_op jit(solution)/shard_map/ppermute | solution.py:410
  85.2 0.0 collective-permute-done
  85.2 0.9 add_add_fusion.mine_ref
  86.2 0.0 copy-start.2
  86.2 6.2 %collective-permute-start.3 = (f32[8,4096]{1,0:T(8,128)S(1)}, f32[8,4096]{1,0:T(8,128)S(1)}, u32[]{:S(2)}, u32[]{:S(2)}) collective-permute-start(f32[8,4096]{1,0:T(8,128)S(1)} %add_add_fusion.mine_ref), channel_id=1, source_target_pairs={{0,128},{32,160},{64,192},{96,224},{128,0},{160,32},{192,64},{224,... | collective-permute-start | bytes 393224 | tf_op jit(solution)/shard_map/ppermute | solution.py:410
  92.4 0.0 all-to-all-done.1.r_hbm
  92.4 4.2 %shard_map.105 = (bf16[1,128,4096]{2,1,0:T(8,128)(2,1)}, bf16[1,128,4096]{2,1,0:T(8,128)(2,1)}, bf16[1,128,4096]{2,1,0:T(8,128)(2,1)}, bf16[1,128,4096]{2,1,0:T(8,128)(2,1)}) custom-call(bf16[32,256,128]{2,1,0:T(8,128)(2,1)S(1)} %all-to-all-done.1.r_hbm, bf16[1,128,4096]{2,1,0:T(8,128)(2,1)} %refs_0_.1, bf16[1,128,4096]{2,1,0:T(8,128)(2,1)} %refs_1_.1, ...), custom_call_target="tpu_custom_call" | custom-call | flops 2097152 | bytes 10485760 | tf_op jit(solution)/shard_map/pallas_call | solution.py:368
  96.6 0.0 copy-done.2
  96.6 1.4 %collective-permute-done.3.others_ref = f32[8,4096]{1,0:T(8,128)S(1)} collective-permute-done((f32[8,4096]{1,0:T(8,128)S(1)}, f32[8,4096]{1,0:T(8,128)S(1)}, u32[]{:S(2)}, u32[]{:S(2)}) %collective-permute-start.3) | collective-permute-done | bytes 131104 | tf_op jit(solution)/shard_map/ppermute | solution.py:410
  98.0 0.0 copy-start.3
  98.0 0.6 copy-done.3
  98.6 1.8 %shard_map.106 = f32[8,4096]{1,0:T(8,128)} custom-call(f32[8,4096]{1,0:T(8,128)} %taps_ref.3, f32[8,4096]{1,0:T(8,128)} %copy-done.2, f32[8,4096]{1,0:T(8,128)} %copy-done.3), custom_call_target="tpu_custom_call" | custom-call | tf_op jit(solution)/shard_map/pallas_call | solution.py:398
Async XLA Ops:
  4.0 35.5 %all-to-all-start = ((bf16[32,256,128]{2,1,0:T(8,128)(2,1)}), bf16[32,256,128]{2,1,0:T(8,128)(2,1)S(1)}, u32[]{:S(2)}, u32[]{:S(2)}) async-start(bf16[32,256,128]{2,1,0:T(8,128)(2,1)} %shard_map.101), calls=%async_computation | async-start | bytes 4194304 | tf_op jit(solution)/shard_map/all_to_all | solution.py:406
  11.6 27.9 %copy-start.1 = (s32[32]{0:T(128)S(1)}, s32[32]{0:T(128)}, u32[]{:S(2)}) copy-start(s32[32]{0:T(128)} %order_ref.3) | copy-start | bytes 388
  39.5 15.1 %copy-start = (bf16[32,256,128]{2,1,0:T(8,128)(2,1)}, bf16[32,256,128]{2,1,0:T(8,128)(2,1)S(1)}, u32[]{:S(2)}) copy-start(bf16[32,256,128]{2,1,0:T(8,128)(2,1)S(1)} %all-to-all-done.x_hbm) | copy-start | bytes 6291460
  54.6 37.8 %all-to-all-start.1 = ((bf16[32,256,128]{2,1,0:T(8,128)(2,1)}), bf16[32,256,128]{2,1,0:T(8,128)(2,1)S(1)}, u32[]{:S(2)}, u32[]{:S(2)}) async-start(bf16[32,256,128]{2,1,0:T(8,128)(2,1)} %shard_map.103), calls=%async_computation.1 | async-start | bytes 4194304 | tf_op jit(solution)/shard_map/all_to_all | solution.py:406
  69.4 9.3 %collective-permute-start.2 = (f32[8,4096]{1,0:T(8,128)}, f32[8,4096]{1,0:T(8,128)S(1)}, u32[]{:S(2)}, u32[]{:S(2)}) collective-permute-start(f32[8,4096]{1,0:T(8,128)} %shard_map.104), channel_id=1, source_target_pairs={{0,96},{32,64},{64,32},{96,0},{128,224},{160,192},{192,160},{224,1... | collective-permute-start | bytes 393224 | tf_op jit(solution)/shard_map/ppermute | solution.py:410
  74.1 11.1 %collective-permute-start.1 = (f32[8,4096]{1,0:T(8,128)}, f32[8,4096]{1,0:T(8,128)S(1)}, u32[]{:S(2)}, u32[]{:S(2)}) collective-permute-start(f32[8,4096]{1,0:T(8,128)} %shard_map.104), channel_id=1, source_target_pairs={{0,64},{32,96},{64,0},{96,32},{128,192},{160,224},{192,128},{224,1... | collective-permute-start | bytes 393224 | tf_op jit(solution)/shard_map/ppermute | solution.py:410
  74.1 11.1 %collective-permute-start = (f32[8,4096]{1,0:T(8,128)}, f32[8,4096]{1,0:T(8,128)S(1)}, u32[]{:S(2)}, u32[]{:S(2)}) collective-permute-start(f32[8,4096]{1,0:T(8,128)} %shard_map.104), channel_id=1, source_target_pairs={{0,32},{32,0},{64,96},{96,64},{128,160},{160,128},{192,224},{224,1... | collective-permute-start | bytes 393224 | tf_op jit(solution)/shard_map/ppermute | solution.py:410
  86.2 10.4 %copy-start.2 = (f32[8,4096]{1,0:T(8,128)}, f32[8,4096]{1,0:T(8,128)S(1)}, u32[]{:S(2)}) copy-start(f32[8,4096]{1,0:T(8,128)S(1)} %add_add_fusion.mine_ref) | copy-start | bytes 393220
  86.2 11.8 %collective-permute-start.3 = (f32[8,4096]{1,0:T(8,128)S(1)}, f32[8,4096]{1,0:T(8,128)S(1)}, u32[]{:S(2)}, u32[]{:S(2)}) collective-permute-start(f32[8,4096]{1,0:T(8,128)S(1)} %add_add_fusion.mine_ref), channel_id=1, source_target_pairs={{0,128},{32,160},{64,192},{96,224},{128,0},{160,32},{192,64},{224,... | collective-permute-start | bytes 393224 | tf_op jit(solution)/shard_map/ppermute | solution.py:410
  98.0 0.6 copy-start.3

commit v7 on v6

--- a/solution.py
+++ b/solution.py
@@ -308,7 +308,7 @@
             one(i * AT_ONCE + k, k % 2)
 
     width = sums.shape[1]
-    out_ref[...] = pltpu.roll(sums[...], width - last, 1)[:, : pieces * BLOCK]
+    out_ref[...] = pltpu.roll(sums[...], width - last, 1)[:, : pieces * BLOCK].astype(jnp.bfloat16)
 
 
 def lag_sums_of(order, x, groups):
@@ -327,7 +327,7 @@
             pltpu.VMEM((groups, length + BLOCK), jnp.float32),
             pltpu.SemaphoreType.DMA((pieces,)),
         ],
-        out_shape=jax.ShapeDtypeStruct((groups, length), jnp.float32),
+        out_shape=jax.ShapeDtypeStruct((groups, length), jnp.bfloat16),
         compiler_params=params(),
         cost_estimate=SHORT,
     )(order, pltpu.with_memory_space_constraint(x, pltpu.HBM))
@@ -398,7 +398,7 @@
     return pl.pallas_call(
         functools.partial(taps_kernel, sequences),
         out_shape=jax.ShapeDtypeStruct(taps.shape, jnp.float32),
-        compiler_params=params(),
+        compiler_params=params(16),
     )(taps, mine, others)
 
 
@@ -419,7 +419,7 @@
     arrived, _ = lax.optimization_barrier((arrived, filtered))
     lag_sums = lag_sums_of(order, arrived, filter_taps.shape[0])
     near = [from_partner(lag_sums, step) for step in range(1, sequences // 2)]
-    half = sum(near, lag_sums)
+    half = sum((part.astype(jnp.float32) for part in near), lag_sums.astype(jnp.float32))
     far = from_partner(half, sequences // 2)
     mixed_out, gate_grad, key_grad, value_grad = post(
         returned, output_gate_input, upstream, value_input, key_input

time: 101 us -> 95.9 us (0.950)
  the two profiles are of different devices: /device:TPU:2 before, /device:TPU:64 now
where the time goes in v7:
time: 95.9 us; the launch traced here: 95.4 us
  Pallas kernels  44.2 us (46%)
  waiting for transfers between devices  29.1 us (30%)
  starting transfers between devices  20.5 us (21%)
    all_to_all x2, waiting for transfers between devices, exchange(): return lax.all_to_all(tiles, 'ctx', split_axis=0, concat_axis=0, tiled=True)  24.6 us
    pallas_call x1, Pallas kernels, filters(): pl.pallas_call(filters_kernel, in_specs=[pl.BlockSpec(memory_space=pltpu....  15.1 us
    pallas_call x1, Pallas kernels, strips(): pl.pallas_call(strip_kernel, grid=(groups,), in_specs=[pl.BlockSpec((grou...  12 us
    all_to_all x2, starting transfers between devices, exchange(): return lax.all_to_all(tiles, 'ctx', split_axis=0, concat_axis=0, tiled=True)  11.4 us
    ppermute x4, starting transfers between devices, from_partner(): lax.ppermute(x, 'dp', [(i, i ^ step) for i in range(lax.axis_size('dp'))])  9.18 us
    pallas_call x1, Pallas kernels, lag_sums_of(): pl.pallas_call(lag_kernel, in_specs=[pl.BlockSpec(memory_space=pltpu.SMEM...  8.76 us
    ppermute x4, waiting for transfers between devices, from_partner(): lax.ppermute(x, 'dp', [(i, i ^ step) for i in range(lax.axis_size('dp'))])  4.49 us
    pallas_call x1, Pallas kernels, post(): pl.pallas_call(post_kernel, in_specs=[anywhere] * 5, out_specs=[anywhere]...  4.19 us
  transfers between devices with their start and end apart: 6, of which 4 were waited for; matrix products, arithmetic and copies ran while one was open for 1% of the time, Pallas kernels for 26%

profile of v7, /device:TPU:64, one launch (start us, length us, event | category | flops | bytes accessed | tf_op | source)
XLA Modules:
  0.0 95.4 jit_solution(4615910627879241730)
XLA Ops:
  0.6 3.4 %shard_map.101 = bf16[32,256,128]{2,1,0:T(8,128)(2,1)} custom-call(bf16[1,128,4096]{2,1,0:T(8,128)(2,1)} %refs_3_.1, bf16[1,128,4096]{2,1,0:T(8,128)(2,1)} %refs_2_.1, bf16[1,128,4096]{2,1,0:T(8,128)(2,1)} %refs_1_.1, bf16[1,128,4096]{2,1,0:T(8,128)(2,1)} %refs_0_.1), custom_call_target="tpu_custom_call" | custom-call | flops 1048576 | bytes 6291456 | tf_op jit(solution)/shard_map/pallas_call | solution.py:89
  4.0 7.3 %all-to-all-start = ((bf16[32,256,128]{2,1,0:T(8,128)(2,1)}), bf16[32,256,128]{2,1,0:T(8,128)(2,1)S(1)}, u32[]{:S(2)}, u32[]{:S(2)}) async-start(bf16[32,256,128]{2,1,0:T(8,128)(2,1)} %shard_map.101), calls=%async_computation | async-start | bytes 4194304 | tf_op jit(solution)/shard_map/all_to_all | solution.py:406
  11.4 0.0 copy-start.2
  11.4 12.0 %shard_map.102.strip_hbm = bf16[8,128,4224]{2,1,0:T(8,128)(2,1)} custom-call(f32[8,4096]{1,0:T(8,128)} %taps_ref.3), custom_call_target="tpu_custom_call" | custom-call | flops 10000000000 | bytes 1000 | tf_op jit(solution)/shard_map/pallas_call | solution.py:129
  23.4 18.0 %all-to-all-done.x_hbm = bf16[32,256,128]{2,1,0:T(8,128)(2,1)S(1)} async-done(((bf16[32,256,128]{2,1,0:T(8,128)(2,1)}), bf16[32,256,128]{2,1,0:T(8,128)(2,1)S(1)}, u32[]{:S(2)}, u32[]{:S(2)}) %all-to-all-start) | async-done | bytes 2097184 | tf_op jit(solution)/shard_map/all_to_all | solution.py:406
  41.3 0.0 copy-done.2
  41.3 0.0 copy-start
  41.3 15.1 %shard_map.103 = bf16[32,256,128]{2,1,0:T(8,128)(2,1)} custom-call(s32[32]{0:T(128)S(1)} %copy-done.2, bf16[32,256,128]{2,1,0:T(8,128)(2,1)S(1)} %all-to-all-done.x_hbm, bf16[8,128,4224]{2,1,0:T(8,128)(2,1)} %shard_map.102.strip_hbm), custom_call_target="tpu_custom_call" | custom-call | flops 10000000000 | bytes 1000 | tf_op jit(solution)/shard_map/pallas_call | solution.py:237
  56.4 0.0 copy-done
  56.4 4.0 %all-to-all-start.1 = ((bf16[32,256,128]{2,1,0:T(8,128)(2,1)}), bf16[32,256,128]{2,1,0:T(8,128)(2,1)S(1)}, u32[]{:S(2)}, u32[]{:S(2)}) async-start(bf16[32,256,128]{2,1,0:T(8,128)(2,1)} %shard_map.103), calls=%async_computation.1 | async-start | bytes 4194304 | tf_op jit(solution)/shard_map/all_to_all | solution.py:406
  60.4 8.8 %shard_map.104 = bf16[8,4096]{1,0:T(8,128)(2,1)} custom-call(s32[32]{0:T(128)} %order_ref.3, bf16[32,256,128]{2,1,0:T(8,128)(2,1)} %copy-done), custom_call_target="tpu_custom_call" | custom-call | flops 1000 | bytes 1000 | tf_op jit(solution)/shard_map/pallas_call | solution.py:317
  69.2 0.2 collective-permute-start.2
  69.4 4.2 %collective-permute-start.1 = (bf16[8,4096]{1,0:T(8,128)(2,1)}, bf16[8,4096]{1,0:T(8,128)(2,1)S(1)}, u32[]{:S(2)}, u32[]{:S(2)}) collective-permute-start(bf16[8,4096]{1,0:T(8,128)(2,1)} %shard_map.104), channel_id=1, source_target_pairs={{0,64},{32,96},{64,0},{96,32},{128,192},{160,224},{192,128},{224,1... | collective-permute-start | bytes 196616 | tf_op jit(solution)/shard_map/ppermute | solution.py:410
  73.6 0.0 collective-permute-start
  73.6 0.3 collective-permute-done.2
  73.9 4.2 %collective-permute-done.1 = bf16[8,4096]{1,0:T(8,128)(2,1)S(1)} collective-permute-done((bf16[8,4096]{1,0:T(8,128)(2,1)}, bf16[8,4096]{1,0:T(8,128)(2,1)S(1)}, u32[]{:S(2)}, u32[]{:S(2)}) %collective-permute-start.1) | collective-permute-done | bytes 65568 | tf_op jit(solution)/shard_map/ppermute | solution.py:410
  78.1 0.0 collective-permute-done
  78.1 0.9 convert_add_fusion.mine_ref
  78.9 0.0 copy-start.1
  79.0 4.8 %collective-permute-start.3 = (f32[8,4096]{1,0:T(8,128)S(1)}, f32[8,4096]{1,0:T(8,128)S(1)}, u32[]{:S(2)}, u32[]{:S(2)}) collective-permute-start(f32[8,4096]{1,0:T(8,128)S(1)} %convert_add_fusion.mine_ref), channel_id=1, source_target_pairs={{0,128},{32,160},{64,192},{96,224},{128,0},{160,32},{192,64},{224,... | collective-permute-start | bytes 393224 | tf_op jit(solution)/shard_map/ppermute | solution.py:410
  83.8 6.6 %all-to-all-done.1.r_hbm = bf16[32,256,128]{2,1,0:T(8,128)(2,1)S(1)} async-done(((bf16[32,256,128]{2,1,0:T(8,128)(2,1)}), bf16[32,256,128]{2,1,0:T(8,128)(2,1)S(1)}, u32[]{:S(2)}, u32[]{:S(2)}) %all-to-all-start.1) | async-done | bytes 2097184 | tf_op jit(solution)/shard_map/all_to_all | solution.py:406
  90.4 4.2 %shard_map.105 = (bf16[1,128,4096]{2,1,0:T(8,128)(2,1)}, bf16[1,128,4096]{2,1,0:T(8,128)(2,1)}, bf16[1,128,4096]{2,1,0:T(8,128)(2,1)}, bf16[1,128,4096]{2,1,0:T(8,128)(2,1)}) custom-call(bf16[32,256,128]{2,1,0:T(8,128)(2,1)S(1)} %all-to-all-done.1.r_hbm, bf16[1,128,4096]{2,1,0:T(8,128)(2,1)} %refs_0_.1, bf16[1,128,4096]{2,1,0:T(8,128)(2,1)} %refs_1_.1, ...), custom_call_target="tpu_custom_call" | custom-call | flops 2097152 | bytes 10485760 | tf_op jit(solution)/shard_map/pallas_call | solution.py:368
  94.6 0.0 collective-permute-done.3.others_ref
  94.6 0.0 copy-done.1
  94.6 0.8 shard_map.106
Async XLA Ops:
  4.0 37.3 %all-to-all-start = ((bf16[32,256,128]{2,1,0:T(8,128)(2,1)}), bf16[32,256,128]{2,1,0:T(8,128)(2,1)S(1)}, u32[]{:S(2)}, u32[]{:S(2)}) async-start(bf16[32,256,128]{2,1,0:T(8,128)(2,1)} %shard_map.101), calls=%async_computation | async-start | bytes 4194304 | tf_op jit(solution)/shard_map/all_to_all | solution.py:406
  11.4 30.0 %copy-start.2 = (s32[32]{0:T(128)S(1)}, s32[32]{0:T(128)}, u32[]{:S(2)}) copy-start(s32[32]{0:T(128)} %order_ref.3) | copy-start | bytes 388
  41.3 15.1 %copy-start = (bf16[32,256,128]{2,1,0:T(8,128)(2,1)}, bf16[32,256,128]{2,1,0:T(8,128)(2,1)S(1)}, u32[]{:S(2)}) copy-start(bf16[32,256,128]{2,1,0:T(8,128)(2,1)S(1)} %all-to-all-done.x_hbm) | copy-start | bytes 6291460
  56.4 34.0 %all-to-all-start.1 = ((bf16[32,256,128]{2,1,0:T(8,128)(2,1)}), bf16[32,256,128]{2,1,0:T(8,128)(2,1)S(1)}, u32[]{:S(2)}, u32[]{:S(2)}) async-start(bf16[32,256,128]{2,1,0:T(8,128)(2,1)} %shard_map.103), calls=%async_computation.1 | async-start | bytes 4194304 | tf_op jit(solution)/shard_map/all_to_all | solution.py:406
  69.2 4.7 %collective-permute-start.2 = (bf16[8,4096]{1,0:T(8,128)(2,1)}, bf16[8,4096]{1,0:T(8,128)(2,1)S(1)}, u32[]{:S(2)}, u32[]{:S(2)}) collective-permute-start(bf16[8,4096]{1,0:T(8,128)(2,1)} %shard_map.104), channel_id=1, source_target_pairs={{0,96},{32,64},{64,32},{96,0},{128,224},{160,192},{192,160},{224,1... | collective-permute-start | bytes 196616 | tf_op jit(solution)/shard_map/ppermute | solution.py:410
  69.4 8.7 %collective-permute-start.1 = (bf16[8,4096]{1,0:T(8,128)(2,1)}, bf16[8,4096]{1,0:T(8,128)(2,1)S(1)}, u32[]{:S(2)}, u32[]{:S(2)}) collective-permute-start(bf16[8,4096]{1,0:T(8,128)(2,1)} %shard_map.104), channel_id=1, source_target_pairs={{0,64},{32,96},{64,0},{96,32},{128,192},{160,224},{192,128},{224,1... | collective-permute-start | bytes 196616 | tf_op jit(solution)/shard_map/ppermute | solution.py:410
  73.6 4.5 %collective-permute-start = (bf16[8,4096]{1,0:T(8,128)(2,1)}, bf16[8,4096]{1,0:T(8,128)(2,1)S(1)}, u32[]{:S(2)}, u32[]{:S(2)}) collective-permute-start(bf16[8,4096]{1,0:T(8,128)(2,1)} %shard_map.104), channel_id=1, source_target_pairs={{0,32},{32,0},{64,96},{96,64},{128,160},{160,128},{192,224},{224,1... | collective-permute-start | bytes 196616 | tf_op jit(solution)/shard_map/ppermute | solution.py:410
  78.9 15.7 %copy-start.1 = (f32[8,4096]{1,0:T(8,128)S(1)}, f32[8,4096]{1,0:T(8,128)}, u32[]{:S(2)}) copy-start(f32[8,4096]{1,0:T(8,128)} %taps_ref.3) | copy-start | bytes 393220
  79.0 15.7 %collective-permute-start.3 = (f32[8,4096]{1,0:T(8,128)S(1)}, f32[8,4096]{1,0:T(8,128)S(1)}, u32[]{:S(2)}, u32[]{:S(2)}) collective-permute-start(f32[8,4096]{1,0:T(8,128)S(1)} %convert_add_fusion.mine_ref), channel_id=1, source_target_pairs={{0,128},{32,160},{64,192},{96,224},{128,0},{160,32},{192,64},{224,... | collective-permute-start | bytes 393224 | tf_op jit(solution)/shard_map/ppermute | solution.py:410

commit v8 on v7

--- a/solution.py
+++ b/solution.py
@@ -424,7 +424,6 @@
     mixed_out, gate_grad, key_grad, value_grad = post(
         returned, output_gate_input, upstream, value_input, key_input
     )
-    half, mixed_out = lax.optimization_barrier((half, mixed_out))
     taps_grad = taps_grad_of(filter_taps, half, far, sequences)
     return mixed_out, gate_grad, key_grad, value_grad, taps_grad
 

time: 95.9 us -> 98.7 us (1.029)
  the two profiles are of different devices: /device:TPU:64 before, /device:TPU:2 now
where the time goes in v8:
time: 98.7 us; the launch traced here: 98.2 us
  Pallas kernels  44.3 us (45%)
  waiting for transfers between devices  27.4 us (28%)
  starting transfers between devices  25 us (25%)
    all_to_all x2, waiting for transfers between devices, exchange(): return lax.all_to_all(tiles, 'ctx', split_axis=0, concat_axis=0, tiled=True)  15.8 us
    pallas_call x1, Pallas kernels, filters(): pl.pallas_call(filters_kernel, in_specs=[pl.BlockSpec(memory_space=pltpu....  15 us
    all_to_all x2, starting transfers between devices, exchange(): return lax.all_to_all(tiles, 'ctx', split_axis=0, concat_axis=0, tiled=True)  13.7 us
    pallas_call x1, Pallas kernels, strips(): pl.pallas_call(strip_kernel, grid=(groups,), in_specs=[pl.BlockSpec((grou...  12 us
    ppermute x4, waiting for transfers between devices, from_partner(): lax.ppermute(x, 'dp', [(i, i ^ step) for i in range(lax.axis_size('dp'))])  11.5 us
    ppermute x4, starting transfers between devices, from_partner(): lax.ppermute(x, 'dp', [(i, i ^ step) for i in range(lax.axis_size('dp'))])  11.3 us
    pallas_call x1, Pallas kernels, lag_sums_of(): pl.pallas_call(lag_kernel, in_specs=[pl.BlockSpec(memory_space=pltpu.SMEM...  8.89 us
    pallas_call x1, Pallas kernels, post(): pl.pallas_call(post_kernel, in_specs=[anywhere] * 5, out_specs=[anywhere]...  4.19 us
  transfers between devices with their start and end apart: 6, of which 5 were waited for; matrix products, arithmetic and copies ran while one was open for 1% of the time, Pallas kernels for 22%

profile of v8, /device:TPU:2, one launch (start us, length us, event | category | flops | bytes accessed | tf_op | source)
XLA Modules:
  0.0 98.2 jit_solution(8806700344235717407)
XLA Ops:
  0.6 3.4 %shard_map.101 = bf16[32,256,128]{2,1,0:T(8,128)(2,1)} custom-call(bf16[1,128,4096]{2,1,0:T(8,128)(2,1)} %refs_3_.1, bf16[1,128,4096]{2,1,0:T(8,128)(2,1)} %refs_2_.1, bf16[1,128,4096]{2,1,0:T(8,128)(2,1)} %refs_1_.1, bf16[1,128,4096]{2,1,0:T(8,128)(2,1)} %refs_0_.1), custom_call_target="tpu_custom_call" | custom-call | flops 1048576 | bytes 6291456 | tf_op jit(solution)/shard_map/pallas_call | solution.py:89
  4.0 7.6 %all-to-all-start = ((bf16[32,256,128]{2,1,0:T(8,128)(2,1)}), bf16[32,256,128]{2,1,0:T(8,128)(2,1)S(1)}, u32[]{:S(2)}, u32[]{:S(2)}) async-start(bf16[32,256,128]{2,1,0:T(8,128)(2,1)} %shard_map.101), calls=%async_computation | async-start | bytes 4194304 | tf_op jit(solution)/shard_map/all_to_all | solution.py:406
  11.7 0.0 copy-start.2
  11.7 12.0 %shard_map.102.strip_hbm = bf16[8,128,4224]{2,1,0:T(8,128)(2,1)} custom-call(f32[8,4096]{1,0:T(8,128)} %taps_ref.3), custom_call_target="tpu_custom_call" | custom-call | flops 10000000000 | bytes 1000 | tf_op jit(solution)/shard_map/pallas_call | solution.py:129
  23.7 15.8 %all-to-all-done.x_hbm = bf16[32,256,128]{2,1,0:T(8,128)(2,1)S(1)} async-done(((bf16[32,256,128]{2,1,0:T(8,128)(2,1)}), bf16[32,256,128]{2,1,0:T(8,128)(2,1)S(1)}, u32[]{:S(2)}, u32[]{:S(2)}) %all-to-all-start) | async-done | bytes 2097184 | tf_op jit(solution)/shard_map/all_to_all | solution.py:406
  39.5 0.0 copy-done.2
  39.5 0.0 copy-start
  39.5 15.0 %shard_map.103 = bf16[32,256,128]{2,1,0:T(8,128)(2,1)} custom-call(s32[32]{0:T(128)S(1)} %copy-done.2, bf16[32,256,128]{2,1,0:T(8,128)(2,1)S(1)} %all-to-all-done.x_hbm, bf16[8,128,4224]{2,1,0:T(8,128)(2,1)} %shard_map.102.strip_hbm), custom_call_target="tpu_custom_call" | custom-call | flops 10000000000 | bytes 1000 | tf_op jit(solution)/shard_map/pallas_call | solution.py:237
  54.6 0.0 copy-done
  54.6 6.0 %all-to-all-start.1 = ((bf16[32,256,128]{2,1,0:T(8,128)(2,1)}), bf16[32,256,128]{2,1,0:T(8,128)(2,1)S(1)}, u32[]{:S(2)}, u32[]{:S(2)}) async-start(bf16[32,256,128]{2,1,0:T(8,128)(2,1)} %shard_map.103), calls=%async_computation.1 | async-start | bytes 4194304 | tf_op jit(solution)/shard_map/all_to_all | solution.py:406
  60.6 0.0 copy-start.1
  60.6 8.9 %shard_map.105 = bf16[8,4096]{1,0:T(8,128)(2,1)} custom-call(s32[32]{0:T(128)} %order_ref.3, bf16[32,256,128]{2,1,0:T(8,128)(2,1)} %copy-done), custom_call_target="tpu_custom_call" | custom-call | flops 1000 | bytes 1000 | tf_op jit(solution)/shard_map/pallas_call | solution.py:317
  69.5 4.7 %collective-permute-start.2 = (bf16[8,4096]{1,0:T(8,128)(2,1)}, bf16[8,4096]{1,0:T(8,128)(2,1)S(1)}, u32[]{:S(2)}, u32[]{:S(2)}) collective-permute-start(bf16[8,4096]{1,0:T(8,128)(2,1)} %shard_map.105), channel_id=1, source_target_pairs={{0,96},{32,64},{64,32},{96,0},{128,224},{160,192},{192,160},{224,1... | collective-permute-start | bytes 196616 | tf_op jit(solution)/shard_map/ppermute | solution.py:410
  74.2 0.0 collective-permute-start.1
  74.3 0.7 collective-permute-start
  74.9 2.4 %collective-permute-done.2 = bf16[8,4096]{1,0:T(8,128)(2,1)S(1)} collective-permute-done((bf16[8,4096]{1,0:T(8,128)(2,1)}, bf16[8,4096]{1,0:T(8,128)(2,1)S(1)}, u32[]{:S(2)}, u32[]{:S(2)}) %collective-permute-start.2) | collective-permute-done | bytes 65568 | tf_op jit(solution)/shard_map/ppermute | solution.py:410
  77.3 2.5 %collective-permute-done.1 = bf16[8,4096]{1,0:T(8,128)(2,1)S(1)} collective-permute-done((bf16[8,4096]{1,0:T(8,128)(2,1)}, bf16[8,4096]{1,0:T(8,128)(2,1)S(1)}, u32[]{:S(2)}, u32[]{:S(2)}) %collective-permute-start.1) | collective-permute-done | bytes 65568 | tf_op jit(solution)/shard_map/ppermute | solution.py:410
  79.9 0.3 collective-permute-done
  80.1 0.9 convert_add_fusion.mine_ref
  81.0 5.9 %collective-permute-start.3 = (f32[8,4096]{1,0:T(8,128)S(1)}, f32[8,4096]{1,0:T(8,128)S(1)}, u32[]{:S(2)}, u32[]{:S(2)}) collective-permute-start(f32[8,4096]{1,0:T(8,128)S(1)} %convert_add_fusion.mine_ref), channel_id=1, source_target_pairs={{0,128},{32,160},{64,192},{96,224},{128,0},{160,32},{192,64},{224,... | collective-permute-start | bytes 393224 | tf_op jit(solution)/shard_map/ppermute | solution.py:410
  86.9 6.3 %collective-permute-done.3.others_ref = f32[8,4096]{1,0:T(8,128)S(1)} collective-permute-done((f32[8,4096]{1,0:T(8,128)S(1)}, f32[8,4096]{1,0:T(8,128)S(1)}, u32[]{:S(2)}, u32[]{:S(2)}) %collective-permute-start.3) | collective-permute-done | bytes 131104 | tf_op jit(solution)/shard_map/ppermute | solution.py:410
  93.2 0.0 copy-done.1
  93.2 0.8 shard_map.106
  94.1 0.0 all-to-all-done.1.r_hbm
  94.1 4.2 %shard_map.104 = (bf16[1,128,4096]{2,1,0:T(8,128)(2,1)}, bf16[1,128,4096]{2,1,0:T(8,128)(2,1)}, bf16[1,128,4096]{2,1,0:T(8,128)(2,1)}, bf16[1,128,4096]{2,1,0:T(8,128)(2,1)}) custom-call(bf16[32,256,128]{2,1,0:T(8,128)(2,1)S(1)} %all-to-all-done.1.r_hbm, bf16[1,128,4096]{2,1,0:T(8,128)(2,1)} %refs_0_.1, bf16[1,128,4096]{2,1,0:T(8,128)(2,1)} %refs_1_.1, ...), custom_call_target="tpu_custom_call" | custom-call | flops 2097152 | bytes 10485760 | tf_op jit(solution)/shard_map/pallas_call | solution.py:368
Async XLA Ops:
  4.0 35.5 %all-to-all-start = ((bf16[32,256,128]{2,1,0:T(8,128)(2,1)}), bf16[32,256,128]{2,1,0:T(8,128)(2,1)S(1)}, u32[]{:S(2)}, u32[]{:S(2)}) async-start(bf16[32,256,128]{2,1,0:T(8,128)(2,1)} %shard_map.101), calls=%async_computation | async-start | bytes 4194304 | tf_op jit(solution)/shard_map/all_to_all | solution.py:406
  11.7 27.9 %copy-start.2 = (s32[32]{0:T(128)S(1)}, s32[32]{0:T(128)}, u32[]{:S(2)}) copy-start(s32[32]{0:T(128)} %order_ref.3) | copy-start | bytes 388
  39.5 15.1 %copy-start = (bf16[32,256,128]{2,1,0:T(8,128)(2,1)}, bf16[32,256,128]{2,1,0:T(8,128)(2,1)S(1)}, u32[]{:S(2)}) copy-start(bf16[32,256,128]{2,1,0:T(8,128)(2,1)S(1)} %all-to-all-done.x_hbm) | copy-start | bytes 6291460
  54.6 39.5 %all-to-all-start.1 = ((bf16[32,256,128]{2,1,0:T(8,128)(2,1)}), bf16[32,256,128]{2,1,0:T(8,128)(2,1)S(1)}, u32[]{:S(2)}, u32[]{:S(2)}) async-start(bf16[32,256,128]{2,1,0:T(8,128)(2,1)} %shard_map.103), calls=%async_computation.1 | async-start | bytes 4194304 | tf_op jit(solution)/shard_map/all_to_all | solution.py:406
  60.6 32.6 %copy-start.1 = (f32[8,4096]{1,0:T(8,128)S(1)}, f32[8,4096]{1,0:T(8,128)}, u32[]{:S(2)}) copy-start(f32[8,4096]{1,0:T(8,128)} %taps_ref.3) | copy-start | bytes 393220
  69.5 7.8 %collective-permute-start.2 = (bf16[8,4096]{1,0:T(8,128)(2,1)}, bf16[8,4096]{1,0:T(8,128)(2,1)S(1)}, u32[]{:S(2)}, u32[]{:S(2)}) collective-permute-start(bf16[8,4096]{1,0:T(8,128)(2,1)} %shard_map.105), channel_id=1, source_target_pairs={{0,96},{32,64},{64,32},{96,0},{128,224},{160,192},{192,160},{224,1... | collective-permute-start | bytes 196616 | tf_op jit(solution)/shard_map/ppermute | solution.py:410
  74.2 5.6 %collective-permute-start.1 = (bf16[8,4096]{1,0:T(8,128)(2,1)}, bf16[8,4096]{1,0:T(8,128)(2,1)S(1)}, u32[]{:S(2)}, u32[]{:S(2)}) collective-permute-start(bf16[8,4096]{1,0:T(8,128)(2,1)} %shard_map.105), channel_id=1, source_target_pairs={{0,64},{32,96},{64,0},{96,32},{128,192},{160,224},{192,128},{224,1... | collective-permute-start | bytes 196616 | tf_op jit(solution)/shard_map/ppermute | solution.py:410
  74.3 5.9 %collective-permute-start = (bf16[8,4096]{1,0:T(8,128)(2,1)}, bf16[8,4096]{1,0:T(8,128)(2,1)S(1)}, u32[]{:S(2)}, u32[]{:S(2)}) collective-permute-start(bf16[8,4096]{1,0:T(8,128)(2,1)} %shard_map.105), channel_id=1, source_target_pairs={{0,32},{32,0},{64,96},{96,64},{128,160},{160,128},{192,224},{224,1... | collective-permute-start | bytes 196616 | tf_op jit(solution)/shard_map/ppermute | solution.py:410
  81.0 12.2 %collective-permute-start.3 = (f32[8,4096]{1,0:T(8,128)S(1)}, f32[8,4096]{1,0:T(8,128)S(1)}, u32[]{:S(2)}, u32[]{:S(2)}) collective-permute-start(f32[8,4096]{1,0:T(8,128)S(1)} %convert_add_fusion.mine_ref), channel_id=1, source_target_pairs={{0,128},{32,160},{64,192},{96,224},{128,0},{160,32},{192,64},{224,... | collective-permute-start | bytes 393224 | tf_op jit(solution)/shard_map/ppermute | solution.py:410
